TPU v7x, 32 devices: a whole 2x2x4 slice. The times are simulated.
32 devices in a mesh: dp: 16 (over z, y, x), tensor: 2 (over core).
Axes of the slice: x: 2, y: 2, z: 4, core: 2. Of those that a mesh axis runs over, the one named last changes fastest.
Arguments:
- tokens: bfloat16 [2048, 8192], P('dp', 'tensor'), may hold values from -6 to 6
- hidden_grad: bfloat16 [2048, 28672], P('dp', 'tensor'), may hold values from -0.125 to 0.125
- masters: float32 [2, 64, 128, 128], P('tensor', 'dp'), may hold values from -0.5 to 0.5
- block_row: int32 [2, 32], P('tensor'), may hold values from 0 to 63, as said below
- block_col: int32 [2, 32], P('tensor'), may hold values from 0 to 111
- owners: int32 [2, 64], P('tensor'), may hold values from 0 to 15, as said below
Outputs:
- grads: float32 [2, 192, 128, 128], P('tensor', 'dp')
Inputs may be any that keep to these rules, and one draw needn't show every extreme that they name: `block_row`: in each slice the kept places are distinct. `owners`: in each slice every owner takes at most 12 of the 64 kept blocks, and some owner takes exactly 12.
All inputs are finite; a program needn't handle non-finite values.
Results may differ from a plain program's by a relative error of at most 0.0044.
Values may be sent and summed in bfloat16 or wider, within the bound.
No kernel may reach another device: no remote copies, remote signals or barrier semaphores. Data moves between devices by JAX's collectives and lax.ppermute only.
A program may use at most 64 MiB of HBM per device.

v0:
```python
import jax
import jax.numpy as jnp
from jax import lax
from jax.sharding import PartitionSpec as P


def slot_index(owner_row, capacity):
    count_all = owner_row.shape[0]
    same_owner = owner_row[:, None] == owner_row[None, :]
    earlier = (
        jnp.arange(count_all, dtype=jnp.int32)[None, :]
        < jnp.arange(count_all, dtype=jnp.int32)[:, None]
    )
    rank_index = jnp.sum(
        jnp.logical_and(same_owner, earlier).astype(jnp.int32), axis=1, dtype=jnp.int32
    )
    return owner_row * capacity + rank_index


def column_total(part, same_column):
    return jnp.einsum("tjc,kj->tkc", part, same_column, precision=lax.Precision.HIGHEST)


def local(tokens, hidden_grad, masters, block_row, block_col, owners):
    high = lax.Precision.HIGHEST
    features = lax.all_gather(tokens, "tensor", axis=1, tiled=True)
    token_count = features.shape[0]
    block_side = masters.shape[-1]
    kept_count = block_row.shape[1]
    weights = lax.all_gather(masters.astype(jnp.bfloat16), "dp", axis=1, tiled=True)[0]
    row_index = block_row[0]
    column_index = block_col[0]
    by_block = features.reshape(token_count, features.shape[1] // block_side, block_side)
    selected = jnp.take(by_block, row_index, axis=1)
    gate_part = jnp.einsum(
        "tkb,kbc->tkc", selected, weights[:kept_count], preferred_element_type=jnp.float32
    )
    up_part = jnp.einsum(
        "tkb,kbc->tkc", selected, weights[kept_count:], preferred_element_type=jnp.float32
    )
    same_column = (column_index[:, None] == column_index[None, :]).astype(jnp.float32)
    gate_value = column_total(gate_part, same_column)
    up_value = column_total(up_part, same_column)
    grad_columns = hidden_grad.reshape(token_count, hidden_grad.shape[1] // block_side, block_side)
    upstream = jnp.take(grad_columns, column_index, axis=1).astype(jnp.float32)
    sigmoid_gate = jax.nn.sigmoid(gate_value)
    gate_grad = (
        upstream * up_value * sigmoid_gate * (1.0 + gate_value * (1.0 - sigmoid_gate))
    ).astype(jnp.bfloat16)
    up_grad = (upstream * gate_value * sigmoid_gate).astype(jnp.bfloat16)
    grad_gate = jnp.einsum("tkb,tkc->kbc", selected, gate_grad, preferred_element_type=jnp.float32)
    grad_up = jnp.einsum("tkb,tkc->kbc", selected, up_grad, preferred_element_type=jnp.float32)
    block_grads = jnp.concatenate([grad_gate, grad_up], axis=0)
    owner_count = lax.axis_size("dp")
    capacity = 3 * block_grads.shape[0] // owner_count
    slot_list = slot_index(owners[0], capacity)
    summed = lax.psum(block_grads, "dp")
    own_slots = lax.axis_index("dp") * capacity + jnp.arange(capacity, dtype=jnp.int32)
    selector = (own_slots[:, None] == slot_list[None, :]).astype(jnp.float32)
    result = jnp.einsum("sk,kbc->sbc", selector, summed, precision=high)
    return result[None]


def solution(mesh):
    return jax.shard_map(
        local,
        mesh=mesh,
        in_specs=(
            P("dp", "tensor"),
            P("dp", "tensor"),
            P("tensor", "dp", None, None),
            P("tensor", None),
            P("tensor", None),
            P("tensor", None),
        ),
        out_specs=P("tensor", "dp", None, None),
        check_vma=False,
    )
```

profile of v0, /device:TPU:0, one launch (start us, length us, event | category | flops | bytes accessed | tf_op | source)
XLA Modules:
  0.0 282.0 jit_solution(3581329587527085117)
XLA Ops:
  6.5 0.0 copy-start.2
  6.5 0.0 all-gather.3.cloned.1.call-start
  6.5 2.3 copy.46
  8.9 0.0 all-gather.3.cloned.1.call-update
  8.9 0.0 all-gather.5.cloned.1.call-start
  8.9 0.0 copy-done.2
  8.9 0.7 bitcast_convert_fusion
  9.6 0.0 all-gather.5.cloned.1.call-update
  9.6 0.0 all-reduce.2.cloned.1.call-start
  9.7 6.1 %copy.49 = bf16[128,14336]{0,1:T(8,128)(2,1)} copy(bf16[128,14336]{1,0:T(8,128)(2,1)} %param.7) | data formatting | bytes 7340032 | tf_op args[1]
  15.8 0.0 copy-start.4
  15.8 6.1 %copy.50 = bf16[128,112,128]{2,0,1:T(8,128)(2,1)} copy(bf16[128,112,128]{0,2,1:T(8,128)(2,1)} %bitcast.86) | data formatting | bytes 7340032 | tf_op jit(solution)/shard_map/reshape | solution.py:44
  21.9 0.0 copy-done.4
  21.9 0.0 copy-start.3
  21.9 3.7 %gather_fusion.1 = bf16[32,128,128]{2,1,0:T(8,128)(2,1)} fusion(bf16[128,112,128]{2,0,1:T(8,128)(2,1)} %copy.50, s32[1024]{0:T(1024)S(1)} %pad_clamp_fusion), kind=kCustom, calls=%fused_computation.1 | custom fusion | bytes 2097280 | tf_op jit(solution)/shard_map/jit(_take)/gather | solution.py:45
  25.6 0.0 copy-done.3
  25.7 0.0 all-gather.3.cloned.1.call-done
  25.7 3.2 %copy.47 = bf16[128,64,128]{2,0,1:T(8,128)(2,1)S(1)} copy(bf16[128,64,128]{0,2,1:T(8,128)(2,1)} %bitcast.87) | data formatting | bytes 4194304 | tf_op jit(solution)/shard_map/reshape | solution.py:33
  28.9 0.7 gather_fusion
  29.7 0.6 fusion.24
  30.3 1.2 copy.59
  31.5 55.5 %all-gather.5.cloned.1.call-done = bf16[1,64,128,128]{3,2,0,1:T(8,128)(2,1)} async-done(((bf16[1,4,128,128]{3,2,0,1:T(8,128)(2,1)}), bf16[1,64,128,128]{3,2,0,1:T(8,128)(2,1)}) %all-gather.5.cloned.1.call-update) | async-done | bytes 2097168 | tf_op jit(solution)/shard_map/all_gather | solution.py:30
  87.0 0.0 copy-start
  87.0 1.9 convolution_bitcast_fusion
  88.9 0.0 copy-done
  88.9 0.0 copy-start.1
  88.9 0.5 convolution_bitcast_fusion.1
  89.5 0.7 copy-done.1
  90.1 3.5 %fusion.9 = (bf16[128,32,128]{2,1,0:T(8,128)(2,1)S(1)}, f32[32,128,128]{2,0,1:T(8,128)S(1)}) fusion(bf16[32,128,128]{2,1,0:T(8,128)(2,1)S(1)} %copy-done.1, pred[32]{0:T(512)(128)(4,1)S(1)} %compare_and_fusion, f32[128,32,128]{2,0,1:T(8,128)S(1)} %convolution_bitcast_fusion, s32[32]{0:T(128)S(1)} %bitcast.90), kind=kOutput, calls=%fused_computation.15 | convolution fusion | flops 205521920 | bytes 6291616 | tf_op jit(solution)/shard_map/tjc,kj->tkc/dot_general | solution.py:21
  93.6 0.8 fusion.20
  94.4 3.8 %fusion.7 = bf16[128,32,128]{2,1,0:T(8,128)(2,1)S(1)} fusion(f32[32,128,128]{2,0,1:T(8,128)S(1)} %get-tuple-element.6, f32[128,32,128]{2,0,1:T(8,128)S(1)} %convolution_bitcast_fusion.1, bf16[32,128,128]{2,1,0:T(8,128)(2,1)S(1)} %copy-done.1, pred[32]{0:T(512)(128)(4,1)S(1)} %compare_and_fusion, s32[32]{0:T(128)S(1)} %bitcast.91), kind=kOutput, calls=%fused_computation.13 | convolution fusion | flops 207619072 | bytes 6291616 | tf_op jit(solution)/shard_map/tjc,kj->tkc/dot_general | solution.py:21
  98.2 0.8 fusion.22
  98.9 2.5 pad_maximum_fusion
  101.4 0.0 copy-start.5
  101.4 0.0 all-reduce.2.cloned.1.call-update
  101.5 0.6 copy-done.5
  102.1 0.2 convert_reduce_fusion
  102.3 166.2 %all-reduce.2.cloned.1.call-done = f32[64,128,128]{2,1,0:T(8,128)} async-done(((f32[64,128,128]{2,1,0:T(8,128)}), f32[64,128,128]{2,1,0:T(8,128)}) %all-reduce.2.cloned.1.call-update) | async-done | bytes 4194320 | tf_op jit(solution)/shard_map/psum | solution.py:57
  268.4 5.9 %fusion.17 = f32[1,12,128,128]{3,1,2,0:T(8,128)S(1)} fusion(f32[64,128,128]{2,1,0:T(8,128)} %all-reduce.2.cloned.1.call-done, s32[64]{0:T(128)S(1)} %fusion.40, s32[12]{0:T(128)S(1)} %iota_add_fusion), kind=kOutput, calls=%fused_computation.24 | convolution fusion | flops 150995712 | bytes 4981040 | tf_op jit(solution)/shard_map/sk,kbc->sbc/dot_general | solution.py:60
  274.3 1.1 copy.64
  (8 shorter events, 0.0 us)
Async XLA Ops:
  6.5 2.4 copy-start.2
  6.5 19.2 %all-gather.3.cloned.1.call-start = ((), (), s32[]{:S(2)}) async-start(), calls=%async_computation | async-start | bytes 3145728 | tf_op jit(solution)/shard_map/all_gather | solution.py:26
  8.9 78.1 %all-gather.5.cloned.1.call-start = ((), (), s32[]{:S(2)}) async-start(), calls=%async_computation.1 | async-start | bytes 2228224 | tf_op jit(solution)/shard_map/all_gather | solution.py:30
  9.6 258.8 %all-reduce.2.cloned.1.call-start = ((), (), s32[]{:S(2)}) async-start(), calls=%async_computation.2 | async-start | bytes 8388608 | tf_op jit(solution)/shard_map/psum | solution.py:57
  15.8 6.1 %copy-start.4 = (s32[1,32]{1,0:T(1,128)S(1)}, s32[1,32]{1,0:T(1,128)}, u32[]{:S(2)}) copy-start(s32[1,32]{1,0:T(1,128)} %param.10) | copy-start | bytes 388
  21.9 3.7 %copy-start.3 = (s32[1,32]{1,0:T(1,128)S(1)}, s32[1,32]{1,0:T(1,128)}, u32[]{:S(2)}) copy-start(s32[1,32]{1,0:T(1,128)} %param.9) | copy-start | bytes 388
  87.0 1.9 copy-start
  88.9 1.2 copy-start.1
  101.4 0.7 copy-start.5
Sparse Core Ops, SparseCore 0:
  9.0 13.2 all-gather.2
  25.1 61.8 all-gather.4
  101.6 166.8 all-reduce.1
where the time goes:
time: 283 us; the launch traced here: 282 us
  waiting for transfers between devices  222 us (78%)
  local copies, waits for them, and re-layouts  25.8 us (9%)
  matrix products  17.1 us (6%)
  between operations  13.2 us (5%)
  other arithmetic  4.02 us (1%)
    psum x1, waiting for transfers between devices, local(): summed = lax.psum(block_grads, 'dp')  166 us
    all_gather x1, waiting for transfers between devices, local(): lax.all_gather(masters.astype(jnp.bfloat16), 'dp', axis=1, tiled=True)[0]  55.5 us
    unnamed x14, local copies, waits for them, and re-layouts  9.69 us
    dot_general x2, matrix products, column_total(): jnp.einsum('tjc,kj->tkc', part, same_column, precision=lax.Precision.HIGH...  7.25 us
    reshape x1, local copies, waits for them, and re-layouts, local(): hidden_grad.reshape(token_count, hidden_grad.shape[1] // block_side, bloc...  6.14 us
    dot_general x1, matrix products, local(): result = jnp.einsum('sk,kbc->sbc', selector, summed, precision=high)  5.9 us
  transfers between devices with their start and end apart: 3, of which 2 were waited for; matrix products, arithmetic and copies ran while one was open for 8% of the time, Pallas kernels for 0%

commit v1 on v0

v1 whole, which is shorter than its diff:
```python
import functools

import jax
import jax.numpy as jnp
import numpy as np
from jax import lax
from jax.experimental import pallas as pl
from jax.experimental.pallas import tpu as pltpu
from jax.sharding import PartitionSpec as P

VMEM = pl.BlockSpec(memory_space=pltpu.VMEM)
SMEM = pl.BlockSpec(memory_space=pltpu.SMEM)
BF16 = jnp.bfloat16
F32 = jnp.float32


def call(body, name, outs, in_specs, args, flops=0, scratch=()):
    moved = sum(int(np.prod(o.shape)) * o.dtype.itemsize for o in outs)
    moved += sum(int(np.prod(a.shape)) * a.dtype.itemsize for a in args)
    return pl.pallas_call(
        body,
        name=name,
        out_shape=tuple(outs),
        in_specs=in_specs,
        out_specs=tuple(VMEM for _ in outs),
        scratch_shapes=list(scratch),
        compiler_params=pltpu.CompilerParams(vmem_limit_bytes=40 << 20),
        cost_estimate=pl.CostEstimate(flops=flops, bytes_accessed=moved, transcendentals=0),
    )(*args)


def swap(value, axis, bit):
    size = lax.axis_size(axis)
    return lax.ppermute(value, axis, [(i, i ^ (1 << bit)) for i in range(size)])


def spread(value):
    parts = [value[None]]
    for bit in range(lax.axis_size("tensor").bit_length() - 1):
        whole = parts[0] if len(parts) == 1 else jnp.concatenate(parts, 0)
        parts.append(swap(whole, "tensor", bit))
    return parts


def split_masters(place, masters, kept, sent):
    half = kept.shape[1]
    for block in range(masters.shape[1]):
        turned = masters[0, block].T.astype(BF16)

        @pl.when(place[0] == 0)
        def _():
            kept[block] = turned[:half]
            sent[block] = turned[half:]

        @pl.when(place[0] != 0)
        def _():
            kept[block] = turned[half:]
            sent[block] = turned[:half]


def split_upstream(place, column, grad, kept, sent):
    count, half, side = kept.shape[0], kept.shape[1], kept.shape[2]

    def step(k, _):
        start = pl.multiple_of(column[0, k] * side, side)
        turned = grad[:, pl.ds(start, side)].T

        @pl.when(place[0] == 0)
        def _():
            kept[k] = turned[:half]
            sent[k] = turned[half:]

        @pl.when(place[0] != 0)
        def _():
            kept[k] = turned[half:]
            sent[k] = turned[:half]

        return 0

    lax.fori_loop(0, count, step, 0)


def select_rows(place, row, *refs):
    sources, chosen = refs[:-1], refs[-1]
    side = chosen.shape[2]
    per_shard = sources[0].shape[2] // side

    def step(k, _):
        shard = row[0, k] // per_shard
        start = pl.multiple_of((row[0, k] - shard * per_shard) * side, side)
        offset = shard ^ place[1]
        first = 0
        for source in sources:
            size = source.shape[0]

            @pl.when(jnp.logical_and(offset >= first, offset < first + size))
            def _():
                chosen[k] = source[offset - first, :, pl.ds(start, side)]

            first += size
        return 0

    lax.fori_loop(0, chosen.shape[0], step, 0)


def put(value, dst, sent, kept):
    @pl.when(dst >= 0)
    def _():
        sent[dst] = value.astype(BF16)

    @pl.when(dst < 0)
    def _():
        kept[-1 - dst] = value


def gradients(rows, table, *refs):
    (
        weight_a0, weight_a1, weight_b0, weight_b1, own_tokens, other_tokens, own_up, other_up,
        sent_a, kept_a, sent_b, kept_b, weights, total,
    ) = refs
    places, half = own_up.shape[0], own_up.shape[1]
    quarter = half // 2
    block_count = 2 * places
    tokens = own_tokens.shape[1]

    position = 0
    for source in (weight_a0, weight_a1, weight_b0, weight_b1):

        def order(p, _, source=source, position=position):
            block = table[rows["order"], position + p]
            up = (block >= places).astype(jnp.int32)
            start = pl.multiple_of(up * half, half)
            weights[block - up * places, pl.ds(start, half), :] = source[p]
            return 0

        lax.fori_loop(0, source.shape[0], order, 0, unroll=4)
        position += source.shape[0]

    contract_last = (((1,), (1,)), ((), ()))

    def forward(k, _):
        first = table[rows["first"], k]
        for n, source in enumerate((own_tokens, other_tokens)):
            part = lax.dot_general(weights[k], source[k], contract_last, preferred_element_type=F32)
            lanes = slice(n * tokens, (n + 1) * tokens)

            @pl.when(first == k)
            def _():
                total[k, :, lanes] = part

            @pl.when(first != k)
            def _():
                total[first, :, lanes] += part

        return 0

    lax.fori_loop(0, places, forward, 0)

    def backward(k, _):
        first = table[rows["first"], k]
        result = None
        for n, (source, upstream) in enumerate(((own_tokens, own_up), (other_tokens, other_up))):
            lanes = slice(n * tokens, (n + 1) * tokens)
            gate = total[first, :half, lanes]
            up = total[first, half:, lanes]
            sigmoid = 0.5 + 0.5 * jnp.tanh(0.5 * gate)
            scaled = upstream[k].astype(F32) * sigmoid
            gate_grad = scaled * up * (1.0 + gate * (1.0 - sigmoid))
            up_grad = scaled * gate
            both = jnp.concatenate([gate_grad.astype(BF16), up_grad.astype(BF16)], axis=0)
            term = jnp.dot(both, source[k], preferred_element_type=F32)
            result = term if result is None else result + term
        for which in range(2):
            block = k + which * places
            start = which * half
            put(result[start : start + quarter], table[rows["a"], block], sent_a, kept_a)
            put(result[start + quarter : start + half], table[rows["b"], block], sent_b, kept_b)
        return 0

    lax.fori_loop(0, places, backward, 0)


def combine(row, count_at, pieces, table, *refs):
    kept_in, received, sent, kept = refs[:pieces], refs[pieces : 2 * pieces], refs[-2], refs[-1]

    def step(r, _):
        value = [kept_in[n][r] + received[n][r].astype(F32) for n in range(pieces)]
        put(value[0] if pieces == 1 else jnp.concatenate(value, 0), table[row, r], sent, kept)
        return 0

    lax.fori_loop(0, table[count_at[0], count_at[1]], step, 0)


def finish(count_at, place, table, kept, received, out):
    count = table[count_at[0], count_at[1]]
    for slot in range(out.shape[1]):

        @pl.when(slot < count)
        def _():
            mine, other = kept[slot], received[slot].astype(F32)
            swapped = place[0] != 0
            low = jnp.where(swapped, other, mine)
            high = jnp.where(swapped, mine, other)
            out[0, slot] = jnp.concatenate([low, high], axis=0).T

        @pl.when(slot >= count)
        def _():
            out[0, slot] = jnp.zeros(out.shape[2:], F32)


def axes_of(owner_count):
    bits = owner_count.bit_length() - 1
    if bits == 4:
        return 2, (0, 1), (3,)
    return 0, (bits - 1, 1), tuple(b for b in range(2, bits - 1))


def rank(mask):
    count = mask.shape[0]
    earlier = np.tril(np.ones((count, count), bool), -1)
    return jnp.sum(jnp.logical_and(mask[None, :], earlier).astype(jnp.int32), axis=1, dtype=jnp.int32)


def plan(owner, column, me, order, bits):
    pair, (bit_a, bit_b), rest = bits
    block_count = owner.shape[0]
    differs = owner ^ me

    def alive(done):
        return (differs & sum(1 << b for b in done)) == 0

    def target(done, bit):
        live, away = alive(done), ((differs >> bit) & 1) == 1
        send, keep = jnp.logical_and(live, away), jnp.logical_and(live, jnp.logical_not(away))
        return jnp.where(send, rank(send), -1 - rank(keep))

    def listed(done, values):
        live = alive(done)
        place = rank(live)
        hit = jnp.logical_and(live[None, :], place[None, :] == np.arange(block_count)[:, None])
        return jnp.sum(jnp.where(hit, values[None, :], 0), axis=1, dtype=jnp.int32)

    rows, table, counts = {}, [], {}

    def add(name, values):
        rows[name] = len(table)
        table.append(jnp.pad(values.astype(jnp.int32), (0, block_count - values.shape[0])))

    def add_count(name, done):
        counts[name] = (-1, len(counts)), jnp.sum(alive(done).astype(jnp.int32), dtype=jnp.int32)

    add("order", order)
    places = column.shape[0]
    same = column[:, None] == column[None, :]
    add("first", jnp.min(jnp.where(same, np.arange(places, dtype=np.int32)[None, :], places), axis=1))
    add("a", target((), bit_a))
    add("b", target((), bit_b))
    steps = [("a2", (bit_a,), bit_b), ("b2", (bit_b,), bit_a)]
    done = (bit_a, bit_b)
    for bit in (*rest, pair):
        steps.append((f"s{len(done)}", done, bit))
        done = (*done, bit)
    for name, before, bit in steps:
        add(name, listed(before, target(before, bit)))
        add_count(name, before)
    add_count("end", done)
    last = len(table)
    table.append(jnp.pad(jnp.stack([c for _, c in counts.values()]), (0, block_count - len(counts))))
    return rows, {n: (last, at[1]) for n, (at, _) in counts.items()}, jnp.stack(table), steps


def most(owner, done):
    group = owner & sum(1 << b for b in done)
    return jnp.max(jnp.sum((group[:, None] == group[None, :]).astype(jnp.int32), axis=1, dtype=jnp.int32))


def local(tokens, hidden_grad, masters, block_row, block_col, owners):
    owner_count = lax.axis_size("dp")
    me = lax.axis_index("dp")
    bits = axes_of(owner_count)
    pair, (bit_a, bit_b), rest = bits
    own_blocks, side = masters.shape[1], masters.shape[2]
    places, half, quarter = block_row.shape[1], side // 2, side // 4
    block_count = owners.shape[1]
    token_count = tokens.shape[0]
    capacity = 3 * block_count // owner_count
    place = jnp.stack([(me >> pair) & 1, lax.axis_index("tensor")]).astype(jnp.int32)

    def struct(shape, dtype):
        return jax.ShapeDtypeStruct(shape, dtype)

    with jax.named_scope("weights"):
        kept, sent = call(
            split_masters, "split_masters", [struct((own_blocks, half, side), BF16)] * 2, [SMEM, VMEM], [place, masters]
        )
        entries = [(0, b) for b in range(own_blocks)]

        def moved(bit):
            return [(delta ^ (1 << bit), b) for delta, b in entries]

        current = jnp.concatenate([kept, swap(sent, "dp", pair)], 0)
        entries += moved(pair)
        for bit in rest[:0:-1]:
            current = jnp.concatenate([current, swap(current, "dp", bit)], 0)
            entries += moved(bit)
        base, first_part = entries, current
        second_part = swap(current, "dp", rest[0])
        entries = base
        a0 = jnp.concatenate([first_part, swap(first_part, "dp", bit_a)], 0)
        entries_a = base + moved(bit_a)
        entries = entries_a
        entries_a = entries_a + moved(bit_b)
        entries = base
        base_b = moved(rest[0])
        entries = base_b
        entries_b = base_b + moved(bit_b)
        entries = entries_b
        entries_b = entries_b + moved(bit_a)
        b0 = jnp.concatenate([second_part, swap(second_part, "dp", bit_b)], 0)
        a1, b1 = swap(a0, "dp", bit_b), swap(b0, "dp", bit_a)
        found = entries_a + entries_b
        order = (me ^ np.array([d for d, _ in found], np.int32)) * own_blocks + np.array([b for _, b in found], np.int32)

    with jax.named_scope("tokens"):
        other = swap(tokens, "dp", pair)
        chosen = [
            call(
                select_rows, "select_rows", [struct((places, token_count, side), BF16)],
                [SMEM, SMEM] + [VMEM] * len(parts), [place, block_row, *parts],
            )[0]
            for parts in (spread(tokens), spread(other))
        ]

    with jax.named_scope("upstream"):
        own_up, sent_up = call(
            split_upstream, "split_upstream", [struct((places, half, token_count), BF16)] * 2,
            [SMEM, SMEM, VMEM], [place, block_col, hidden_grad],
        )
        other_up = swap(sent_up, "dp", pair)

    with jax.named_scope("plan"):
        rows, count_at, table, steps = plan(owners[0], block_col[0], me, order, bits)

        def full(done):
            return min(block_count, (owner_count >> len(done)) * capacity)

        def usual(done):
            return min(full(done), (block_count >> len(done)) + capacity)

        fits = jnp.bool_(True)
        for _, done, _ in steps:
            if done and usual(done) < full(done):
                fits = jnp.logical_and(fits, most(owners[0], done) <= usual(done))
        fits = fits.astype(jnp.int32).reshape(1, 1)
        for bit in range(lax.axis_size("tensor").bit_length() - 1):
            fits = jnp.minimum(fits, swap(fits, "tensor", bit))

    def reduce(size, *args):
        (table, place, *inputs) = args
        outs = []
        for bit in (bit_a, bit_b):
            room = size((bit,))
            outs += [struct((room, quarter, side), BF16), struct((room, quarter, side), F32)]
        work = 2 * 2 * places * side * side * 2 * token_count
        sent_a, kept_a, sent_b, kept_b = call(
            functools.partial(gradients, rows), "gradients", outs, [SMEM] + [VMEM] * 8, [table, *inputs], work,
            [pltpu.VMEM((places, side, side), BF16), pltpu.VMEM((places, side, 2 * token_count), F32)],
        )

        def join(name, done, kept_in, received):
            pieces = len(kept_in)
            room, height = size(done), sum(k.shape[1] for k in kept_in)
            return call(
                functools.partial(combine, rows[name], count_at[name], pieces), "combine",
                [struct((room, height, side), BF16), struct((room, height, side), F32)],
                [SMEM] + [VMEM] * (2 * pieces), [table, *kept_in, *received],
            )

        got_a, got_b = swap(sent_a, "dp", bit_a), swap(sent_b, "dp", bit_b)
        both = (bit_a, bit_b)
        sent_a, kept_a = join("a2", both, [kept_a], [got_a])
        got_a = swap(sent_a, "dp", bit_b)
        sent_b, kept_b = join("b2", both, [kept_b], [got_b])
        got_b = swap(sent_b, "dp", bit_a)
        kept, got, done = [kept_a, kept_b], [got_a, got_b], both
        for name, _, bit in steps[2:]:
            done = (*done, bit)
            sent, held = join(name, done, kept, got)
            kept, got = [held], [swap(sent, "dp", bit)]
        return call(
            functools.partial(finish, count_at["end"]), "finish", [struct((1, capacity, side, side), F32)],
            [SMEM, SMEM, VMEM, VMEM], [place, table, kept[0], got[0]],
        )[0]

    operands = (table, place, a0, a1, b0, b1, *chosen, own_up, other_up)
    return lax.cond(
        fits[0, 0] == 1, functools.partial(reduce, usual), functools.partial(reduce, full), *operands
    )


def solution(mesh):
    return jax.shard_map(
        local,
        mesh=mesh,
        in_specs=(
            P("dp", "tensor"),
            P("dp", "tensor"),
            P("tensor", "dp", None, None),
            P("tensor", None),
            P("tensor", None),
            P("tensor", None),
        ),
        out_specs=P("tensor", "dp", None, None),
        check_vma=False,
    )
```

time: 283 us -> 123 us (0.43)
  waiting for transfers between devices: 222 us -> 46.9 us
  Pallas kernels: 0 us -> 33 us
  matrix products: 17.1 us -> 0 us
  starting transfers between devices: 0.09 us -> 16.9 us
  local copies, waits for them, and re-layouts: 25.8 us -> 12.8 us
  between operations: 13.2 us -> 3.33 us
  other arithmetic: 4.02 us -> 9.7 us
    psum x1 -> x0, waiting for transfers between devices: 166 us -> none  [local(): summed = lax.psum(block_grads, 'dp')]
    all_gather x2 -> x0, waiting for transfers between devices: 55.5 us -> none  [the longest x1 55.5 us: local(): lax.all_gather(masters.astype(jnp.bfloat16), 'dp', axis=1, tiled=True)[0]]
    ppermute x0 -> x17, waiting for transfers between devices: none -> 46.9 us  [swap(): return lax.ppermute(value, axis, [(i, i ^ 1 << bit) for i in range(size)])]
    pallas_call x0 -> x10, Pallas kernels: none -> 33 us  [call(): pl.pallas_call(body, name=name, out_shape=tuple(outs), in_specs=in_specs,...]
    dot_general x7 -> x0, matrix products: 17.1 us -> none  [the longest x2 7.25 us: column_total(): jnp.einsum('tjc,kj->tkc', part, same_column, precision=lax.Precision.HIGH...]
    ppermute x0 -> x17, starting transfers between devices: none -> 16.9 us  [swap(): return lax.ppermute(value, axis, [(i, i ^ 1 << bit) for i in range(size)])]
    reshape x2 -> x0, local copies, waits for them, and re-layouts: 9.36 us -> none  [the longest x1 6.14 us: local(): hidden_grad.reshape(token_count, hidden_grad.shape[1] // block_side, bloc...]
    another operation x0 -> x3, local copies, waits for them, and re-layouts: none -> 4.54 us  [the longest x1 3.18 us: plan(): jnp.stack([c for _, c in counts.values()])]
  transfers between devices with their start and end apart: 3 -> 17, of which waited for: 2 -> 8; matrix products, arithmetic and copies ran while one was open for 8% -> 14% of each run, Pallas kernels for 0% -> 9%
where the time goes in v1:
time: 123 us
  waiting for transfers between devices  46.9 us (38%)
  Pallas kernels  33 us (27%)
  starting transfers between devices  16.9 us (14%)
  local copies, waits for them, and re-layouts  12.8 us (10%)
  other arithmetic  9.7 us (8%)
  between operations  3.33 us (3%)
    ppermute x17, waiting for transfers between devices, swap(): return lax.ppermute(value, axis, [(i, i ^ 1 << bit) for i in range(size)])  46.9 us
    pallas_call x10, Pallas kernels, call(): pl.pallas_call(body, name=name, out_shape=tuple(outs), in_specs=in_specs,...  33 us
    ppermute x17, starting transfers between devices, swap(): return lax.ppermute(value, axis, [(i, i ^ 1 << bit) for i in range(size)])  16.9 us
    unnamed x24, local copies, waits for them, and re-layouts  6 us
    another operation x1, local copies, waits for them, and re-layouts, plan(): jnp.stack([c for _, c in counts.values()])  3.18 us
    reduce_max x4, other arithmetic, most(): jnp.max(jnp.sum((group[:, None] == group[None, :]).astype(jnp.int32), axi...  2.64 us
  transfers between devices with their start and end apart: 17, of which 8 were waited for; matrix products, arithmetic and copies ran while one was open for 14% of the time, Pallas kernels for 9%

profile of v1, /device:TPU:0, one launch (start us, length us, event | category | flops | bytes accessed | tf_op | source)
XLA Modules:
  0.0 122.7 jit_solution(17782012992230661947)
XLA Ops:
  0.0 3.0 %collective-permute-start.20 = (bf16[128,4096]{1,0:T(8,128)(2,1)}, bf16[128,4096]{1,0:T(8,128)(2,1)S(1)}, u32[]{:S(2)}, u32[]{:S(2)}) collective-permute-start(bf16[128,4096]{1,0:T(8,128)(2,1)} %param.31), channel_id=1, source_target_pairs={{0,8},{2,10},{4,12},{6,14},{8,0},{10,2},{12,4},{14,6},{16,24},{18,... | collective-permute-start | bytes 3145736 | tf_op jit(solution)/shard_map/tokens/ppermute | solution.py:34
  3.0 1.4 %fusion.5 = (s32[]{:T(128)}, s32[]{:T(128)}, s32[]{:T(128)}, s32[]{:T(128)}, s32[]{:T(128)}, /*index=5*/s32[1,64]{1,0:T(1,128)S(1)}, s32[64]{0:T(128)S(1)}, s32[64]{0:T(128)S(1)}, s32[64]{0:T(128)S(1)}, s32[64]{0:T(128)S(1)}) fusion(s32[1,64]{1,0:T(1,128)} %param.36, s32[]{:T(128)S(6)} %axis_index.23), kind=kLoop, calls=%fused_computation.50 | loop fusion | flops 1595 | bytes 1560 | tf_op jit(solution)/shard_map/plan/reduce_sum | solution.py:250
  4.5 0.2 convert_reduce_fusion.16
  4.6 0.7 reduce_max.38
  5.4 0.6 reduce_max.39
  6.0 0.2 convert_reduce_fusion.18
  6.2 0.6 reduce_max.36
  6.8 0.7 reduce_max.37
  10.0 1.0 collective-permute-start.12
  11.0 0.1 pad_add_fusion.place
  11.1 0.9 copy-done.2
  12.1 0.9 split_masters.1
  13.0 0.1 collective-permute-start.13
  13.1 0.6 collective-permute-start.19
  13.7 0.6 constant_dynamic-update-slice_fusion.1
  14.3 1.1 convert_reduce_fusion.2
  15.4 0.6 fusion.6
  16.0 11.1 %collective-permute-done.20 = bf16[128,4096]{1,0:T(8,128)(2,1)S(1)} collective-permute-done((bf16[128,4096]{1,0:T(8,128)(2,1)}, bf16[128,4096]{1,0:T(8,128)(2,1)S(1)}, u32[]{:S(2)}, u32[]{:S(2)}) %collective-permute-start.20) | collective-permute-done | bytes 1048608 | tf_op jit(solution)/shard_map/tokens/ppermute | solution.py:34
  27.1 0.7 select_reduce_fusion.2
  27.8 0.0 collective-permute-done.13
  27.8 0.6 constant_dynamic-update-slice_fusion
  28.4 2.8 %collective-permute-start.16 = (bf16[8,64,128]{2,1,0:T(8,128)(2,1)}, bf16[8,64,128]{2,1,0:T(8,128)(2,1)S(1)}, u32[]{:S(2)}, u32[]{:S(2)}) collective-permute-start(bf16[8,64,128]{2,1,0:T(8,128)(2,1)} %get-tuple-element.123), channel_id=1, source_target_pairs={{0,16},{2,18},{4,20},{6,22},{8,24},{10,26},{12,28},{14,30},{16,0},... | collective-permute-start | bytes 393224 | tf_op jit(solution)/shard_map/weights/ppermute | solution.py:34
  31.2 0.6 select_reduce_fusion
  31.8 1.5 %collective-permute-start.14 = (bf16[8,64,128]{2,1,0:T(8,128)(2,1)}, bf16[8,64,128]{2,1,0:T(8,128)(2,1)}, u32[]{:S(2)}, u32[]{:S(2)}) collective-permute-start(bf16[8,64,128]{2,1,0:T(8,128)(2,1)} %get-tuple-element.123), channel_id=1, source_target_pairs={{0,2},{2,0},{4,6},{6,4},{8,10},{10,8},{12,14},{14,12},{16,18},{18,... | collective-permute-start | bytes 393224 | tf_op jit(solution)/shard_map/weights/ppermute | solution.py:34
  33.3 1.5 %fusion.4 = s32[32]{0:T(128)} fusion(s32[32]{0:T(128)} %bitcast.106), kind=kLoop, calls=%fused_computation.40 | loop fusion | flops 3040 | bytes 256 | tf_op jit(solution)/shard_map/plan/reduce_min | solution.py:255
  34.8 2.0 %copy-done = bf16[128,14336]{1,0:T(8,128)(2,1)S(1)} copy-done((bf16[128,14336]{1,0:T(8,128)(2,1)S(1)}, bf16[128,14336]{1,0:T(8,128)(2,1)}, u32[]{:S(2)}) %copy-start) | copy-done | bytes 3670040
  36.9 0.7 copy-done.4
  37.5 4.0 %split_upstream.1 = (bf16[32,64,128]{2,1,0:T(8,128)(2,1)}, bf16[32,64,128]{2,1,0:T(8,128)(2,1)S(1)}) custom-call(s32[2]{0:T(128)S(1)} %pad_add_fusion.place, s32[1,32]{1,0:T(1,128)S(1)} %copy-done.4, bf16[128,14336]{1,0:T(8,128)(2,1)S(1)} %copy-done), custom_call_target="tpu_custom_call" | custom-call | bytes 4718728 | tf_op jit(solution)/shard_map/upstream/split_upstream/pallas_call | solution.py:20
  41.6 0.8 copy-done.5
  42.4 3.2 %stack.64 = s32[5]{0:T(128)S(1)} concatenate(s32[1]{0:T(128)} %bitcast.45, s32[1]{0:T(128)} %bitcast.46, s32[1]{0:T(128)} %bitcast.47, s32[1]{0:T(128)} %bitcast.48, s32[1]{0:T(128)} %bitcast.49), dimensions={0} | concatenate | bytes 40 | tf_op jit(solution)/shard_map/plan/stack | solution.py:268
  45.6 1.5 %collective-permute-start.17 = (bf16[8,64,128]{2,1,0:T(8,128)(2,1)S(1)}, bf16[8,64,128]{2,1,0:T(8,128)(2,1)S(1)}, u32[]{:S(2)}, u32[]{:S(2)}) collective-permute-start(bf16[8,64,128]{2,1,0:T(8,128)(2,1)S(1)} %collective-permute-done.16), channel_id=1, source_target_pairs={{0,4},{2,6},{4,0},{6,2},{8,12},{10,14},{12,8},{14,10},{16,20},{18,... | collective-permute-start | bytes 393224 | tf_op jit(solution)/shard_map/weights/ppermute | solution.py:34
  47.1 0.0 collective-permute-done.14
  47.1 1.4 %collective-permute-start.22 = (bf16[32,64,128]{2,1,0:T(8,128)(2,1)}, bf16[32,64,128]{2,1,0:T(8,128)(2,1)}, u32[]{:S(2)}, u32[]{:S(2)}) collective-permute-start(bf16[32,64,128]{2,1,0:T(8,128)(2,1)} %copy-done.5), channel_id=1, source_target_pairs={{0,8},{2,10},{4,12},{6,14},{8,0},{10,2},{12,4},{14,6},{16,24},{18,... | collective-permute-start | bytes 1572872 | tf_op jit(solution)/shard_map/upstream/ppermute | solution.py:34
  48.5 1.6 %constant_dynamic-update-slice_fusion.2 = bf16[16,64,128]{2,1,0:T(8,128)(2,1)} fusion(bf16[16,64,128]{2,1,0:T(8,128)(2,1)} %copy-done.7, bf16[8,64,128]{2,1,0:T(8,128)(2,1)} %collective-permute-done.14), kind=kLoop, calls=%fused_computation.34 | loop fusion | bytes 262144 | tf_op jit(solution)/shard_map/weights/concatenate | solution.py:309
  50.1 0.8 collective-permute-done.17
  50.9 1.5 %collective-permute-start.15 = (bf16[16,64,128]{2,1,0:T(8,128)(2,1)}, bf16[16,64,128]{2,1,0:T(8,128)(2,1)}, u32[]{:S(2)}, u32[]{:S(2)}) collective-permute-start(bf16[16,64,128]{2,1,0:T(8,128)(2,1)} %constant_dynamic-update-slice_fusion.2), channel_id=1, source_target_pairs={{0,4},{2,6},{4,0},{6,2},{8,12},{10,14},{12,8},{14,10},{16,20},{18,... | collective-permute-start | bytes 786440 | tf_op jit(solution)/shard_map/weights/ppermute | solution.py:34
  52.4 0.6 collective-permute-start.18
  53.0 0.7 pad_bitcast_fusion
  53.7 0.7 add_bitcast_fusion
  54.4 0.7 stack.66
  55.7 0.0 collective-permute-done.19.refs_1_
  55.7 1.6 %select_rows.2 = bf16[32,128,128]{2,1,0:T(8,128)(2,1)S(1)} custom-call(s32[2]{0:T(128)S(1)} %pad_add_fusion.place, s32[1,32]{1,0:T(1,128)S(1)} %copy-done.3, bf16[1,128,4096]{2,1,0:T(8,128)(2,1)S(1)} %bitcast.103, bf16[1,128,4096]{2,1,0:T(8,128)(2,1)S(1)} %collective-permute-done.19.refs_1_), custom_call_target="tpu_custom_call" | custom-call | bytes 3145864 | tf_op jit(solution)/shard_map/tokens/select_rows/pallas_call | solution.py:20
  57.4 2.3 %select_rows.3 = bf16[32,128,128]{2,1,0:T(8,128)(2,1)S(1)} custom-call(s32[2]{0:T(128)S(1)} %pad_add_fusion.place, s32[1,32]{1,0:T(1,128)S(1)} %copy-done.3, bf16[1,128,4096]{2,1,0:T(8,128)(2,1)S(1)} %bitcast.105, bf16[1,128,4096]{2,1,0:T(8,128)(2,1)} %collective-permute-done.21.refs_1_), custom_call_target="tpu_custom_call" | custom-call | bytes 3145864 | tf_op jit(solution)/shard_map/tokens/select_rows/pallas_call | solution.py:20
  59.7 1.2 %collective-permute-done.22 = bf16[32,64,128]{2,1,0:T(8,128)(2,1)} collective-permute-done((bf16[32,64,128]{2,1,0:T(8,128)(2,1)}, bf16[32,64,128]{2,1,0:T(8,128)(2,1)}, u32[]{:S(2)}, u32[]{:S(2)}) %collective-permute-start.22) | collective-permute-done | bytes 524320 | tf_op jit(solution)/shard_map/upstream/ppermute | solution.py:34
  61.0 60.8 %conditional.1 = (f32[1,12,128,128]{3,2,1,0:T(8,128)S(1)}) conditional(s32[]{:T(128)} %bitcast.5, (s32[9,64]{1,0:T(8,128)S(1)}, bf16[16,64,128]{2,1,0:T(8,128)(2,1)S(1)}, bf16[16,64,128]{2,1,0:T(8,128)(2,1)}, bf16[16,64,128]{2,1,0:T(8,128)(2,1)S(1)}, bf16[16,64,128]{2,1,0:T(8,128)(2,1)}, /*index=5*/bf16[32,128,128]{2,1,0:T(8,128)(2,1)S(1)}, ...), branch_computations={%region_34.35_spmd, %region_35.36_spmd} | conditional | flops 536870912 | bytes 29243136 | solution.py:396
  61.0 18.6 %gradients.3 = (bf16[44,32,128]{2,1,0:T(8,128)(2,1)S(1)}, f32[44,32,128]{2,1,0:T(8,128)S(1)}, bf16[44,32,128]{2,1,0:T(8,128)(2,1)S(1)}, f32[44,32,128]{2,1,0:T(8,128)S(1)}) custom-call(s32[9,64]{1,0:T(8,128)S(1)} %get-tuple-element.71.table, bf16[16,64,128]{2,1,0:T(8,128)(2,1)S(1)} %get-tuple-element.72.refs_0_, ...), custom_call_target="tpu_custom_call" | custom-call | flops 536870912 | bytes 6359296 | tf_op jit(solution)/shard_map/cond/branch_1_fun/gradients/pallas_call | solution.py:20
  79.6 0.6 collective-permute-start.6
  80.2 0.5 collective-permute-start.7
  80.7 8.0 %collective-permute-done.6.refs_1_ = bf16[44,32,128]{2,1,0:T(8,128)(2,1)S(1)} collective-permute-done((bf16[44,32,128]{2,1,0:T(8,128)(2,1)S(1)}, bf16[44,32,128]{2,1,0:T(8,128)(2,1)S(1)}, u32[]{:S(2)}, u32[]{:S(2)}) %collective-permute-start.6) | collective-permute-done | bytes 360480 | tf_op jit(solution)/shard_map/cond/branch_1_fun/ppermute | solution.py:34
  88.7 1.3 %combine.12 = (bf16[28,32,128]{2,1,0:T(8,128)(2,1)S(1)}, f32[28,32,128]{2,1,0:T(8,128)S(1)}) custom-call(s32[9,64]{1,0:T(8,128)S(1)} %get-tuple-element.71.table, f32[44,32,128]{2,1,0:T(8,128)S(1)} %get-tuple-element.80.refs_0_, bf16[44,32,128]{2,1,0:T(8,128)(2,1)S(1)} %collective-permute-done.6.refs_1_), custom_call_target="tpu_custom_call" | custom-call | bytes 1771776 | tf_op jit(solution)/shard_map/cond/branch_1_fun/combine/pallas_call | solution.py:20
  90.0 0.6 collective-permute-start.8
  90.6 1.2 combine.13
  91.8 0.7 collective-permute-start.9
  92.5 3.6 %collective-permute-done.8.refs_2_ = bf16[28,32,128]{2,1,0:T(8,128)(2,1)S(1)} collective-permute-done((bf16[28,32,128]{2,1,0:T(8,128)(2,1)S(1)}, bf16[28,32,128]{2,1,0:T(8,128)(2,1)S(1)}, u32[]{:S(2)}, u32[]{:S(2)}) %collective-permute-start.8) | collective-permute-done | bytes 229408 | tf_op jit(solution)/shard_map/cond/branch_1_fun/ppermute | solution.py:34
  96.1 1.8 %collective-permute-done.9.refs_3_ = bf16[28,32,128]{2,1,0:T(8,128)(2,1)S(1)} collective-permute-done((bf16[28,32,128]{2,1,0:T(8,128)(2,1)S(1)}, bf16[28,32,128]{2,1,0:T(8,128)(2,1)S(1)}, u32[]{:S(2)}, u32[]{:S(2)}) %collective-permute-start.9) | collective-permute-done | bytes 229408 | tf_op jit(solution)/shard_map/cond/branch_1_fun/ppermute | solution.py:34
  97.9 0.9 combine.14
  98.8 0.4 collective-permute-start.10
  99.2 14.3 %collective-permute-done.10.refs_1_ = bf16[20,64,128]{2,1,0:T(8,128)(2,1)S(1)} collective-permute-done((bf16[20,64,128]{2,1,0:T(8,128)(2,1)S(1)}, bf16[20,64,128]{2,1,0:T(8,128)(2,1)S(1)}, u32[]{:S(2)}, u32[]{:S(2)}) %collective-permute-start.10) | collective-permute-done | bytes 327712 | tf_op jit(solution)/shard_map/cond/branch_1_fun/ppermute | solution.py:34
  113.6 0.8 combine.15
  114.4 0.1 collective-permute-start.11
  114.5 6.1 %collective-permute-done.11.received = bf16[12,64,128]{2,1,0:T(8,128)(2,1)S(1)} collective-permute-done((bf16[12,64,128]{2,1,0:T(8,128)(2,1)S(1)}, bf16[12,64,128]{2,1,0:T(8,128)(2,1)S(1)}, u32[]{:S(2)}, u32[]{:S(2)}) %collective-permute-start.11) | collective-permute-done | bytes 196640 | tf_op jit(solution)/shard_map/cond/branch_1_fun/ppermute | solution.py:34
  120.5 1.3 %finish.3 = f32[1,12,128,128]{3,2,1,0:T(8,128)S(1)} custom-call(s32[2]{0:T(128)S(1)} %get-tuple-element.70.place, s32[9,64]{1,0:T(8,128)S(1)} %get-tuple-element.71.table, f32[12,64,128]{2,1,0:T(8,128)S(1)} %get-tuple-element.90.kept, bf16[12,64,128]{2,1,0:T(8,128)(2,1)S(1)} %collective-permute-done.11.received), custom_call_target="tpu_custom_call" | custom-call | bytes 1378568 | tf_op jit(solution)/shard_map/cond/branch_1_fun/finish/pallas_call | solution.py:20
  121.8 0.0 copy-start.9
  121.8 0.9 copy-done.9
  (26 shorter events, 0.1 us)
Async XLA Ops:
  0.0 55.7 %copy-start.3 = (s32[1,32]{1,0:T(1,128)S(1)}, s32[1,32]{1,0:T(1,128)}, u32[]{:S(2)}) copy-start(s32[1,32]{1,0:T(1,128)} %row.3) | copy-start | bytes 388
  0.0 27.1 %collective-permute-start.20 = (bf16[128,4096]{1,0:T(8,128)(2,1)}, bf16[128,4096]{1,0:T(8,128)(2,1)S(1)}, u32[]{:S(2)}, u32[]{:S(2)}) collective-permute-start(bf16[128,4096]{1,0:T(8,128)(2,1)} %param.31), channel_id=1, source_target_pairs={{0,8},{2,10},{4,12},{6,14},{8,0},{10,2},{12,4},{14,6},{16,24},{18,... | collective-permute-start | bytes 3145736 | tf_op jit(solution)/shard_map/tokens/ppermute | solution.py:34
  10.0 42.4 %collective-permute-start.12 = (s32[1,1]{1,0:T(1,128)}, s32[1,1]{1,0:T(1,128)}, u32[]{:S(2)}, u32[]{:S(2)}) collective-permute-start(s32[1,1]{1,0:T(1,128)} %bitcast.4), channel_id=1, source_target_pairs={{0,1},{1,0},{2,3},{3,2},{4,5},{5,4},{6,7},{7,6},{8,9},{9,8},{10,11... | collective-permute-start | bytes 20 | tf_op jit(solution)/shard_map/plan/ppermute | solution.py:34
  11.1 0.9 copy-start.2
  13.0 14.8 %collective-permute-start.13 = (bf16[4,64,128]{2,1,0:T(8,128)(2,1)S(1)}, bf16[4,64,128]{2,1,0:T(8,128)(2,1)S(1)}, u32[]{:S(2)}, u32[]{:S(2)}) collective-permute-start(bf16[4,64,128]{2,1,0:T(8,128)(2,1)S(1)} %get-tuple-element.97), channel_id=1, source_target_pairs={{0,8},{2,10},{4,12},{6,14},{8,0},{10,2},{12,4},{14,6},{16,24},{18,... | collective-permute-start | bytes 196616 | tf_op jit(solution)/shard_map/weights/ppermute | solution.py:34
  13.1 42.6 %collective-permute-start.19 = (bf16[1,128,4096]{2,1,0:T(8,128)(2,1)}, bf16[1,128,4096]{2,1,0:T(8,128)(2,1)S(1)}, u32[]{:S(2)}, u32[]{:S(2)}) collective-permute-start(bf16[1,128,4096]{2,1,0:T(8,128)(2,1)} %bitcast.102), channel_id=1, source_target_pairs={{0,1},{1,0},{2,3},{3,2},{4,5},{5,4},{6,7},{7,6},{8,9},{9,8},{10,11... | collective-permute-start | bytes 3145736 | tf_op jit(solution)/shard_map/tokens/ppermute | solution.py:34
  27.1 30.3 %collective-permute-start.21 = (bf16[1,128,4096]{2,1,0:T(8,128)(2,1)S(1)}, bf16[1,128,4096]{2,1,0:T(8,128)(2,1)}, u32[]{:S(2)}, u32[]{:S(2)}) collective-permute-start(bf16[1,128,4096]{2,1,0:T(8,128)(2,1)S(1)} %bitcast.104), channel_id=1, source_target_pairs={{0,1},{1,0},{2,3},{3,2},{4,5},{5,4},{6,7},{7,6},{8,9},{9,8},{10,11... | collective-permute-start | bytes 3145736 | tf_op jit(solution)/shard_map/tokens/ppermute | solution.py:34
  28.4 4.9 %copy-start.7 = (bf16[16,64,128]{2,1,0:T(8,128)(2,1)}, bf16[16,64,128]{2,1,0:T(8,128)(2,1)S(1)}, u32[]{:S(2)}) copy-start(bf16[16,64,128]{2,1,0:T(8,128)(2,1)S(1)} %get-tuple-element.124) | copy-start | bytes 786436
  28.4 17.1 %collective-permute-start.16 = (bf16[8,64,128]{2,1,0:T(8,128)(2,1)}, bf16[8,64,128]{2,1,0:T(8,128)(2,1)S(1)}, u32[]{:S(2)}, u32[]{:S(2)}) collective-permute-start(bf16[8,64,128]{2,1,0:T(8,128)(2,1)} %get-tuple-element.123), channel_id=1, source_target_pairs={{0,16},{2,18},{4,20},{6,22},{8,24},{10,26},{12,28},{14,30},{16,0},... | collective-permute-start | bytes 393224 | tf_op jit(solution)/shard_map/weights/ppermute | solution.py:34
  31.8 21.9 %copy-start.10 = (s32[64]{0:T(128)S(1)}, s32[64]{0:T(128)}, u32[]{:S(2)}) copy-start(s32[64]{0:T(128)} %constant.52.clone) | copy-start | bytes 772
  31.8 15.3 %collective-permute-start.14 = (bf16[8,64,128]{2,1,0:T(8,128)(2,1)}, bf16[8,64,128]{2,1,0:T(8,128)(2,1)}, u32[]{:S(2)}, u32[]{:S(2)}) collective-permute-start(bf16[8,64,128]{2,1,0:T(8,128)(2,1)} %get-tuple-element.123), channel_id=1, source_target_pairs={{0,2},{2,0},{4,6},{6,4},{8,10},{10,8},{12,14},{14,12},{16,18},{18,... | collective-permute-start | bytes 393224 | tf_op jit(solution)/shard_map/weights/ppermute | solution.py:34
  34.8 2.0 %copy-start = (bf16[128,14336]{1,0:T(8,128)(2,1)S(1)}, bf16[128,14336]{1,0:T(8,128)(2,1)}, u32[]{:S(2)}) copy-start(bf16[128,14336]{1,0:T(8,128)(2,1)} %grad.1) | copy-start | bytes 11010052
  36.9 0.7 copy-start.4
  37.5 18.2 %copy-start.1 = (bf16[128,4096]{1,0:T(8,128)(2,1)S(1)}, bf16[128,4096]{1,0:T(8,128)(2,1)}, u32[]{:S(2)}) copy-start(bf16[128,4096]{1,0:T(8,128)(2,1)} %param.31) | copy-start | bytes 3145732
  41.6 0.8 copy-start.5
  45.6 5.3 %collective-permute-start.17 = (bf16[8,64,128]{2,1,0:T(8,128)(2,1)S(1)}, bf16[8,64,128]{2,1,0:T(8,128)(2,1)S(1)}, u32[]{:S(2)}, u32[]{:S(2)}) collective-permute-start(bf16[8,64,128]{2,1,0:T(8,128)(2,1)S(1)} %collective-permute-done.16), channel_id=1, source_target_pairs={{0,4},{2,6},{4,0},{6,2},{8,12},{10,14},{12,8},{14,10},{16,20},{18,... | collective-permute-start | bytes 393224 | tf_op jit(solution)/shard_map/weights/ppermute | solution.py:34
  47.1 13.8 %collective-permute-start.22 = (bf16[32,64,128]{2,1,0:T(8,128)(2,1)}, bf16[32,64,128]{2,1,0:T(8,128)(2,1)}, u32[]{:S(2)}, u32[]{:S(2)}) collective-permute-start(bf16[32,64,128]{2,1,0:T(8,128)(2,1)} %copy-done.5), channel_id=1, source_target_pairs={{0,8},{2,10},{4,12},{6,14},{8,0},{10,2},{12,4},{14,6},{16,24},{18,... | collective-permute-start | bytes 1572872 | tf_op jit(solution)/shard_map/upstream/ppermute | solution.py:34
  50.9 8.8 %collective-permute-start.15 = (bf16[16,64,128]{2,1,0:T(8,128)(2,1)}, bf16[16,64,128]{2,1,0:T(8,128)(2,1)}, u32[]{:S(2)}, u32[]{:S(2)}) collective-permute-start(bf16[16,64,128]{2,1,0:T(8,128)(2,1)} %constant_dynamic-update-slice_fusion.2), channel_id=1, source_target_pairs={{0,4},{2,6},{4,0},{6,2},{8,12},{10,14},{12,8},{14,10},{16,20},{18,... | collective-permute-start | bytes 786440 | tf_op jit(solution)/shard_map/weights/ppermute | solution.py:34
  52.4 8.5 %collective-permute-start.18 = (bf16[16,64,128]{2,1,0:T(8,128)(2,1)S(1)}, bf16[16,64,128]{2,1,0:T(8,128)(2,1)}, u32[]{:S(2)}, u32[]{:S(2)}) collective-permute-start(bf16[16,64,128]{2,1,0:T(8,128)(2,1)S(1)} %constant_dynamic-update-slice_fusion.5), channel_id=1, source_target_pairs={{0,2},{2,0},{4,6},{6,4},{8,10},{10,8},{12,14},{14,12},{16,18},{18,... | collective-permute-start | bytes 786440 | tf_op jit(solution)/shard_map/weights/ppermute | solution.py:34
  55.1 5.9 %copy-start.6 = (bf16[32,64,128]{2,1,0:T(8,128)(2,1)S(1)}, bf16[32,64,128]{2,1,0:T(8,128)(2,1)}, u32[]{:S(2)}) copy-start(bf16[32,64,128]{2,1,0:T(8,128)(2,1)} %get-tuple-element.98) | copy-start | bytes 1572868
  55.1 5.9 %copy-start.8 = (bf16[16,64,128]{2,1,0:T(8,128)(2,1)S(1)}, bf16[16,64,128]{2,1,0:T(8,128)(2,1)}, u32[]{:S(2)}) copy-start(bf16[16,64,128]{2,1,0:T(8,128)(2,1)} %constant_dynamic-update-slice_fusion.2) | copy-start | bytes 786436
  79.6 9.1 %collective-permute-start.6 = (bf16[44,32,128]{2,1,0:T(8,128)(2,1)S(1)}, bf16[44,32,128]{2,1,0:T(8,128)(2,1)S(1)}, u32[]{:S(2)}, u32[]{:S(2)}) collective-permute-start(bf16[44,32,128]{2,1,0:T(8,128)(2,1)S(1)} %get-tuple-element.81), channel_id=1, source_target_pairs={{0,2},{2,0},{4,6},{6,4},{8,10},{10,8},{12,14},{14,12},{16,18},{18,... | collective-permute-start | bytes 1081352 | tf_op jit(solution)/shard_map/cond/branch_1_fun/ppermute | solution.py:34
  80.2 10.4 %collective-permute-start.7 = (bf16[44,32,128]{2,1,0:T(8,128)(2,1)S(1)}, bf16[44,32,128]{2,1,0:T(8,128)(2,1)S(1)}, u32[]{:S(2)}, u32[]{:S(2)}) collective-permute-start(bf16[44,32,128]{2,1,0:T(8,128)(2,1)S(1)} %get-tuple-element.84), channel_id=1, source_target_pairs={{0,4},{2,6},{4,0},{6,2},{8,12},{10,14},{12,8},{14,10},{16,20},{18,... | collective-permute-start | bytes 1081352 | tf_op jit(solution)/shard_map/cond/branch_1_fun/ppermute | solution.py:34
  90.0 6.1 %collective-permute-start.8 = (bf16[28,32,128]{2,1,0:T(8,128)(2,1)S(1)}, bf16[28,32,128]{2,1,0:T(8,128)(2,1)S(1)}, u32[]{:S(2)}, u32[]{:S(2)}) collective-permute-start(bf16[28,32,128]{2,1,0:T(8,128)(2,1)S(1)} %get-tuple-element.86), channel_id=1, source_target_pairs={{0,4},{2,6},{4,0},{6,2},{8,12},{10,14},{12,8},{14,10},{16,20},{18,... | collective-permute-start | bytes 688136 | tf_op jit(solution)/shard_map/cond/branch_1_fun/ppermute | solution.py:34
  91.8 6.1 %collective-permute-start.9 = (bf16[28,32,128]{2,1,0:T(8,128)(2,1)S(1)}, bf16[28,32,128]{2,1,0:T(8,128)(2,1)S(1)}, u32[]{:S(2)}, u32[]{:S(2)}) collective-permute-start(bf16[28,32,128]{2,1,0:T(8,128)(2,1)S(1)} %get-tuple-element.87), channel_id=1, source_target_pairs={{0,2},{2,0},{4,6},{6,4},{8,10},{10,8},{12,14},{14,12},{16,18},{18,... | collective-permute-start | bytes 688136 | tf_op jit(solution)/shard_map/cond/branch_1_fun/ppermute | solution.py:34
  98.8 14.7 %collective-permute-start.10 = (bf16[20,64,128]{2,1,0:T(8,128)(2,1)S(1)}, bf16[20,64,128]{2,1,0:T(8,128)(2,1)S(1)}, u32[]{:S(2)}, u32[]{:S(2)}) collective-permute-start(bf16[20,64,128]{2,1,0:T(8,128)(2,1)S(1)} %get-tuple-element.89), channel_id=1, source_target_pairs={{0,16},{2,18},{4,20},{6,22},{8,24},{10,26},{12,28},{14,30},{16,0},... | collective-permute-start | bytes 983048 | tf_op jit(solution)/shard_map/cond/branch_1_fun/ppermute | solution.py:34
  114.4 6.1 %collective-permute-start.11 = (bf16[12,64,128]{2,1,0:T(8,128)(2,1)S(1)}, bf16[12,64,128]{2,1,0:T(8,128)(2,1)S(1)}, u32[]{:S(2)}, u32[]{:S(2)}) collective-permute-start(bf16[12,64,128]{2,1,0:T(8,128)(2,1)S(1)} %get-tuple-element.91), channel_id=1, source_target_pairs={{0,8},{2,10},{4,12},{6,14},{8,0},{10,2},{12,4},{14,6},{16,24},{18,... | collective-permute-start | bytes 589832 | tf_op jit(solution)/shard_map/cond/branch_1_fun/ppermute | solution.py:34
  121.8 0.9 copy-start.9

commit v2 on v0

v2 whole, which is shorter than its diff:
```python
import functools

import jax
import jax.numpy as jnp
import numpy as np
from jax import lax
from jax.experimental import pallas as pl
from jax.experimental.pallas import tpu as pltpu
from jax.sharding import PartitionSpec as P

VMEM = pl.BlockSpec(memory_space=pltpu.VMEM)
SMEM = pl.BlockSpec(memory_space=pltpu.SMEM)
BF16 = jnp.bfloat16
F32 = jnp.float32


def call(body, name, outs, in_specs, args, flops=0, scratch=()):
    moved = sum(int(np.prod(o.shape)) * o.dtype.itemsize for o in outs)
    moved += sum(int(np.prod(a.shape)) * a.dtype.itemsize for a in args)
    return pl.pallas_call(
        body,
        name=name,
        out_shape=tuple(outs),
        in_specs=in_specs,
        out_specs=tuple(VMEM for _ in outs),
        scratch_shapes=list(scratch),
        compiler_params=pltpu.CompilerParams(vmem_limit_bytes=40 << 20),
        cost_estimate=pl.CostEstimate(flops=flops, bytes_accessed=moved, transcendentals=0),
    )(*args)


def swap(value, axis, bit):
    size = lax.axis_size(axis)
    return lax.ppermute(value, axis, [(i, i ^ (1 << bit)) for i in range(size)])


def spread(value):
    parts = [value[None]]
    for bit in range(lax.axis_size("tensor").bit_length() - 1):
        whole = parts[0] if len(parts) == 1 else jnp.concatenate(parts, 0)
        parts.append(swap(whole, "tensor", bit))
    return parts


def split_masters(place, masters, kept, sent):
    half = kept.shape[1]
    for block in range(masters.shape[1]):
        turned = masters[0, block].T.astype(BF16)

        @pl.when(place[0] == 0)
        def _():
            kept[block] = turned[:half]
            sent[block] = turned[half:]

        @pl.when(place[0] != 0)
        def _():
            kept[block] = turned[half:]
            sent[block] = turned[:half]


def split_upstream(place, column, grad, kept, sent, blocks, arrived):
    count, half, side = kept.shape[0], kept.shape[1], kept.shape[2]

    def fetch(k):
        start = pl.multiple_of(column[0, k] * side, side)
        return pltpu.make_async_copy(grad.at[:, pl.ds(start, side)], blocks.at[k], arrived.at[k])

    for k in range(count):
        fetch(k).start()
    for k in range(count):
        fetch(k).wait()
        turned = blocks[k].T
        low, high = turned[:half], turned[half:]
        swapped = place[0] != 0
        kept[k] = jnp.where(swapped, high, low)
        sent[k] = jnp.where(swapped, low, high)


def select(place, row, sources, k, side):
    per_shard = sources[0].shape[2] // side
    shard = row[0, k] // per_shard
    start = pl.multiple_of((row[0, k] - shard * per_shard) * side, side)
    offset = shard ^ place[1]
    value, first = None, 0
    for source in sources:
        size = source.shape[0]
        here = source[jnp.clip(offset - first, 0, size - 1), :, pl.ds(start, side)]
        value = here if value is None else jnp.where(offset >= first, here, value)
        first += size
    return value


def select_rows(place, row, *refs):
    sources, chosen = refs[:-1], refs[-1]
    for k in range(chosen.shape[0]):
        chosen[k] = select(place, row, sources, k, chosen.shape[2])


def add_duplicates(first, table, total):
    for k in range(1, total.shape[0]):

        @pl.when(table[first, k] != k)
        def _():
            total[table[first, k]] += total[k]


def slopes(gate, up):
    sigmoid = 0.5 + 0.5 * jnp.tanh(0.5 * gate)
    return sigmoid * up * (1.0 + gate * (1.0 - sigmoid)), sigmoid * gate


def project(weight, source):
    return lax.dot_general(weight, source, (((1,), (1,)), ((), ())), preferred_element_type=F32)


def term(upstream, gate_slope, up_slope, source):
    upstream = upstream.astype(F32)
    both = [(upstream * gate_slope).astype(BF16), (upstream * up_slope).astype(BF16)]
    return jnp.dot(jnp.concatenate(both, axis=0), source, preferred_element_type=F32)


def own_part(rows, table, *refs):
    sources, own_tokens, own_up, weights, grad, total = refs[:4], refs[4], refs[5], refs[6], refs[7], refs[8]
    places, half = own_up.shape[0], own_up.shape[1]
    position = 0
    for source in sources:
        for p in range(source.shape[0]):
            block = table[rows["order"], position + p]
            up = (block >= places).astype(jnp.int32)
            weights[block - up * places, pl.ds(pl.multiple_of(up * half, half), half), :] = source[p]
        position += source.shape[0]
    for k in range(places):
        total[k] = project(weights[k], own_tokens[k])
    add_duplicates(rows["first"], table, total)
    for k in range(places):
        first = table[rows["first"], k]
        grad[k] = term(own_up[k], *slopes(total[first, :half], total[first, half:]), own_tokens[k])


def other_slopes(rows, table, place, row, weights, *refs):
    sources, chosen, slope, total = refs[:-3], refs[-3], refs[-2], refs[-1]
    places, half = weights.shape[0], weights.shape[1] // 2
    for k in range(places):
        value = select(place, row, sources, k, chosen.shape[2])
        chosen[k] = value
        total[k] = project(weights[k], value)
    add_duplicates(rows["first"], table, total)
    for k in range(places):
        first = table[rows["first"], k]
        slope[k, :half], slope[k, half:] = slopes(total[first, :half], total[first, half:])


def other_part(rows, table, slope, other_tokens, other_up, grad, sent_a, kept_a, sent_b, kept_b, total):
    places, half = other_up.shape[0], other_up.shape[1]
    quarter = half // 2
    for k in range(places):
        total[k] = grad[k] + term(other_up[k], slope[k, :half], slope[k, half:], other_tokens[k])
    for block in range(2 * places):
        which, k = divmod(block, places)
        for name, start, sent, kept in (("a", 0, sent_a, kept_a), ("b", quarter, sent_b, kept_b)):
            value = total[k, pl.ds(which * half + start, quarter), :]
            sent[table[rows[name + "_sent"], block]] = value.astype(BF16)
            kept[table[rows[name + "_kept"], block]] = value


def combine(sent_row, kept_row, pieces, table, *refs):
    kept_in, received, sent, kept = refs[:pieces], refs[pieces : 2 * pieces], refs[-2], refs[-1]
    room = sent.shape[0]
    for r in range(kept_in[0].shape[0]):
        value = [kept_in[n][r] + received[n][r].astype(F32) for n in range(pieces)]
        value = value[0] if pieces == 1 else jnp.concatenate(value, 0)
        sent[jnp.minimum(table[sent_row, r], room - 1)] = value.astype(BF16)
        kept[jnp.minimum(table[kept_row, r], room - 1)] = value


def combine_last(sent_row, kept_row, count_row, table, kept_in, received, sent, kept):
    def step(r, _):
        value = kept_in[r] + received[r].astype(F32)
        away = table[sent_row, r]

        @pl.when(away >= 0)
        def _():
            sent[away] = value.astype(BF16)

        @pl.when(away < 0)
        def _():
            kept[table[kept_row, r]] = value

        return 0

    lax.fori_loop(0, table[count_row, 0], step, 0)


def finish(count_row, place, table, kept, received, out):
    count = table[count_row, 0]
    for slot in range(out.shape[1]):

        @pl.when(slot < count)
        def _():
            mine, other = kept[slot], received[slot].astype(F32)
            swapped = place[0] != 0
            low = jnp.where(swapped, other, mine)
            high = jnp.where(swapped, mine, other)
            out[0, slot] = jnp.concatenate([low, high], axis=0).T

        @pl.when(slot >= count)
        def _():
            out[0, slot] = jnp.zeros(out.shape[2:], F32)


def axes_of(owner_count):
    bits = owner_count.bit_length() - 1
    if bits == 4:
        return 0, (1, 2), (3,)
    return bits - 2, (0, bits - 1), tuple(range(1, bits - 2))


def steps_of(bits):
    pair, (bit_a, bit_b), rest = bits
    steps = [("a2", (bit_a,), bit_b), ("b2", (bit_b,), bit_a)]
    done = (bit_a, bit_b)
    for bit in (*rest, pair):
        steps.append((f"s{len(done)}", done, bit))
        done = (*done, bit)
    return steps


def rows_of(bits):
    names = ["order", "first"]
    for name in ["a", "b"] + [name for name, _, _ in steps_of(bits)]:
        names += [name + "_sent", name + "_kept"]
    return {name: n for n, name in enumerate(names + ["last", "end", "fits"])}


def make_plan(bits, usual, own_blocks, place, owners, columns, found, table):
    pair, (bit_a, bit_b), _ = bits
    rows = rows_of(bits)
    count, places = owners.shape[1], columns.shape[1]
    me = place[2]
    across = lax.broadcasted_iota(jnp.int32, (count, count), 1)
    down = lax.broadcasted_iota(jnp.int32, (count, count), 0)
    owner_row, column_row = owners[...], columns[...]

    def as_column(row):
        size = row.shape[1]
        kept = jnp.where((across == down)[:size, :size], row.astype(F32), 0.0)
        return jnp.sum(kept, axis=1, keepdims=True).astype(jnp.int32)

    owner_col, column_col = as_column(owner_row), as_column(column_row)
    before = across < down
    differs_row, differs_col = owner_row ^ me, owner_col ^ me

    def alive(differs, done):
        return (differs & sum(1 << b for b in done)) == 0

    def number(mask):
        return jnp.where(mask, 1.0, 0.0)

    def rank(mask_row):
        return jnp.sum(jnp.where(before, number(mask_row), 0.0), axis=1, keepdims=True)

    def turned(column):
        return jnp.sum(jnp.where(across == down, column, 0.0), axis=0, keepdims=True)

    def write(name, row):
        table[pl.ds(rows[name], 1), :] = row.astype(jnp.int32)

    def going(done, bit):
        live, away = alive(differs_row, done), ((differs_row >> bit) & 1) == 1
        return rank(jnp.logical_and(live, away)), rank(jnp.logical_and(live, jnp.logical_not(away)))

    table[...] = jnp.zeros(table.shape, jnp.int32)
    table[pl.ds(rows["order"], 1), :] = (found[0:1, :] ^ me) * own_blocks + found[1:2, :]
    same = column_row == column_col
    place_at = lax.broadcasted_iota(jnp.int32, (places, places), 0).astype(F32)
    first = jnp.min(jnp.where(same, place_at, float(places)), axis=0, keepdims=True)
    table[pl.ds(rows["first"], 1), :places] = first.astype(jnp.int32)
    for name, bit in (("a", bit_a), ("b", bit_b)):
        sent, kept = going((), bit)
        write(name + "_sent", turned(sent))
        write(name + "_kept", turned(kept))
    full, at_most = float(count), None
    for name, done, bit in steps_of(bits):
        sent, kept = going(done, bit)
        live = rank(alive(differs_row, done))
        hit = jnp.logical_and(alive(differs_col, done), live == across.astype(F32))
        if bit == pair:
            sent = jnp.where(((differs_col >> bit) & 1) == 1, sent, -1.0)
        for kind, values in (("_sent", sent), ("_kept", kept)):
            write(name + kind, full + jnp.sum(jnp.where(hit, values - full, 0.0), axis=0, keepdims=True))
        if name in usual:
            mask = sum(1 << b for b in done)
            group = (owner_row & mask) == (owner_col & mask)
            over = jnp.max(jnp.sum(number(group), axis=1, keepdims=True), axis=0, keepdims=True) - usual[name]
            at_most = over if at_most is None else jnp.maximum(at_most, over)
    for name, done in (("last", done), ("end", (*done, pair))):
        total = jnp.sum(number(alive(differs_row, done)), axis=1, keepdims=True)
        write(name, jnp.broadcast_to(total, (1, count)))
    fits = jnp.zeros((1, 1), F32) if at_most is None else at_most
    write("fits", jnp.broadcast_to(number(fits <= 0.0), (1, count)))


def local(tokens, hidden_grad, masters, block_row, block_col, owners):
    owner_count = lax.axis_size("dp")
    me = lax.axis_index("dp")
    bits = axes_of(owner_count)
    pair, (bit_a, bit_b), rest = bits
    own_blocks, side = masters.shape[1], masters.shape[2]
    places, half, quarter = block_row.shape[1], side // 2, side // 4
    block_count = owners.shape[1]
    token_count = tokens.shape[0]
    capacity = 3 * block_count // owner_count
    place = jnp.stack([(me >> pair) & 1, lax.axis_index("tensor"), me]).astype(jnp.int32)

    def struct(shape, dtype):
        return jax.ShapeDtypeStruct(shape, dtype)

    with jax.named_scope("weights"):
        kept, sent = call(
            split_masters, "split_masters", [struct((own_blocks, half, side), BF16)] * 2, [SMEM, VMEM], [place, masters]
        )
        entries = [(0, b) for b in range(own_blocks)]

        def moved(found, bit):
            return [(delta ^ (1 << bit), b) for delta, b in found]

        got = swap(sent, "dp", pair)
        entries = entries + moved(entries, pair)
        tokens, hidden_grad, owners, got = lax.optimization_barrier((tokens, hidden_grad, owners, got))
        current = jnp.concatenate([kept, got], 0)
        for bit in rest[:0:-1]:
            current = jnp.concatenate([current, swap(current, "dp", bit)], 0)
            entries = entries + moved(entries, bit)
        far = swap(current, "dp", rest[0])
        own_up, sent_up = call(
            split_upstream, "split_upstream", [struct((places, half, token_count), BF16)] * 2,
            [SMEM, SMEM, pl.BlockSpec(memory_space=pl.ANY)], [place, block_col, hidden_grad], 0,
            [pltpu.VMEM((places, token_count, side), BF16), pltpu.SemaphoreType.DMA((places,))],
        )
        current, far, sent_up = lax.optimization_barrier((current, far, sent_up))
        a0 = jnp.concatenate([current, swap(current, "dp", bit_a)], 0)
        b0 = jnp.concatenate([far, swap(far, "dp", bit_b)], 0)
        entries_a, entries_b = entries + moved(entries, bit_a), moved(entries, rest[0])
        entries_b = entries_b + moved(entries_b, bit_b)
        a1, b1 = swap(a0, "dp", bit_b), swap(b0, "dp", bit_a)
        found = entries_a + moved(entries_a, bit_b) + entries_b + moved(entries_b, bit_a)
        found = np.array(found, np.int32).T

    with jax.named_scope("plan"):

        def most_of(done):
            return min(block_count, (owner_count >> len(done)) * capacity)

        def load_of(done):
            return min(most_of(done), (block_count >> len(done)) + capacity)

        rows, steps = rows_of(bits), steps_of(bits)
        usual = {name: load_of(done) for name, done, _ in steps if load_of(done) < most_of(done)}
        table = call(
            functools.partial(make_plan, bits, usual, own_blocks), "make_plan",
            [struct((-(-len(rows) // 8) * 8, block_count), jnp.int32)], [SMEM] + [VMEM] * 3,
            [place, owners, block_col, jnp.asarray(found)],
        )[0]
        fits = table[rows["fits"], :1]
        for bit in range(lax.axis_size("tensor").bit_length() - 1):
            fits = jnp.minimum(fits, swap(fits, "tensor", bit))

    with jax.named_scope("tokens"):
        other = swap(tokens, "dp", pair)
        parts = spread(tokens)
        own_chosen = call(
            select_rows, "select_rows", [struct((places, token_count, side), BF16)],
            [SMEM, SMEM] + [VMEM] * len(parts), [place, block_row, *parts],
        )[0]
        other, _ = lax.optimization_barrier((other, (a1, b1)))
        other_parts = spread(other)

    with jax.named_scope("upstream"):
        other_up = swap(sent_up, "dp", pair)

    work = 2 * 2 * places * side * side * token_count
    with jax.named_scope("own_tokens"):
        weights, grad = call(
            functools.partial(own_part, rows), "own_part",
            [struct((places, side, side), BF16), struct((places, side, side), F32)], [SMEM] + [VMEM] * 6,
            [table, a0, a1, b0, b1, own_chosen, own_up], work, [pltpu.VMEM((places, side, token_count), F32)],
        )
    with jax.named_scope("other_tokens"):
        other_chosen, slope = call(
            functools.partial(other_slopes, rows), "other_slopes",
            [struct((places, token_count, side), BF16), struct((places, side, token_count), F32)],
            [SMEM] * 3 + [VMEM] * (1 + len(other_parts)), [table, place, block_row, weights, *other_parts], work // 2,
            [pltpu.VMEM((places, side, token_count), F32)],
        )

    def reduce(load, table, slope, other_chosen, other_up, grad):
        outs = []
        for bit in (bit_a, bit_b):
            room = load((bit,)) + 1
            outs += [struct((room, quarter, side), BF16), struct((room, quarter, side), F32)]
        sent_a, kept_a, sent_b, kept_b = call(
            functools.partial(other_part, rows), "other_part", outs, [SMEM] + [VMEM] * 4,
            [table, slope, other_chosen, other_up, grad], work // 2, [pltpu.VMEM((places, side, side), F32)],
        )

        def join(name, done, kept_in, received):
            pieces = len(kept_in)
            at = rows[name + "_sent"], rows[name + "_kept"]
            if done[-1] == pair:
                body, room = functools.partial(combine_last, *at, rows["last"]), capacity
            else:
                body, room = functools.partial(combine, *at, pieces), load(done) + 1
            height = sum(k.shape[1] for k in kept_in)
            return call(
                body, "combine", [struct((room, height, side), BF16), struct((room, height, side), F32)],
                [SMEM] + [VMEM] * (2 * pieces), [table, *kept_in, *received],
            )

        got_a, got_b = swap(sent_a, "dp", bit_a), swap(sent_b, "dp", bit_b)
        both = (bit_a, bit_b)
        sent_a, kept_a = join("a2", both, [kept_a], [got_a])
        got_a = swap(sent_a, "dp", bit_b)
        sent_b, kept_b = join("b2", both, [kept_b], [got_b])
        got_b = swap(sent_b, "dp", bit_a)
        kept, got, done = [kept_a, kept_b], [got_a, got_b], both
        for name, _, bit in steps[2:]:
            done = (*done, bit)
            sent, held = join(name, done, kept, got)
            kept, got = [held], [swap(sent, "dp", bit)]
        return kept[0], got[0]

    operands = (table, slope, other_chosen, other_up, grad)
    kept, got = lax.cond(
        fits[0] == 1, functools.partial(reduce, load_of), functools.partial(reduce, most_of), *operands
    )
    return call(
        functools.partial(finish, rows["end"]), "finish", [struct((1, capacity, side, side), F32)],
        [SMEM, SMEM, VMEM, VMEM], [place, table, kept, got],
    )[0]


def solution(mesh):
    return jax.shard_map(
        local,
        mesh=mesh,
        in_specs=(
            P("dp", "tensor"),
            P("dp", "tensor"),
            P("tensor", "dp", None, None),
            P("tensor", None),
            P("tensor", None),
            P("tensor", None),
        ),
        out_specs=P("tensor", "dp", None, None),
        check_vma=False,
    )
```

time: 283 us -> 94.7 us (0.33)
  waiting for transfers between devices: 222 us -> 45.3 us
  starting transfers between devices: 0.09 us -> 24.9 us
  local copies, waits for them, and re-layouts: 25.8 us -> 4.25 us
  Pallas kernels: 0 us -> 18.6 us
  matrix products: 17.1 us -> 0 us
  between operations: 13.2 us -> 1.33 us
  other arithmetic: 4.02 us -> 0.08 us
    psum x1 -> x0, waiting for transfers between devices: 166 us -> none  [local(): summed = lax.psum(block_grads, 'dp')]
    all_gather x2 -> x0, waiting for transfers between devices: 55.5 us -> none  [the longest x1 55.5 us: local(): lax.all_gather(masters.astype(jnp.bfloat16), 'dp', axis=1, tiled=True)[0]]
    ppermute x0 -> x17, waiting for transfers between devices: none -> 45.3 us  [swap(): return lax.ppermute(value, axis, [(i, i ^ 1 << bit) for i in range(size)])]
    ppermute x0 -> x17, starting transfers between devices: none -> 24.9 us  [swap(): return lax.ppermute(value, axis, [(i, i ^ 1 << bit) for i in range(size)])]
    pallas_call x0 -> x12, Pallas kernels: none -> 18.6 us  [call(): pl.pallas_call(body, name=name, out_shape=tuple(outs), in_specs=in_specs,...]
    dot_general x7 -> x0, matrix products: 17.1 us -> none  [the longest x2 7.25 us: column_total(): jnp.einsum('tjc,kj->tkc', part, same_column, precision=lax.Precision.HIGH...]
    reshape x2 -> x0, local copies, waits for them, and re-layouts: 9.36 us -> none  [the longest x1 6.14 us: local(): hidden_grad.reshape(token_count, hidden_grad.shape[1] // block_side, bloc...]
    unnamed x14 -> x19, local copies, waits for them, and re-layouts: 9.69 us -> 3.69 us
  transfers between devices with their start and end apart: 3 -> 17, of which waited for: 2 -> 11; matrix products, arithmetic and copies ran while one was open for 8% -> 1% of each run, Pallas kernels for 0% -> 13%
where the time goes in v2:
time: 94.7 us; the launch traced here: 94.5 us
  waiting for transfers between devices  45.3 us (48%)
  starting transfers between devices  24.9 us (26%)
  Pallas kernels  18.6 us (20%)
  local copies, waits for them, and re-layouts  4.25 us (4%)
  between operations  1.33 us (1%)
    ppermute x17, waiting for transfers between devices, swap(): return lax.ppermute(value, axis, [(i, i ^ 1 << bit) for i in range(size)])  45.3 us
    ppermute x17, starting transfers between devices, swap(): return lax.ppermute(value, axis, [(i, i ^ 1 << bit) for i in range(size)])  24.9 us
    pallas_call x12, Pallas kernels, call(): pl.pallas_call(body, name=name, out_shape=tuple(outs), in_specs=in_specs,...  18.6 us
    unnamed x19, local copies, waits for them, and re-layouts  3.69 us
  transfers between devices with their start and end apart: 17, of which 11 were waited for; matrix products, arithmetic and copies ran while one was open for 1% of the time, Pallas kernels for 13%

profile of v2, /device:TPU:0, one launch (start us, length us, event | category | flops | bytes accessed | tf_op | source)
XLA Modules:
  0.0 94.5 jit_solution(7163241408189905233)
XLA Ops:
  0.0 0.1 pad_add_fusion.place
  0.1 0.0 copy-start.2
  0.1 0.9 %copy-done.2 = f32[1,4,128,128]{3,2,1,0:T(8,128)S(1)} copy-done((f32[1,4,128,128]{3,2,1,0:T(8,128)S(1)}, f32[1,4,128,128]{3,2,1,0:T(8,128)}, u32[]{:S(2)}) %copy-start.2) | copy-done | bytes 262168
  1.0 0.9 split_masters.1
  2.0 3.0 %collective-permute-start.12 = (bf16[4,64,128]{2,1,0:T(8,128)(2,1)S(1)}, bf16[4,64,128]{2,1,0:T(8,128)(2,1)S(1)}, u32[]{:S(2)}, u32[]{:S(2)}) collective-permute-start(bf16[4,64,128]{2,1,0:T(8,128)(2,1)S(1)} %get-tuple-element.77), channel_id=1, source_target_pairs={{0,2},{2,0},{4,6},{6,4},{8,10},{10,8},{12,14},{14,12},{16,18},{18,... | collective-permute-start | bytes 196616 | tf_op jit(solution)/shard_map/weights/ppermute | solution.py:34
  5.0 2.2 %collective-permute-done.12 = bf16[4,64,128]{2,1,0:T(8,128)(2,1)S(1)} collective-permute-done((bf16[4,64,128]{2,1,0:T(8,128)(2,1)S(1)}, bf16[4,64,128]{2,1,0:T(8,128)(2,1)S(1)}, u32[]{:S(2)}, u32[]{:S(2)}) %collective-permute-start.12) | collective-permute-done | bytes 65568 | tf_op jit(solution)/shard_map/weights/ppermute | solution.py:34
  7.2 2.0 %collective-permute-start.20 = (bf16[128,4096]{1,0:T(8,128)(2,1)}, bf16[128,4096]{1,0:T(8,128)(2,1)S(1)}, u32[]{:S(2)}, u32[]{:S(2)}) collective-permute-start(bf16[128,4096]{1,0:T(8,128)(2,1)} %param.9), channel_id=1, source_target_pairs={{0,2},{2,0},{4,6},{6,4},{8,10},{10,8},{12,14},{14,12},{16,18},{18,... | collective-permute-start | bytes 3145736 | tf_op jit(solution)/shard_map/tokens/ppermute | solution.py:34
  9.3 2.7 %collective-permute-start.14 = (bf16[8,64,128]{2,1,0:T(8,128)(2,1)S(1)}, bf16[8,64,128]{2,1,0:T(8,128)(2,1)S(1)}, u32[]{:S(2)}, u32[]{:S(2)}) collective-permute-start(bf16[8,64,128]{2,1,0:T(8,128)(2,1)S(1)} %constant_dynamic-update-slice_fusion), channel_id=1, source_target_pairs={{0,16},{2,18},{4,20},{6,22},{8,24},{10,26},{12,28},{14,30},{16,0},... | collective-permute-start | bytes 393224 | tf_op jit(solution)/shard_map/weights/ppermute | solution.py:34
  11.9 0.0 copy-start
  11.9 2.0 %copy-done = bf16[128,14336]{1,0:T(8,128)(2,1)S(1)} copy-done((bf16[128,14336]{1,0:T(8,128)(2,1)S(1)}, bf16[128,14336]{1,0:T(8,128)(2,1)}, u32[]{:S(2)}) %copy-start) | copy-done | bytes 3670040
  13.9 0.0 copy-start.4
  14.0 0.7 copy-done.4
  14.6 0.0 copy-start.1
  14.6 0.0 copy-start.5
  14.6 0.0 copy-start.7
  14.6 0.0 copy-start.3
  14.6 3.6 %split_upstream.1 = (bf16[32,64,128]{2,1,0:T(8,128)(2,1)S(1)}, bf16[32,64,128]{2,1,0:T(8,128)(2,1)S(1)}) custom-call(s32[3]{0:T(128)S(1)} %pad_add_fusion.place, s32[1,32]{1,0:T(1,128)S(1)} %copy-done.4, bf16[128,14336]{1,0:T(8,128)(2,1)S(1)} %copy-done), custom_call_target="tpu_custom_call" | custom-call | bytes 4718732 | tf_op jit(solution)/shard_map/weights/split_upstream/pallas_call | solution.py:20
  18.2 0.0 collective-permute-done.14
  18.3 1.6 %collective-permute-start.15 = (bf16[8,64,128]{2,1,0:T(8,128)(2,1)S(1)}, bf16[8,64,128]{2,1,0:T(8,128)(2,1)S(1)}, u32[]{:S(2)}, u32[]{:S(2)}) collective-permute-start(bf16[8,64,128]{2,1,0:T(8,128)(2,1)S(1)} %constant_dynamic-update-slice_fusion), channel_id=1, source_target_pairs={{0,4},{2,6},{4,0},{6,2},{8,12},{10,14},{12,8},{14,10},{16,20},{18,... | collective-permute-start | bytes 393224 | tf_op jit(solution)/shard_map/weights/ppermute | solution.py:34
  19.8 1.6 %collective-permute-start.17 = (bf16[8,64,128]{2,1,0:T(8,128)(2,1)S(1)}, bf16[8,64,128]{2,1,0:T(8,128)(2,1)S(1)}, u32[]{:S(2)}, u32[]{:S(2)}) collective-permute-start(bf16[8,64,128]{2,1,0:T(8,128)(2,1)S(1)} %collective-permute-done.14), channel_id=1, source_target_pairs={{0,8},{2,10},{4,12},{6,14},{8,0},{10,2},{12,4},{14,6},{16,24},{18,... | collective-permute-start | bytes 393224 | tf_op jit(solution)/shard_map/weights/ppermute | solution.py:34
  21.4 3.4 %collective-permute-done.17 = bf16[8,64,128]{2,1,0:T(8,128)(2,1)S(1)} collective-permute-done((bf16[8,64,128]{2,1,0:T(8,128)(2,1)S(1)}, bf16[8,64,128]{2,1,0:T(8,128)(2,1)S(1)}, u32[]{:S(2)}, u32[]{:S(2)}) %collective-permute-start.17) | collective-permute-done | bytes 131104 | tf_op jit(solution)/shard_map/weights/ppermute | solution.py:34
  24.8 0.6 collective-permute-start.18
  25.4 0.0 collective-permute-done.15
  25.4 1.6 %collective-permute-start.16 = (bf16[16,64,128]{2,1,0:T(8,128)(2,1)S(1)}, bf16[16,64,128]{2,1,0:T(8,128)(2,1)S(1)}, u32[]{:S(2)}, u32[]{:S(2)}) collective-permute-start(bf16[16,64,128]{2,1,0:T(8,128)(2,1)S(1)} %constant_dynamic-update-slice_fusion.2.refs_0_), channel_id=1, source_target_pairs={{0,8},{2,10},{4,12},{6,14},{8,0},{10,2},{12,4},{14,6},{16,24},{18,... | collective-permute-start | bytes 786440 | tf_op jit(solution)/shard_map/weights/ppermute | solution.py:34
  27.1 0.0 copy-done.1
  27.1 0.0 collective-permute-start.19
  27.1 4.2 %collective-permute-done.18.refs_3_ = bf16[16,64,128]{2,1,0:T(8,128)(2,1)S(1)} collective-permute-done((bf16[16,64,128]{2,1,0:T(8,128)(2,1)S(1)}, bf16[16,64,128]{2,1,0:T(8,128)(2,1)S(1)}, u32[]{:S(2)}, u32[]{:S(2)}) %collective-permute-start.18) | collective-permute-done | bytes 262176 | tf_op jit(solution)/shard_map/weights/ppermute | solution.py:34
  31.3 0.6 collective-permute-done.16.refs_1_
  31.9 0.0 collective-permute-done.20
  31.9 0.0 collective-permute-start.21
  31.9 1.3 %collective-permute-start.22 = (bf16[32,64,128]{2,1,0:T(8,128)(2,1)S(1)}, bf16[32,64,128]{2,1,0:T(8,128)(2,1)S(1)}, u32[]{:S(2)}, u32[]{:S(2)}) collective-permute-start(bf16[32,64,128]{2,1,0:T(8,128)(2,1)S(1)} %get-tuple-element.91), channel_id=1, source_target_pairs={{0,2},{2,0},{4,6},{6,4},{8,10},{10,8},{12,14},{14,12},{16,18},{18,... | collective-permute-start | bytes 1572872 | tf_op jit(solution)/shard_map/upstream/ppermute | solution.py:34
  33.2 0.0 copy-done.5
  33.2 0.0 copy-done.6
  33.2 0.0 copy-done.7
  33.2 0.8 make_plan.1.table
  34.0 0.5 slice.4
  34.5 0.2 collective-permute-start.13
  34.8 1.2 %collective-permute-done.13 = s32[1]{0:T(128)} collective-permute-done((s32[1]{0:T(128)}, s32[1]{0:T(128)}, u32[]{:S(2)}, u32[]{:S(2)}) %collective-permute-start.13) | collective-permute-done | bytes 36 | tf_op jit(solution)/shard_map/plan/ppermute | solution.py:34
  37.1 0.0 collective-permute-done.19.refs_1_
  37.1 0.0 copy-done.3
  37.2 1.2 %select_rows.1.refs_4_ = bf16[32,128,128]{2,1,0:T(8,128)(2,1)S(1)} custom-call(s32[3]{0:T(128)S(1)} %pad_add_fusion.place, s32[1,32]{1,0:T(1,128)S(1)} %copy-done.3, bf16[1,128,4096]{2,1,0:T(8,128)(2,1)S(1)} %bitcast.10, bf16[1,128,4096]{2,1,0:T(8,128)(2,1)S(1)} %collective-permute-done.19.refs_1_), custom_call_target="tpu_custom_call" | custom-call | bytes 3145868 | tf_op jit(solution)/shard_map/tokens/select_rows/pallas_call | solution.py:20
  38.4 2.7 %own_part.1 = (bf16[32,128,128]{2,1,0:T(8,128)(2,1)S(1)}, f32[32,128,128]{2,1,0:T(8,128)S(1)}) custom-call(s32[24,64]{1,0:T(8,128)S(1)} %make_plan.1.table, bf16[16,64,128]{2,1,0:T(8,128)(2,1)S(1)} %constant_dynamic-update-slice_fusion.2.refs_0_, bf16[16,64,128]{2,1,0:T(8,128)(2,1)S(1)} %collective-permute-done.16.refs_1_, ...), custom_call_target="tpu_custom_call" | custom-call | flops 268435456 | bytes 5773312 | tf_op jit(solution)/shard_map/own_tokens/own_part/pallas_call | solution.py:20
  41.1 0.0 collective-permute-done.21.refs_1_
  41.1 2.2 %other_slopes.1 = (bf16[32,128,128]{2,1,0:T(8,128)(2,1)S(1)}, f32[32,128,128]{2,1,0:T(8,128)S(1)}) custom-call(s32[24,64]{1,0:T(8,128)S(1)} %make_plan.1.table, s32[3]{0:T(128)S(1)} %pad_add_fusion.place, s32[1,32]{1,0:T(1,128)S(1)} %copy-done.3, bf16[32,128,128]{2,1,0:T(8,128)(2,1)S(1)} %get-tuple-element.87.weights, bf16[1,128,4096]{2,1,0:T(8,128)(2,1)S(1)} %bitcast.8, ...), custom_call_target="tpu_custom_call" | custom-call | flops 134217728 | bytes 6297740 | tf_op jit(solution)/shard_map/other_tokens/other_slopes/pallas_call | solution.py:20
  43.3 2.9 %collective-permute-done.22 = bf16[32,64,128]{2,1,0:T(8,128)(2,1)S(1)} collective-permute-done((bf16[32,64,128]{2,1,0:T(8,128)(2,1)S(1)}, bf16[32,64,128]{2,1,0:T(8,128)(2,1)S(1)}, u32[]{:S(2)}, u32[]{:S(2)}) %collective-permute-start.22) | collective-permute-done | bytes 524320 | tf_op jit(solution)/shard_map/upstream/ppermute | solution.py:34
  46.2 46.0 %conditional.1 = (f32[12,64,128]{2,1,0:T(8,128)S(1)}, bf16[12,64,128]{2,1,0:T(8,128)(2,1)}) conditional(s32[]{:T(128)} %bitcast.4, (s32[24,64]{1,0:T(8,128)S(1)}, f32[32,128,128]{2,1,0:T(8,128)S(1)}, bf16[32,128,128]{2,1,0:T(8,128)(2,1)S(1)}, bf16[32,64,128]{2,1,0:T(8,128)(2,1)S(1)}, f32[32,128,128]{2,1,0:T(8,128)S(1)}) %tuple.19, ...), branch_computations={%region_0.0_spmd, %region_1.0_spmd} | conditional | flops 134217728 | bytes 29948160 | solution.py:433
  46.2 1.4 %other_part.3 = (bf16[45,32,128]{2,1,0:T(8,128)(2,1)S(1)}, f32[45,32,128]{2,1,0:T(8,128)S(1)}, bf16[45,32,128]{2,1,0:T(8,128)(2,1)S(1)}, f32[45,32,128]{2,1,0:T(8,128)S(1)}) custom-call(s32[24,64]{1,0:T(8,128)S(1)} %get-tuple-element.42.table, f32[32,128,128]{2,1,0:T(8,128)S(1)} %get-tuple-element.43.slope, ...), custom_call_target="tpu_custom_call" | custom-call | flops 134217728 | bytes 7985152 | tf_op jit(solution)/shard_map/cond/branch_1_fun/other_part/pallas_call | solution.py:20
  47.6 1.6 %collective-permute-start.6 = (bf16[45,32,128]{2,1,0:T(8,128)(2,1)S(1)}, bf16[45,32,128]{2,1,0:T(8,128)(2,1)S(1)}, u32[]{:S(2)}, u32[]{:S(2)}) collective-permute-start(bf16[45,32,128]{2,1,0:T(8,128)(2,1)S(1)} %get-tuple-element.48), channel_id=1, source_target_pairs={{0,4},{2,6},{4,0},{6,2},{8,12},{10,14},{12,8},{14,10},{16,20},{18,... | collective-permute-start | bytes 1105928 | tf_op jit(solution)/shard_map/cond/branch_1_fun/ppermute | solution.py:34
  49.2 1.6 %collective-permute-start.7 = (bf16[45,32,128]{2,1,0:T(8,128)(2,1)S(1)}, bf16[45,32,128]{2,1,0:T(8,128)(2,1)S(1)}, u32[]{:S(2)}, u32[]{:S(2)}) collective-permute-start(bf16[45,32,128]{2,1,0:T(8,128)(2,1)S(1)} %get-tuple-element.51), channel_id=1, source_target_pairs={{0,8},{2,10},{4,12},{6,14},{8,0},{10,2},{12,4},{14,6},{16,24},{18,... | collective-permute-start | bytes 1105928 | tf_op jit(solution)/shard_map/cond/branch_1_fun/ppermute | solution.py:34
  50.8 7.1 %collective-permute-done.6.refs_1_ = bf16[45,32,128]{2,1,0:T(8,128)(2,1)S(1)} collective-permute-done((bf16[45,32,128]{2,1,0:T(8,128)(2,1)S(1)}, bf16[45,32,128]{2,1,0:T(8,128)(2,1)S(1)}, u32[]{:S(2)}, u32[]{:S(2)}) %collective-permute-start.6) | collective-permute-done | bytes 368672 | tf_op jit(solution)/shard_map/cond/branch_1_fun/ppermute | solution.py:34
  57.9 0.9 combine.12
  58.7 1.6 %collective-permute-start.8 = (bf16[29,32,128]{2,1,0:T(8,128)(2,1)S(1)}, bf16[29,32,128]{2,1,0:T(8,128)(2,1)S(1)}, u32[]{:S(2)}, u32[]{:S(2)}) collective-permute-start(bf16[29,32,128]{2,1,0:T(8,128)(2,1)S(1)} %get-tuple-element.53), channel_id=1, source_target_pairs={{0,8},{2,10},{4,12},{6,14},{8,0},{10,2},{12,4},{14,6},{16,24},{18,... | collective-permute-start | bytes 712712 | tf_op jit(solution)/shard_map/cond/branch_1_fun/ppermute | solution.py:34
  60.4 0.0 collective-permute-done.7.refs_1_
  60.4 0.9 combine.13
  61.2 1.6 %collective-permute-start.9 = (bf16[29,32,128]{2,1,0:T(8,128)(2,1)S(1)}, bf16[29,32,128]{2,1,0:T(8,128)(2,1)S(1)}, u32[]{:S(2)}, u32[]{:S(2)}) collective-permute-start(bf16[29,32,128]{2,1,0:T(8,128)(2,1)S(1)} %get-tuple-element.54), channel_id=1, source_target_pairs={{0,4},{2,6},{4,0},{6,2},{8,12},{10,14},{12,8},{14,10},{16,20},{18,... | collective-permute-start | bytes 712712 | tf_op jit(solution)/shard_map/cond/branch_1_fun/ppermute | solution.py:34
  62.8 2.5 %collective-permute-done.8.refs_2_ = bf16[29,32,128]{2,1,0:T(8,128)(2,1)S(1)} collective-permute-done((bf16[29,32,128]{2,1,0:T(8,128)(2,1)S(1)}, bf16[29,32,128]{2,1,0:T(8,128)(2,1)S(1)}, u32[]{:S(2)}, u32[]{:S(2)}) %collective-permute-start.8) | collective-permute-done | bytes 237600 | tf_op jit(solution)/shard_map/cond/branch_1_fun/ppermute | solution.py:34
  65.3 2.2 %collective-permute-done.9.refs_3_ = bf16[29,32,128]{2,1,0:T(8,128)(2,1)S(1)} collective-permute-done((bf16[29,32,128]{2,1,0:T(8,128)(2,1)S(1)}, bf16[29,32,128]{2,1,0:T(8,128)(2,1)S(1)}, u32[]{:S(2)}, u32[]{:S(2)}) %collective-permute-start.9) | collective-permute-done | bytes 237600 | tf_op jit(solution)/shard_map/cond/branch_1_fun/ppermute | solution.py:34
  67.6 0.8 combine.14
  68.4 2.5 %collective-permute-start.10 = (bf16[21,64,128]{2,1,0:T(8,128)(2,1)S(1)}, bf16[21,64,128]{2,1,0:T(8,128)(2,1)S(1)}, u32[]{:S(2)}, u32[]{:S(2)}) collective-permute-start(bf16[21,64,128]{2,1,0:T(8,128)(2,1)S(1)} %get-tuple-element.56), channel_id=1, source_target_pairs={{0,16},{2,18},{4,20},{6,22},{8,24},{10,26},{12,28},{14,30},{16,0},... | collective-permute-start | bytes 1032200 | tf_op jit(solution)/shard_map/cond/branch_1_fun/ppermute | solution.py:34
  70.9 13.3 %collective-permute-done.10.received = bf16[21,64,128]{2,1,0:T(8,128)(2,1)S(1)} collective-permute-done((bf16[21,64,128]{2,1,0:T(8,128)(2,1)S(1)}, bf16[21,64,128]{2,1,0:T(8,128)(2,1)S(1)}, u32[]{:S(2)}, u32[]{:S(2)}) %collective-permute-start.10) | collective-permute-done | bytes 344096 | tf_op jit(solution)/shard_map/cond/branch_1_fun/ppermute | solution.py:34
  84.2 0.9 combine.15
  85.1 1.4 %collective-permute-start.11 = (bf16[12,64,128]{2,1,0:T(8,128)(2,1)S(1)}, bf16[12,64,128]{2,1,0:T(8,128)(2,1)}, u32[]{:S(2)}, u32[]{:S(2)}) collective-permute-start(bf16[12,64,128]{2,1,0:T(8,128)(2,1)S(1)} %get-tuple-element.58), channel_id=1, source_target_pairs={{0,2},{2,0},{4,6},{6,4},{8,10},{10,8},{12,14},{14,12},{16,18},{18,... | collective-permute-start | bytes 589832 | tf_op jit(solution)/shard_map/cond/branch_1_fun/ppermute | solution.py:34
  86.5 5.7 %collective-permute-done.11 = bf16[12,64,128]{2,1,0:T(8,128)(2,1)} collective-permute-done((bf16[12,64,128]{2,1,0:T(8,128)(2,1)S(1)}, bf16[12,64,128]{2,1,0:T(8,128)(2,1)}, u32[]{:S(2)}, u32[]{:S(2)}) %collective-permute-start.11) | collective-permute-done | bytes 196640 | tf_op jit(solution)/shard_map/cond/branch_1_fun/ppermute | solution.py:34
  92.2 2.3 %finish.1 = f32[1,12,128,128]{3,2,1,0:T(8,128)} custom-call(s32[3]{0:T(128)S(1)} %pad_add_fusion.place, s32[24,64]{1,0:T(8,128)S(1)} %make_plan.1.table, f32[12,64,128]{2,1,0:T(8,128)S(1)} %get-tuple-element.93.kept, bf16[12,64,128]{2,1,0:T(8,128)(2,1)} %get-tuple-element.94.received), custom_call_target="tpu_custom_call" | custom-call | bytes 1382412 | tf_op jit(solution)/shard_map/finish/pallas_call | solution.py:20
  (7 shorter events, 0.1 us)
Async XLA Ops:
  0.1 1.0 %copy-start.2 = (f32[1,4,128,128]{3,2,1,0:T(8,128)S(1)}, f32[1,4,128,128]{3,2,1,0:T(8,128)}, u32[]{:S(2)}) copy-start(f32[1,4,128,128]{3,2,1,0:T(8,128)} %masters.1) | copy-start | bytes 786436
  2.0 5.2 %collective-permute-start.12 = (bf16[4,64,128]{2,1,0:T(8,128)(2,1)S(1)}, bf16[4,64,128]{2,1,0:T(8,128)(2,1)S(1)}, u32[]{:S(2)}, u32[]{:S(2)}) collective-permute-start(bf16[4,64,128]{2,1,0:T(8,128)(2,1)S(1)} %get-tuple-element.77), channel_id=1, source_target_pairs={{0,2},{2,0},{4,6},{6,4},{8,10},{10,8},{12,14},{14,12},{16,18},{18,... | collective-permute-start | bytes 196616 | tf_op jit(solution)/shard_map/weights/ppermute | solution.py:34
  7.2 24.7 %collective-permute-start.20 = (bf16[128,4096]{1,0:T(8,128)(2,1)}, bf16[128,4096]{1,0:T(8,128)(2,1)S(1)}, u32[]{:S(2)}, u32[]{:S(2)}) collective-permute-start(bf16[128,4096]{1,0:T(8,128)(2,1)} %param.9), channel_id=1, source_target_pairs={{0,2},{2,0},{4,6},{6,4},{8,10},{10,8},{12,14},{14,12},{16,18},{18,... | collective-permute-start | bytes 3145736 | tf_op jit(solution)/shard_map/tokens/ppermute | solution.py:34
  9.3 9.0 %collective-permute-start.14 = (bf16[8,64,128]{2,1,0:T(8,128)(2,1)S(1)}, bf16[8,64,128]{2,1,0:T(8,128)(2,1)S(1)}, u32[]{:S(2)}, u32[]{:S(2)}) collective-permute-start(bf16[8,64,128]{2,1,0:T(8,128)(2,1)S(1)} %constant_dynamic-update-slice_fusion), channel_id=1, source_target_pairs={{0,16},{2,18},{4,20},{6,22},{8,24},{10,26},{12,28},{14,30},{16,0},... | collective-permute-start | bytes 393224 | tf_op jit(solution)/shard_map/weights/ppermute | solution.py:34
  11.9 2.0 %copy-start = (bf16[128,14336]{1,0:T(8,128)(2,1)S(1)}, bf16[128,14336]{1,0:T(8,128)(2,1)}, u32[]{:S(2)}) copy-start(bf16[128,14336]{1,0:T(8,128)(2,1)} %grad) | copy-start | bytes 11010052
  13.9 0.7 copy-start.4
  14.6 12.5 %copy-start.1 = (bf16[128,4096]{1,0:T(8,128)(2,1)S(1)}, bf16[128,4096]{1,0:T(8,128)(2,1)}, u32[]{:S(2)}) copy-start(bf16[128,4096]{1,0:T(8,128)(2,1)} %param.9) | copy-start | bytes 3145732
  14.6 18.6 %copy-start.5 = (s32[1,32]{1,0:T(1,128)S(1)}, s32[1,32]{1,0:T(1,128)}, u32[]{:S(2)}) copy-start(s32[1,32]{1,0:T(1,128)} %column.1) | copy-start | bytes 388
  14.6 18.6 %copy-start.6 = (s32[2,64]{1,0:T(2,128)S(1)}, s32[2,64]{1,0:T(2,128)}, u32[]{:S(2)}) copy-start(s32[2,64]{1,0:T(2,128)} %constant.16.clone.found) | copy-start | bytes 1540
  14.6 18.6 %copy-start.7 = (s32[1,64]{1,0:T(1,128)S(1)}, s32[1,64]{1,0:T(1,128)}, u32[]{:S(2)}) copy-start(s32[1,64]{1,0:T(1,128)} %owners) | copy-start | bytes 772
  14.6 22.5 %copy-start.3 = (s32[1,32]{1,0:T(1,128)S(1)}, s32[1,32]{1,0:T(1,128)}, u32[]{:S(2)}) copy-start(s32[1,32]{1,0:T(1,128)} %row.3) | copy-start | bytes 388
  18.3 7.2 %collective-permute-start.15 = (bf16[8,64,128]{2,1,0:T(8,128)(2,1)S(1)}, bf16[8,64,128]{2,1,0:T(8,128)(2,1)S(1)}, u32[]{:S(2)}, u32[]{:S(2)}) collective-permute-start(bf16[8,64,128]{2,1,0:T(8,128)(2,1)S(1)} %constant_dynamic-update-slice_fusion), channel_id=1, source_target_pairs={{0,4},{2,6},{4,0},{6,2},{8,12},{10,14},{12,8},{14,10},{16,20},{18,... | collective-permute-start | bytes 393224 | tf_op jit(solution)/shard_map/weights/ppermute | solution.py:34
  19.8 5.0 %collective-permute-start.17 = (bf16[8,64,128]{2,1,0:T(8,128)(2,1)S(1)}, bf16[8,64,128]{2,1,0:T(8,128)(2,1)S(1)}, u32[]{:S(2)}, u32[]{:S(2)}) collective-permute-start(bf16[8,64,128]{2,1,0:T(8,128)(2,1)S(1)} %collective-permute-done.14), channel_id=1, source_target_pairs={{0,8},{2,10},{4,12},{6,14},{8,0},{10,2},{12,4},{14,6},{16,24},{18,... | collective-permute-start | bytes 393224 | tf_op jit(solution)/shard_map/weights/ppermute | solution.py:34
  24.8 6.4 %collective-permute-start.18 = (bf16[16,64,128]{2,1,0:T(8,128)(2,1)S(1)}, bf16[16,64,128]{2,1,0:T(8,128)(2,1)S(1)}, u32[]{:S(2)}, u32[]{:S(2)}) collective-permute-start(bf16[16,64,128]{2,1,0:T(8,128)(2,1)S(1)} %constant_dynamic-update-slice_fusion.4.refs_2_), channel_id=1, source_target_pairs={{0,4},{2,6},{4,0},{6,2},{8,12},{10,14},{12,8},{14,10},{16,20},{18,... | collective-permute-start | bytes 786440 | tf_op jit(solution)/shard_map/weights/ppermute | solution.py:34
  25.4 6.4 %collective-permute-start.16 = (bf16[16,64,128]{2,1,0:T(8,128)(2,1)S(1)}, bf16[16,64,128]{2,1,0:T(8,128)(2,1)S(1)}, u32[]{:S(2)}, u32[]{:S(2)}) collective-permute-start(bf16[16,64,128]{2,1,0:T(8,128)(2,1)S(1)} %constant_dynamic-update-slice_fusion.2.refs_0_), channel_id=1, source_target_pairs={{0,8},{2,10},{4,12},{6,14},{8,0},{10,2},{12,4},{14,6},{16,24},{18,... | collective-permute-start | bytes 786440 | tf_op jit(solution)/shard_map/weights/ppermute | solution.py:34
  27.1 10.1 %collective-permute-start.19 = (bf16[1,128,4096]{2,1,0:T(8,128)(2,1)S(1)}, bf16[1,128,4096]{2,1,0:T(8,128)(2,1)S(1)}, u32[]{:S(2)}, u32[]{:S(2)}) collective-permute-start(bf16[1,128,4096]{2,1,0:T(8,128)(2,1)S(1)} %bitcast.9), channel_id=1, source_target_pairs={{0,1},{1,0},{2,3},{3,2},{4,5},{5,4},{6,7},{7,6},{8,9},{9,8},{10,11... | collective-permute-start | bytes 3145736 | tf_op jit(solution)/shard_map/tokens/ppermute | solution.py:34
  31.9 9.2 %collective-permute-start.21 = (bf16[1,128,4096]{2,1,0:T(8,128)(2,1)S(1)}, bf16[1,128,4096]{2,1,0:T(8,128)(2,1)S(1)}, u32[]{:S(2)}, u32[]{:S(2)}) collective-permute-start(bf16[1,128,4096]{2,1,0:T(8,128)(2,1)S(1)} %bitcast.7), channel_id=1, source_target_pairs={{0,1},{1,0},{2,3},{3,2},{4,5},{5,4},{6,7},{7,6},{8,9},{9,8},{10,11... | collective-permute-start | bytes 3145736 | tf_op jit(solution)/shard_map/tokens/ppermute | solution.py:34
  31.9 14.3 %collective-permute-start.22 = (bf16[32,64,128]{2,1,0:T(8,128)(2,1)S(1)}, bf16[32,64,128]{2,1,0:T(8,128)(2,1)S(1)}, u32[]{:S(2)}, u32[]{:S(2)}) collective-permute-start(bf16[32,64,128]{2,1,0:T(8,128)(2,1)S(1)} %get-tuple-element.91), channel_id=1, source_target_pairs={{0,2},{2,0},{4,6},{6,4},{8,10},{10,8},{12,14},{14,12},{16,18},{18,... | collective-permute-start | bytes 1572872 | tf_op jit(solution)/shard_map/upstream/ppermute | solution.py:34
  34.5 1.4 %collective-permute-start.13 = (s32[1]{0:T(128)}, s32[1]{0:T(128)}, u32[]{:S(2)}, u32[]{:S(2)}) collective-permute-start(s32[1]{0:T(128)} %bitcast.3), channel_id=1, source_target_pairs={{0,1},{1,0},{2,3},{3,2},{4,5},{5,4},{6,7},{7,6},{8,9},{9,8},{10,11... | collective-permute-start | bytes 20 | tf_op jit(solution)/shard_map/plan/ppermute | solution.py:34
  47.6 10.3 %collective-permute-start.6 = (bf16[45,32,128]{2,1,0:T(8,128)(2,1)S(1)}, bf16[45,32,128]{2,1,0:T(8,128)(2,1)S(1)}, u32[]{:S(2)}, u32[]{:S(2)}) collective-permute-start(bf16[45,32,128]{2,1,0:T(8,128)(2,1)S(1)} %get-tuple-element.48), channel_id=1, source_target_pairs={{0,4},{2,6},{4,0},{6,2},{8,12},{10,14},{12,8},{14,10},{16,20},{18,... | collective-permute-start | bytes 1105928 | tf_op jit(solution)/shard_map/cond/branch_1_fun/ppermute | solution.py:34
  49.2 11.2 %collective-permute-start.7 = (bf16[45,32,128]{2,1,0:T(8,128)(2,1)S(1)}, bf16[45,32,128]{2,1,0:T(8,128)(2,1)S(1)}, u32[]{:S(2)}, u32[]{:S(2)}) collective-permute-start(bf16[45,32,128]{2,1,0:T(8,128)(2,1)S(1)} %get-tuple-element.51), channel_id=1, source_target_pairs={{0,8},{2,10},{4,12},{6,14},{8,0},{10,2},{12,4},{14,6},{16,24},{18,... | collective-permute-start | bytes 1105928 | tf_op jit(solution)/shard_map/cond/branch_1_fun/ppermute | solution.py:34
  58.7 6.6 %collective-permute-start.8 = (bf16[29,32,128]{2,1,0:T(8,128)(2,1)S(1)}, bf16[29,32,128]{2,1,0:T(8,128)(2,1)S(1)}, u32[]{:S(2)}, u32[]{:S(2)}) collective-permute-start(bf16[29,32,128]{2,1,0:T(8,128)(2,1)S(1)} %get-tuple-element.53), channel_id=1, source_target_pairs={{0,8},{2,10},{4,12},{6,14},{8,0},{10,2},{12,4},{14,6},{16,24},{18,... | collective-permute-start | bytes 712712 | tf_op jit(solution)/shard_map/cond/branch_1_fun/ppermute | solution.py:34
  61.2 6.3 %collective-permute-start.9 = (bf16[29,32,128]{2,1,0:T(8,128)(2,1)S(1)}, bf16[29,32,128]{2,1,0:T(8,128)(2,1)S(1)}, u32[]{:S(2)}, u32[]{:S(2)}) collective-permute-start(bf16[29,32,128]{2,1,0:T(8,128)(2,1)S(1)} %get-tuple-element.54), channel_id=1, source_target_pairs={{0,4},{2,6},{4,0},{6,2},{8,12},{10,14},{12,8},{14,10},{16,20},{18,... | collective-permute-start | bytes 712712 | tf_op jit(solution)/shard_map/cond/branch_1_fun/ppermute | solution.py:34
  68.4 15.8 %collective-permute-start.10 = (bf16[21,64,128]{2,1,0:T(8,128)(2,1)S(1)}, bf16[21,64,128]{2,1,0:T(8,128)(2,1)S(1)}, u32[]{:S(2)}, u32[]{:S(2)}) collective-permute-start(bf16[21,64,128]{2,1,0:T(8,128)(2,1)S(1)} %get-tuple-element.56), channel_id=1, source_target_pairs={{0,16},{2,18},{4,20},{6,22},{8,24},{10,26},{12,28},{14,30},{16,0},... | collective-permute-start | bytes 1032200 | tf_op jit(solution)/shard_map/cond/branch_1_fun/ppermute | solution.py:34
  85.1 7.1 %collective-permute-start.11 = (bf16[12,64,128]{2,1,0:T(8,128)(2,1)S(1)}, bf16[12,64,128]{2,1,0:T(8,128)(2,1)}, u32[]{:S(2)}, u32[]{:S(2)}) collective-permute-start(bf16[12,64,128]{2,1,0:T(8,128)(2,1)S(1)} %get-tuple-element.58), channel_id=1, source_target_pairs={{0,2},{2,0},{4,6},{6,4},{8,10},{10,8},{12,14},{14,12},{16,18},{18,... | collective-permute-start | bytes 589832 | tf_op jit(solution)/shard_map/cond/branch_1_fun/ppermute | solution.py:34

commit v3 on v2

v3 whole, which is shorter than its diff:
```python
import functools

import jax
import jax.numpy as jnp
import numpy as np
from jax import lax
from jax.experimental import pallas as pl
from jax.experimental.pallas import tpu as pltpu
from jax.sharding import PartitionSpec as P

VMEM = pl.BlockSpec(memory_space=pltpu.VMEM)
SMEM = pl.BlockSpec(memory_space=pltpu.SMEM)
BF16 = jnp.bfloat16
F32 = jnp.float32


def call(body, name, outs, in_specs, args, flops=0, scratch=()):
    moved = sum(int(np.prod(o.shape)) * o.dtype.itemsize for o in outs)
    moved += sum(int(np.prod(a.shape)) * a.dtype.itemsize for a in args)
    return pl.pallas_call(
        body,
        name=name,
        out_shape=tuple(outs),
        in_specs=in_specs,
        out_specs=tuple(VMEM for _ in outs),
        scratch_shapes=list(scratch),
        compiler_params=pltpu.CompilerParams(vmem_limit_bytes=40 << 20),
        cost_estimate=pl.CostEstimate(flops=flops, bytes_accessed=moved, transcendentals=0),
    )(*args)


def swap(value, axis, bit):
    size = lax.axis_size(axis)
    return lax.ppermute(value, axis, [(i, i ^ (1 << bit)) for i in range(size)])


def spread(value):
    parts = [value[None]]
    for bit in range(lax.axis_size("tensor").bit_length() - 1):
        whole = parts[0] if len(parts) == 1 else jnp.concatenate(parts, 0)
        parts.append(swap(whole, "tensor", bit))
    return parts


def split_masters(place, masters, kept, sent):
    half = kept.shape[1]
    for block in range(masters.shape[1]):
        turned = masters[0, block].T.astype(BF16)

        @pl.when(place[0] == 0)
        def _():
            kept[block] = turned[:half]
            sent[block] = turned[half:]

        @pl.when(place[0] != 0)
        def _():
            kept[block] = turned[half:]
            sent[block] = turned[:half]


def split_upstream(place, grad, kept, *refs):
    parts, blocks, arrived = refs[:-2], refs[-2], refs[-1]
    count, half, side = kept.shape[0], kept.shape[1], kept.shape[2]

    def fetch(k):
        start = pl.multiple_of(place[3 + count + k] * side, side)
        return pltpu.make_async_copy(grad.at[:, pl.ds(start, side)], blocks.at[k], arrived.at[k])

    for k in range(count):
        fetch(k).start()
    for k in range(count):
        fetch(k).wait()
        turned = blocks[k].T
        low, high = turned[:half], turned[half:]
        swapped = place[0] != 0
        kept[k] = jnp.where(swapped, high, low)
        sent = jnp.where(swapped, low, high)
        start = 0
        for part in parts:
            part[k] = sent[start : start + part.shape[1]]
            start += part.shape[1]


def select_rows(first, place, *refs):
    sources, before, chosen = refs[: 1 if first == 0 else -2], refs[-2], refs[-1]
    side = chosen.shape[2]
    per_shard = sources[0].shape[2] // side
    for k in range(chosen.shape[0]):
        shard = place[3 + k] // per_shard
        start = pl.multiple_of((place[3 + k] - shard * per_shard) * side, side)
        offset = shard ^ place[1]
        value, at = None if first == 0 else before[k], first
        for source in sources:
            size = source.shape[0]
            here = source[jnp.clip(offset - at, 0, size - 1), :, pl.ds(start, side)]
            value = here if value is None else jnp.where(offset >= at, here, value)
            at += size
        chosen[k] = value


def add_duplicates(first, table, total):
    for k in range(1, total.shape[0]):

        @pl.when(table[first, k] != k)
        def _():
            total[table[first, k]] += total[k]


def slopes(gate, up):
    sigmoid = 0.5 + 0.5 * jnp.tanh(0.5 * gate)
    return sigmoid * up * (1.0 + gate * (1.0 - sigmoid)), sigmoid * gate


def project(weight, source):
    return lax.dot_general(weight, source, (((1,), (1,)), ((), ())), preferred_element_type=F32)


def term(upstream, gate_slope, up_slope, source):
    upstream = upstream.astype(F32)
    both = [(upstream * gate_slope).astype(BF16), (upstream * up_slope).astype(BF16)]
    return jnp.dot(jnp.concatenate(both, axis=0), source, preferred_element_type=F32)


def own_part(rows, table, *refs):
    sources, own_tokens, own_up, weights, grad, total = refs[:4], refs[4], refs[5], refs[6], refs[7], refs[8]
    places, half = own_up.shape[0], own_up.shape[1]
    position = 0
    for source in sources:
        for p in range(source.shape[0]):
            block = table[rows["order"], position + p]
            up = (block >= places).astype(jnp.int32)
            weights[block - up * places, pl.ds(pl.multiple_of(up * half, half), half), :] = source[p]
        position += source.shape[0]
    for k in range(places):
        total[k] = project(weights[k], own_tokens[k])
    add_duplicates(rows["first"], table, total)
    for k in range(places):
        first = table[rows["first"], k]
        grad[k] = term(own_up[k], *slopes(total[first, :half], total[first, half:]), own_tokens[k])


def other_slopes(rows, table, weights, other_tokens, slope, total):
    places, half = weights.shape[0], weights.shape[1] // 2
    for k in range(places):
        total[k] = project(weights[k], other_tokens[k])
    add_duplicates(rows["first"], table, total)
    for k in range(places):
        first = table[rows["first"], k]
        slope[k, :half], slope[k, half:] = slopes(total[first, :half], total[first, half:])


def other_part(rows, names, start, table, slope, other_tokens, other_up, grad, *refs):
    outs, total = refs[:-1], refs[-1]
    places, height, half = other_up.shape[0], other_up.shape[1], grad.shape[1] // 2
    gate, up = pl.ds(start, height), pl.ds(half + start, height)
    for k in range(places):
        result = term(other_up[k], slope[k, gate], slope[k, up], other_tokens[k])
        total[k, :height] = grad[k, gate] + result[:height]
        total[k, height:] = grad[k, up] + result[height:]
    first = 0
    for n, name in enumerate(names):
        sent, kept = outs[2 * n], outs[2 * n + 1]
        room, size = sent.shape[0], sent.shape[1]
        for block in range(2 * places):
            which, k = divmod(block, places)
            value = total[k, pl.ds(which * height + first, size), :]
            sent[jnp.minimum(table[rows[name, "sent"], block], room - 1)] = value.astype(BF16)
            kept[jnp.minimum(table[rows[name, "kept"], block], room - 1)] = value
        first += size


def combine(sent_row, kept_row, table, kept_in, received, sent, kept):
    room = sent.shape[0]
    for r in range(kept_in.shape[0] - 1):
        value = kept_in[r] + received[r].astype(F32)
        sent[jnp.minimum(table[sent_row, r], room - 1)] = value.astype(BF16)
        kept[jnp.minimum(table[kept_row, r], room - 1)] = value


def combine_last(sent_row, kept_row, count_row, table, kept_in, received, sent, kept):
    def step(r, _):
        value = kept_in[r] + received[r].astype(F32)
        away = table[sent_row, r]

        @pl.when(away >= 0)
        def _():
            sent[jnp.minimum(away, sent.shape[0] - 1)] = value.astype(BF16)

        @pl.when(away < 0)
        def _():
            kept[jnp.minimum(table[kept_row, r], kept.shape[0] - 1)] = value

        return 0

    lax.fori_loop(0, jnp.minimum(table[count_row, 0], kept_in.shape[0]), step, 0)


def finish(count_row, place, table, *refs):
    ends, out = refs[:-1], refs[-1]
    count = table[count_row, 0]
    swapped = place[0] != 0
    for slot in range(out.shape[1]):
        mine = jnp.concatenate([end[slot] for end in ends[0::2]], axis=0)
        other = jnp.concatenate([end[slot] for end in ends[1::2]], axis=0).astype(F32)
        low, high = jnp.where(swapped, other, mine), jnp.where(swapped, mine, other)
        whole = jnp.concatenate([low, high], axis=0).T
        out[0, slot] = jnp.where(slot < count, whole, 0.0)


def axes_of(owner_count):
    bits = owner_count.bit_length() - 1
    if bits == 4:
        y, near, far = 1, 2, 3
        parts = ((1, (y, near, far)), (1, (near, y, far))), ((1, (y, far, near)), (1, (near, y, far)))
        turns = tuple((part, 0) for part in range(2)) + tuple((piece, n) for n in range(1, 4) for piece in range(4))
        return 0, (y, near), (far,), parts, turns
    pair, ends, rest = bits - 2, (0, bits - 1), tuple(range(1, bits - 2))
    parts = ((2, (*ends, *rest)),), ((2, (*ends[::-1], *rest)),)
    return pair, ends, rest, parts, tuple((piece, n) for n in range(bits) for piece in range(2))


def steps_of(axes):
    pair, _, _, parts, _ = axes
    steps = {}
    for part in parts:
        for _, order in part:
            order = (*order, pair)
            for n, bit in enumerate(order):
                steps[tuple(sorted(order[:n])), bit] = None
    return list(steps)


def rows_of(axes):
    names = ["order", "first", "last", "end", "fits"]
    names += [(step, kind) for step in steps_of(axes) for kind in ("sent", "kept")]
    return {name: n for n, name in enumerate(names)}


def make_plan(axes, usual, own_blocks, place, owners, columns, found, table):
    pair, rows = axes[0], rows_of(axes)
    count, places = owners.shape[1], columns.shape[1]
    me = place[2]
    across = lax.broadcasted_iota(jnp.int32, (count, count), 1)
    down = lax.broadcasted_iota(jnp.int32, (count, count), 0)
    owner_row, column_row = owners[...], columns[...]

    def as_column(row):
        size = row.shape[1]
        kept = jnp.where((across == down)[:size, :size], row.astype(F32), 0.0)
        return jnp.sum(kept, axis=1, keepdims=True).astype(jnp.int32)

    owner_col, column_col = as_column(owner_row), as_column(column_row)
    before = across < down
    differs_row, differs_col = owner_row ^ me, owner_col ^ me

    def alive(differs, done):
        return (differs & sum(1 << b for b in done)) == 0

    def number(mask):
        return jnp.where(mask, 1.0, 0.0)

    def rank(mask_row):
        return jnp.sum(jnp.where(before, number(mask_row), 0.0), axis=1, keepdims=True)

    def turned(column):
        return jnp.sum(jnp.where(across == down, column, 0.0), axis=0, keepdims=True)

    def write(name, row):
        table[pl.ds(rows[name], 1), :] = row.astype(jnp.int32)

    def going(done, bit):
        live, away = alive(differs_row, done), ((differs_row >> bit) & 1) == 1
        return rank(jnp.logical_and(live, away)), rank(jnp.logical_and(live, jnp.logical_not(away)))

    table[...] = jnp.zeros(table.shape, jnp.int32)
    table[pl.ds(rows["order"], 1), :] = (found[0:1, :] ^ me) * own_blocks + found[1:2, :]
    same = column_row == column_col
    place_at = lax.broadcasted_iota(jnp.int32, (places, places), 0).astype(F32)
    first = jnp.min(jnp.where(same, place_at, float(places)), axis=0, keepdims=True)
    table[pl.ds(rows["first"], 1), :places] = first.astype(jnp.int32)
    full, at_most, everything = float(count), None, ()
    for step in steps_of(axes):
        done, bit = step
        sent, kept = going(done, bit)
        if not done:
            write((step, "sent"), turned(sent))
            write((step, "kept"), turned(kept))
            continue
        live = rank(alive(differs_row, done))
        hit = jnp.logical_and(alive(differs_col, done), live == across.astype(F32))
        if bit == pair:
            sent, everything = jnp.where(((differs_col >> bit) & 1) == 1, sent, -1.0), done
        for kind, values in (("sent", sent), ("kept", kept)):
            write((step, kind), full + jnp.sum(jnp.where(hit, values - full, 0.0), axis=0, keepdims=True))
    for done, most in usual.items():
        mask = sum(1 << b for b in done)
        group = (owner_row & mask) == (owner_col & mask)
        over = jnp.max(jnp.sum(number(group), axis=1, keepdims=True), axis=0, keepdims=True) - most
        at_most = over if at_most is None else jnp.maximum(at_most, over)
    for name, done in (("last", everything), ("end", (*everything, pair))):
        total = jnp.sum(number(alive(differs_row, done)), axis=1, keepdims=True)
        write(name, jnp.broadcast_to(total, (1, count)))
    fits = jnp.zeros((1, 1), F32) if at_most is None else at_most
    write("fits", jnp.broadcast_to(number(fits <= 0.0), (1, count)))


def local(tokens, hidden_grad, masters, block_row, block_col, owners):
    owner_count = lax.axis_size("dp")
    me = lax.axis_index("dp")
    axes = axes_of(owner_count)
    pair, (bit_a, bit_b), rest, parts, turns = axes
    own_blocks, side = masters.shape[1], masters.shape[2]
    places, half, quarter = block_row.shape[1], side // 2, side // 8
    block_count = owners.shape[1]
    token_count = tokens.shape[0]
    capacity = 3 * block_count // owner_count
    place = jnp.stack([(me >> pair) & 1, lax.axis_index("tensor"), me]).astype(jnp.int32)
    place = jnp.concatenate([place, block_row[0], block_col[0]])

    def struct(shape, dtype):
        return jax.ShapeDtypeStruct(shape, dtype)

    with jax.named_scope("tokens"):
        shape = [struct((places, token_count, side), BF16)]
        near = call(functools.partial(select_rows, 0), "select_rows", shape, [SMEM, VMEM], [place, tokens[None]])[0]
        first_chosen, others = near, spread(tokens)[1:]
        if others:
            near = call(
                functools.partial(select_rows, 1), "select_rows", shape, [SMEM] + [VMEM] * (len(others) + 1),
                [place, *others, near],
            )[0]
        own_chosen = near
        masters, _ = lax.optimization_barrier((masters, first_chosen))

    with jax.named_scope("weights"):
        kept, sent = call(
            split_masters, "split_masters", [struct((own_blocks, half, side), BF16)] * 2, [SMEM, VMEM], [place, masters]
        )
        entries = [(0, b) for b in range(own_blocks)]

        def moved(found, bit):
            return [(delta ^ (1 << bit), b) for delta, b in found]

        got = swap(sent, "dp", pair)
        entries = entries + moved(entries, pair)
        later, got = lax.optimization_barrier((place, got))
        other_chosen = swap(own_chosen, "dp", pair)
        current = jnp.concatenate([kept, got], 0)
        for bit in rest[:0:-1]:
            current = jnp.concatenate([current, swap(current, "dp", bit)], 0)
            entries = entries + moved(entries, bit)
        far = swap(current, "dp", rest[0])
        heights = [sum(share for share, _ in part) * quarter for part in parts]
        own_up, *sent_up = call(
            split_upstream, "split_upstream",
            [struct((places, height, token_count), BF16) for height in (half, *heights)],
            [SMEM, pl.BlockSpec(memory_space=pltpu.HBM)], [later, hidden_grad], 0,
            [pltpu.VMEM((places, token_count, side), BF16), pltpu.SemaphoreType.DMA((places,))],
        )
        current, far, sent_up = lax.optimization_barrier((current, far, sent_up))
        near_a, near_b = swap(current, "dp", bit_a), swap(far, "dp", bit_b)
        entries_a, entries_b = entries + moved(entries, bit_a), moved(entries, rest[0])
        entries_b = entries_b + moved(entries_b, bit_b)
        found = entries_a + moved(entries_a, bit_b) + entries_b + moved(entries_b, bit_a)
        found = np.array(found, np.int32).T

    with jax.named_scope("plan"):

        def most_of(done):
            return min(block_count, (owner_count >> len(done)) * capacity)

        def load_of(done):
            return min(most_of(done), (block_count >> len(done)) + capacity)

        rows = rows_of(axes)
        settled = [tuple(sorted((*done, bit))) for done, bit in steps_of(axes)]
        usual = {done: load_of(done) for done in settled if load_of(done) < most_of(done)}
        table = call(
            functools.partial(make_plan, axes, usual, own_blocks), "make_plan",
            [struct((-(-len(rows) // 8) * 8, block_count), jnp.int32)], [SMEM] + [VMEM] * 3,
            [later, owners, block_col, jnp.asarray(found)],
        )[0]
        fits = table[rows["fits"], :1]
        for bit in range(lax.axis_size("tensor").bit_length() - 1):
            fits = jnp.minimum(fits, swap(fits, "tensor", bit))

    with jax.named_scope("weights"):
        near_a, near_b, table = lax.optimization_barrier((near_a, near_b, table))
        a0, b0 = jnp.concatenate([current, near_a], 0), jnp.concatenate([far, near_b], 0)
        a1, b1 = swap(a0, "dp", bit_b), swap(b0, "dp", bit_a)
        a1, b1, fits = lax.optimization_barrier((a1, b1, fits))

    with jax.named_scope("upstream"):
        other_up = [swap(sent, "dp", pair) for sent in sent_up]

    work = 2 * 2 * places * side * side * token_count
    with jax.named_scope("own_tokens"):
        weights, grad = call(
            functools.partial(own_part, rows), "own_part",
            [struct((places, side, side), BF16), struct((places, side, side), F32)], [SMEM] + [VMEM] * 6,
            [table, a0, a1, b0, b1, own_chosen, own_up], work, [pltpu.VMEM((places, side, token_count), F32)],
        )
    with jax.named_scope("other_tokens"):
        slope = call(
            functools.partial(other_slopes, rows), "other_slopes", [struct((places, side, token_count), F32)],
            [SMEM, VMEM, VMEM], [table, weights, other_chosen], work // 2,
            [pltpu.VMEM((places, side, token_count), F32)],
        )[0]

    def reduce(load, table, slope, other_chosen, other_up, grad):
        held, got, orders, firsts, start = [], [], [], [], 0
        for part in parts:
            firsts.append((len(orders), start))
            orders += [(*order, pair) for _, order in part]
            start += sum(share for share, _ in part) * quarter
        turn = None
        for at, n in turns:
            if n == 0:
                part, up, (piece, start) = parts[at], other_up[at], firsts[at]
                steps = [((), order[0]) for _, order in part]
                shapes = [(load(step[1:]) + 1, share * quarter, side) for step, (share, _) in zip(steps, part)]
                body, spec = functools.partial(other_part, rows, steps, start), [SMEM] + [VMEM] * 4
                args, scratch = [table, slope, other_chosen, up, grad], [pltpu.VMEM((places, 2 * up.shape[1], side), F32)]
            else:
                piece, order = at, orders[at]
                step = tuple(sorted(order[:n])), order[n]
                where = rows[step, "sent"], rows[step, "kept"]
                if order[n] == pair:
                    body, room = functools.partial(combine_last, *where, rows["last"]), capacity
                else:
                    body, room = functools.partial(combine, *where), load(order[: n + 1]) + 1
                shapes = [(room, *held[piece].shape[1:])]
                spec, args, scratch = [SMEM] + [VMEM] * 2, [table, held[piece], got[piece]], []
            if turn is not None:
                args[-1], _ = lax.optimization_barrier((args[-1], turn))
            outs = call(
                body, "combine" if n else "other_part", [struct(shape, dtype) for shape in shapes for dtype in (BF16, F32)],
                spec, args, 0 if n else work // 4, scratch,
            )
            turn = outs[1]
            if n == 0:
                held, got = held + [None] * len(part), got + [None] * len(part)
            for i, (sent, kept) in enumerate(zip(outs[0::2], outs[1::2])):
                held[piece + i], got[piece + i] = kept, swap(sent, "dp", orders[piece + i][n])
        return [end for both in zip(held, got) for end in both]

    operands = (table, slope, other_chosen, other_up, grad)
    ends = reduce(load_of, *operands)
    ends = lax.cond(fits[0] == 1, lambda ends, operands: ends, lambda ends, operands: reduce(most_of, *operands), ends, operands)
    return call(
        functools.partial(finish, rows["end"]), "finish", [struct((1, capacity, side, side), F32)],
        [SMEM, SMEM] + [VMEM] * len(ends), [place, table, *ends],
    )[0]


def solution(mesh):
    return jax.shard_map(
        local,
        mesh=mesh,
        in_specs=(
            P("dp", "tensor"),
            P("dp", "tensor"),
            P("tensor", "dp", None, None),
            P("tensor", None),
            P("tensor", None),
            P("tensor", None),
        ),
        out_specs=P("tensor", "dp", None, None),
        check_vma=False,
    )
```

time: 94.7 us -> 83.8 us (0.88)
  waiting for transfers between devices: 45.3 us -> 15.1 us
  starting transfers between devices: 24.9 us -> 36.2 us
  Pallas kernels: 18.6 us -> 27.7 us
  local copies, waits for them, and re-layouts: 4.25 us -> 2.7 us
    ppermute x17 -> x27, waiting for transfers between devices: 45.3 us -> 15.1 us  [swap(): return lax.ppermute(value, axis, [(i, i ^ 1 << bit) for i in range(size)])]
    ppermute x17 -> x27, starting transfers between devices: 24.9 us -> 36.2 us  [swap(): return lax.ppermute(value, axis, [(i, i ^ 1 << bit) for i in range(size)])]
    pallas_call x12 -> x22, Pallas kernels: 18.6 us -> 27.7 us  [call(): pl.pallas_call(body, name=name, out_shape=tuple(outs), in_specs=in_specs,...]
    unnamed x19 -> x15, local copies, waits for them, and re-layouts: 3.69 us -> 1.37 us
  transfers between devices with their start and end apart: 17 -> 27, of which waited for: 11 -> 10; matrix products, arithmetic and copies ran while one was open for 1% -> 2% of each run, Pallas kernels for 13% -> 31%
where the time goes in v3:
time: 83.8 us; the launch traced here: 83.3 us
  starting transfers between devices  36.2 us (43%)
  Pallas kernels  27.7 us (33%)
  waiting for transfers between devices  15.1 us (18%)
  local copies, waits for them, and re-layouts  2.7 us (3%)
  between operations  1.52 us (2%)
    ppermute x27, starting transfers between devices, swap(): return lax.ppermute(value, axis, [(i, i ^ 1 << bit) for i in range(size)])  36.2 us
    pallas_call x22, Pallas kernels, call(): pl.pallas_call(body, name=name, out_shape=tuple(outs), in_specs=in_specs,...  27.7 us
    ppermute x27, waiting for transfers between devices, swap(): return lax.ppermute(value, axis, [(i, i ^ 1 << bit) for i in range(size)])  15.1 us
  transfers between devices with their start and end apart: 27, of which 10 were waited for; matrix products, arithmetic and copies ran while one was open for 2% of the time, Pallas kernels for 31%

profile of v3, /device:TPU:0, one launch (start us, length us, event | category | flops | bytes accessed | tf_op | source)
XLA Modules:
  0.0 83.3 jit_solution(11124641288948382082)
XLA Ops:
  0.0 0.5 collective-permute-start.23
  0.5 0.7 concatenate.12.place
  1.2 1.2 %copy-done.1 = bf16[128,4096]{1,0:T(8,128)(2,1)S(1)} copy-done((bf16[128,4096]{1,0:T(8,128)(2,1)S(1)}, bf16[128,4096]{1,0:T(8,128)(2,1)}, u32[]{:S(2)}) %copy-start.1) | copy-done | bytes 1048600
  2.4 0.8 %select_rows.2.refs_1_ = bf16[32,128,128]{2,1,0:T(8,128)(2,1)S(1)} custom-call(s32[67]{0:T(128)S(1)} %concatenate.12.place, bf16[1,128,4096]{2,1,0:T(8,128)(2,1)S(1)} %bitcast.9), custom_call_target="tpu_custom_call" | custom-call | bytes 2097420 | tf_op jit(solution)/shard_map/tokens/select_rows/pallas_call | solution.py:20
  3.3 0.1 copy-done.2
  3.4 0.9 %split_masters.1 = (bf16[4,64,128]{2,1,0:T(8,128)(2,1)S(1)}, bf16[4,64,128]{2,1,0:T(8,128)(2,1)S(1)}) custom-call(s32[67]{0:T(128)S(1)} %concatenate.12.place, f32[1,4,128,128]{3,2,1,0:T(8,128)S(1)} %copy-done.2), custom_call_target="tpu_custom_call" | custom-call | bytes 393484 | tf_op jit(solution)/shard_map/weights/split_masters/pallas_call | solution.py:20
  4.3 2.5 %collective-permute-start.16 = (bf16[4,64,128]{2,1,0:T(8,128)(2,1)S(1)}, bf16[4,64,128]{2,1,0:T(8,128)(2,1)S(1)}, u32[]{:S(2)}, u32[]{:S(2)}) collective-permute-start(bf16[4,64,128]{2,1,0:T(8,128)(2,1)S(1)} %get-tuple-element.159), channel_id=1, source_target_pairs={{0,2},{2,0},{4,6},{6,4},{8,10},{10,8},{12,14},{14,12},{16,18},{18,... | collective-permute-start | bytes 196616 | tf_op jit(solution)/shard_map/weights/ppermute | solution.py:34
  6.9 0.9 %select_rows.3.refs_4_ = bf16[32,128,128]{2,1,0:T(8,128)(2,1)S(1)} custom-call(s32[67]{0:T(128)S(1)} %concatenate.12.place, bf16[1,128,4096]{2,1,0:T(8,128)(2,1)S(1)} %collective-permute-done.23.refs_0_, bf16[32,128,128]{2,1,0:T(8,128)(2,1)S(1)} %select_rows.2.refs_1_), custom_call_target="tpu_custom_call" | custom-call | bytes 3145996 | tf_op jit(solution)/shard_map/tokens/select_rows/pallas_call | solution.py:20
  7.8 0.0 copy-start.4
  7.8 0.1 collective-permute-start.24
  7.9 1.7 %collective-permute-done.16 = bf16[4,64,128]{2,1,0:T(8,128)(2,1)S(1)} collective-permute-done((bf16[4,64,128]{2,1,0:T(8,128)(2,1)S(1)}, bf16[4,64,128]{2,1,0:T(8,128)(2,1)S(1)}, u32[]{:S(2)}, u32[]{:S(2)}) %collective-permute-start.16) | collective-permute-done | bytes 65568 | tf_op jit(solution)/shard_map/weights/ppermute | solution.py:34
  9.7 2.9 %collective-permute-start.17 = (bf16[8,64,128]{2,1,0:T(8,128)(2,1)S(1)}, bf16[8,64,128]{2,1,0:T(8,128)(2,1)S(1)}, u32[]{:S(2)}, u32[]{:S(2)}) collective-permute-start(bf16[8,64,128]{2,1,0:T(8,128)(2,1)S(1)} %constant_dynamic-update-slice_fusion), channel_id=1, source_target_pairs={{0,16},{2,18},{4,20},{6,22},{8,24},{10,26},{12,28},{14,30},{16,0},... | collective-permute-start | bytes 393224 | tf_op jit(solution)/shard_map/weights/ppermute | solution.py:34
  12.6 3.6 %split_upstream.1 = (bf16[32,64,128]{2,1,0:T(8,128)(2,1)S(1)}, bf16[32,32,128]{2,1,0:T(8,128)(2,1)S(1)}, bf16[32,32,128]{2,1,0:T(8,128)(2,1)S(1)}) custom-call(s32[67]{0:T(128)S(1)} %concatenate.12.place, bf16[128,14336]{1,0:T(8,128)(2,1)S(1)} %copy-done), custom_call_target="tpu_custom_call" | custom-call | bytes 4718860 | tf_op jit(solution)/shard_map/weights/split_upstream/pallas_call | solution.py:20
  16.2 0.9 %make_plan.1.table = s32[24,64]{1,0:T(8,128)S(1)} custom-call(s32[67]{0:T(128)S(1)} %concatenate.12.place, s32[1,64]{1,0:T(1,128)S(1)} %copy-done.5, s32[1,32]{1,0:T(1,128)S(1)} %copy-done.3, s32[2,64]{1,0:T(2,128)S(1)} %copy-done.4), custom_call_target="tpu_custom_call" | custom-call | bytes 7308 | tf_op jit(solution)/shard_map/plan/make_plan/pallas_call | solution.py:20
  17.1 1.7 %collective-permute-done.17 = bf16[8,64,128]{2,1,0:T(8,128)(2,1)S(1)} collective-permute-done((bf16[8,64,128]{2,1,0:T(8,128)(2,1)S(1)}, bf16[8,64,128]{2,1,0:T(8,128)(2,1)S(1)}, u32[]{:S(2)}, u32[]{:S(2)}) %collective-permute-start.17) | collective-permute-done | bytes 131104 | tf_op jit(solution)/shard_map/weights/ppermute | solution.py:34
  18.8 1.6 %collective-permute-start.18 = (bf16[8,64,128]{2,1,0:T(8,128)(2,1)S(1)}, bf16[8,64,128]{2,1,0:T(8,128)(2,1)S(1)}, u32[]{:S(2)}, u32[]{:S(2)}) collective-permute-start(bf16[8,64,128]{2,1,0:T(8,128)(2,1)S(1)} %constant_dynamic-update-slice_fusion), channel_id=1, source_target_pairs={{0,4},{2,6},{4,0},{6,2},{8,12},{10,14},{12,8},{14,10},{16,20},{18,... | collective-permute-start | bytes 393224 | tf_op jit(solution)/shard_map/weights/ppermute | solution.py:34
  20.3 0.7 collective-permute-start.19
  21.0 2.7 %collective-permute-done.18 = bf16[8,64,128]{2,1,0:T(8,128)(2,1)S(1)} collective-permute-done((bf16[8,64,128]{2,1,0:T(8,128)(2,1)S(1)}, bf16[8,64,128]{2,1,0:T(8,128)(2,1)S(1)}, u32[]{:S(2)}, u32[]{:S(2)}) %collective-permute-start.18) | collective-permute-done | bytes 131104 | tf_op jit(solution)/shard_map/weights/ppermute | solution.py:34
  23.7 1.6 %collective-permute-done.19 = bf16[8,64,128]{2,1,0:T(8,128)(2,1)S(1)} collective-permute-done((bf16[8,64,128]{2,1,0:T(8,128)(2,1)S(1)}, bf16[8,64,128]{2,1,0:T(8,128)(2,1)S(1)}, u32[]{:S(2)}, u32[]{:S(2)}) %collective-permute-start.19) | collective-permute-done | bytes 131104 | tf_op jit(solution)/shard_map/weights/ppermute | solution.py:34
  25.3 0.5 collective-permute-start.21
  25.9 1.0 %collective-permute-start.20 = (bf16[16,64,128]{2,1,0:T(8,128)(2,1)S(1)}, bf16[16,64,128]{2,1,0:T(8,128)(2,1)S(1)}, u32[]{:S(2)}, u32[]{:S(2)}) collective-permute-start(bf16[16,64,128]{2,1,0:T(8,128)(2,1)S(1)} %constant_dynamic-update-slice_fusion.2.refs_0_), channel_id=1, source_target_pairs={{0,8},{2,10},{4,12},{6,14},{8,0},{10,2},{12,4},{14,6},{16,24},{18,... | collective-permute-start | bytes 786440 | tf_op jit(solution)/shard_map/weights/ppermute | solution.py:34
  26.8 1.5 %collective-permute-start.25 = (bf16[32,32,128]{2,1,0:T(8,128)(2,1)S(1)}, bf16[32,32,128]{2,1,0:T(8,128)(2,1)S(1)}, u32[]{:S(2)}, u32[]{:S(2)}) collective-permute-start(bf16[32,32,128]{2,1,0:T(8,128)(2,1)S(1)} %get-tuple-element.174), channel_id=1, source_target_pairs={{0,2},{2,0},{4,6},{6,4},{8,10},{10,8},{12,14},{14,12},{16,18},{18,... | collective-permute-start | bytes 786440 | tf_op jit(solution)/shard_map/upstream/ppermute | solution.py:34
  28.3 0.5 slice.4
  28.8 1.4 %collective-permute-done.22 = s32[1]{0:T(128)} collective-permute-done((s32[1]{0:T(128)}, s32[1]{0:T(128)}, u32[]{:S(2)}, u32[]{:S(2)}) %collective-permute-start.22) | collective-permute-done | bytes 36 | tf_op jit(solution)/shard_map/plan/ppermute | solution.py:34
  30.2 0.5 collective-permute-start.26
  32.0 0.3 collective-permute-done.20.refs_1_
  32.3 2.7 %own_part.1 = (bf16[32,128,128]{2,1,0:T(8,128)(2,1)S(1)}, f32[32,128,128]{2,1,0:T(8,128)S(1)}) custom-call(s32[24,64]{1,0:T(8,128)S(1)} %make_plan.1.table, bf16[16,64,128]{2,1,0:T(8,128)(2,1)S(1)} %constant_dynamic-update-slice_fusion.2.refs_0_, bf16[16,64,128]{2,1,0:T(8,128)(2,1)S(1)} %collective-permute-done.20.refs_1_, ...), custom_call_target="tpu_custom_call" | custom-call | flops 268435456 | bytes 5773312 | tf_op jit(solution)/shard_map/own_tokens/own_part/pallas_call | solution.py:20
  35.0 2.2 %other_slopes.1.slope = f32[32,128,128]{2,1,0:T(8,128)S(1)} custom-call(s32[24,64]{1,0:T(8,128)S(1)} %make_plan.1.table, bf16[32,128,128]{2,1,0:T(8,128)(2,1)S(1)} %get-tuple-element.173.weights, bf16[32,128,128]{2,1,0:T(8,128)(2,1)S(1)} %collective-permute-done.24.other_tokens), custom_call_target="tpu_custom_call" | custom-call | flops 134217728 | bytes 4200448 | tf_op jit(solution)/shard_map/other_tokens/other_slopes/pallas_call | solution.py:20
  37.2 2.3 %collective-permute-done.25.other_up = bf16[32,32,128]{2,1,0:T(8,128)(2,1)S(1)} collective-permute-done((bf16[32,32,128]{2,1,0:T(8,128)(2,1)S(1)}, bf16[32,32,128]{2,1,0:T(8,128)(2,1)S(1)}, u32[]{:S(2)}, u32[]{:S(2)}) %collective-permute-start.25) | collective-permute-done | bytes 262176 | tf_op jit(solution)/shard_map/upstream/ppermute | solution.py:34
  39.5 1.3 %other_part.6 = (bf16[45,16,128]{2,1,0:T(8,128)(2,1)S(1)}, f32[45,16,128]{2,1,0:T(8,128)S(1)}, bf16[45,16,128]{2,1,0:T(8,128)(2,1)S(1)}, f32[45,16,128]{2,1,0:T(8,128)S(1)}) custom-call(s32[24,64]{1,0:T(8,128)S(1)} %make_plan.1.table, f32[32,128,128]{2,1,0:T(8,128)S(1)} %other_slopes.1.slope, bf16[32,128,128]{2,1,0:T(8,128)(2,1)S(1)} %collective-permute-done.24.other_tokens, ...), custom_call_target="tpu_custom_call" | custom-call | flops 67108864 | bytes 6617088 | tf_op jit(solution)/shard_map/other_part/pallas_call | solution.py:20
  40.8 1.6 %collective-permute-start.27 = (bf16[45,16,128]{2,1,0:T(8,128)(2,1)S(1)}, bf16[45,16,128]{2,1,0:T(8,128)(2,1)S(1)}, u32[]{:S(2)}, u32[]{:S(2)}) collective-permute-start(bf16[45,16,128]{2,1,0:T(8,128)(2,1)S(1)} %get-tuple-element.178), channel_id=1, source_target_pairs={{0,4},{2,6},{4,0},{6,2},{8,12},{10,14},{12,8},{14,10},{16,20},{18,... | collective-permute-start | bytes 552968 | tf_op jit(solution)/shard_map/ppermute | solution.py:34
  42.4 1.6 %collective-permute-start.31 = (bf16[45,16,128]{2,1,0:T(8,128)(2,1)S(1)}, bf16[45,16,128]{2,1,0:T(8,128)(2,1)S(1)}, u32[]{:S(2)}, u32[]{:S(2)}) collective-permute-start(bf16[45,16,128]{2,1,0:T(8,128)(2,1)S(1)} %get-tuple-element.188), channel_id=1, source_target_pairs={{0,8},{2,10},{4,12},{6,14},{8,0},{10,2},{12,4},{14,6},{16,24},{18,... | collective-permute-start | bytes 552968 | tf_op jit(solution)/shard_map/ppermute | solution.py:34
  44.0 0.4 collective-permute-done.26.other_up
  44.4 1.3 %other_part.7 = (bf16[45,16,128]{2,1,0:T(8,128)(2,1)S(1)}, f32[45,16,128]{2,1,0:T(8,128)S(1)}, bf16[45,16,128]{2,1,0:T(8,128)(2,1)S(1)}, f32[45,16,128]{2,1,0:T(8,128)S(1)}) custom-call(s32[24,64]{1,0:T(8,128)S(1)} %make_plan.1.table, f32[32,128,128]{2,1,0:T(8,128)S(1)} %other_slopes.1.slope, bf16[32,128,128]{2,1,0:T(8,128)(2,1)S(1)} %collective-permute-done.24.other_tokens, ...), custom_call_target="tpu_custom_call" | custom-call | flops 67108864 | bytes 6617088 | tf_op jit(solution)/shard_map/other_part/pallas_call | solution.py:20
  45.7 1.6 %collective-permute-start.30 = (bf16[45,16,128]{2,1,0:T(8,128)(2,1)S(1)}, bf16[45,16,128]{2,1,0:T(8,128)(2,1)S(1)}, u32[]{:S(2)}, u32[]{:S(2)}) collective-permute-start(bf16[45,16,128]{2,1,0:T(8,128)(2,1)S(1)} %get-tuple-element.186), channel_id=1, source_target_pairs={{0,4},{2,6},{4,0},{6,2},{8,12},{10,14},{12,8},{14,10},{16,20},{18,... | collective-permute-start | bytes 552968 | tf_op jit(solution)/shard_map/ppermute | solution.py:34
  47.3 1.6 %collective-permute-start.29 = (bf16[45,16,128]{2,1,0:T(8,128)(2,1)S(1)}, bf16[45,16,128]{2,1,0:T(8,128)(2,1)S(1)}, u32[]{:S(2)}, u32[]{:S(2)}) collective-permute-start(bf16[45,16,128]{2,1,0:T(8,128)(2,1)S(1)} %get-tuple-element.185), channel_id=1, source_target_pairs={{0,8},{2,10},{4,12},{6,14},{8,0},{10,2},{12,4},{14,6},{16,24},{18,... | collective-permute-start | bytes 552968 | tf_op jit(solution)/shard_map/ppermute | solution.py:34
  48.9 0.9 %combine.36 = (bf16[29,16,128]{2,1,0:T(8,128)(2,1)S(1)}, f32[29,16,128]{2,1,0:T(8,128)S(1)}) custom-call(s32[24,64]{1,0:T(8,128)S(1)} %make_plan.1.table, f32[45,16,128]{2,1,0:T(8,128)S(1)} %get-tuple-element.177.kept_in, bf16[45,16,128]{2,1,0:T(8,128)(2,1)S(1)} %collective-permute-done.27.received), custom_call_target="tpu_custom_call" | custom-call | bytes 915456 | tf_op jit(solution)/shard_map/combine/pallas_call | solution.py:20
  49.8 0.5 collective-permute-start.28
  50.3 0.9 %combine.37 = (bf16[29,16,128]{2,1,0:T(8,128)(2,1)S(1)}, f32[29,16,128]{2,1,0:T(8,128)S(1)}) custom-call(s32[24,64]{1,0:T(8,128)S(1)} %make_plan.1.table, f32[45,16,128]{2,1,0:T(8,128)S(1)} %get-tuple-element.187.kept_in, bf16[45,16,128]{2,1,0:T(8,128)(2,1)S(1)} %collective-permute-done.31.received), custom_call_target="tpu_custom_call" | custom-call | bytes 915456 | tf_op jit(solution)/shard_map/combine/pallas_call | solution.py:20
  51.1 0.6 collective-permute-start.35
  51.7 0.0 collective-permute-done.30.received
  51.8 0.9 %combine.38 = (bf16[29,16,128]{2,1,0:T(8,128)(2,1)S(1)}, f32[29,16,128]{2,1,0:T(8,128)S(1)}) custom-call(s32[24,64]{1,0:T(8,128)S(1)} %make_plan.1.table, f32[45,16,128]{2,1,0:T(8,128)S(1)} %get-tuple-element.180.kept_in, bf16[45,16,128]{2,1,0:T(8,128)(2,1)S(1)} %collective-permute-done.30.received), custom_call_target="tpu_custom_call" | custom-call | bytes 915456 | tf_op jit(solution)/shard_map/combine/pallas_call | solution.py:20
  52.6 2.7 %collective-permute-start.34 = (bf16[29,16,128]{2,1,0:T(8,128)(2,1)S(1)}, bf16[29,16,128]{2,1,0:T(8,128)(2,1)S(1)}, u32[]{:S(2)}, u32[]{:S(2)}) collective-permute-start(bf16[29,16,128]{2,1,0:T(8,128)(2,1)S(1)} %get-tuple-element.199), channel_id=1, source_target_pairs={{0,16},{2,18},{4,20},{6,22},{8,24},{10,26},{12,28},{14,30},{16,0},... | collective-permute-start | bytes 356360 | tf_op jit(solution)/shard_map/ppermute | solution.py:34
  55.3 0.9 %combine.39 = (bf16[29,16,128]{2,1,0:T(8,128)(2,1)S(1)}, f32[29,16,128]{2,1,0:T(8,128)S(1)}) custom-call(s32[24,64]{1,0:T(8,128)S(1)} %make_plan.1.table, f32[45,16,128]{2,1,0:T(8,128)S(1)} %get-tuple-element.184.kept_in, bf16[45,16,128]{2,1,0:T(8,128)(2,1)S(1)} %collective-permute-done.29.received), custom_call_target="tpu_custom_call" | custom-call | bytes 915456 | tf_op jit(solution)/shard_map/combine/pallas_call | solution.py:20
  56.1 1.9 %collective-permute-start.33 = (bf16[29,16,128]{2,1,0:T(8,128)(2,1)S(1)}, bf16[29,16,128]{2,1,0:T(8,128)(2,1)S(1)}, u32[]{:S(2)}, u32[]{:S(2)}) collective-permute-start(bf16[29,16,128]{2,1,0:T(8,128)(2,1)S(1)} %get-tuple-element.198), channel_id=1, source_target_pairs={{0,4},{2,6},{4,0},{6,2},{8,12},{10,14},{12,8},{14,10},{16,20},{18,... | collective-permute-start | bytes 356360 | tf_op jit(solution)/shard_map/ppermute | solution.py:34
  58.0 0.8 combine.40
  58.9 1.4 %collective-permute-start.32 = (bf16[21,16,128]{2,1,0:T(8,128)(2,1)S(1)}, bf16[21,16,128]{2,1,0:T(8,128)(2,1)S(1)}, u32[]{:S(2)}, u32[]{:S(2)}) collective-permute-start(bf16[21,16,128]{2,1,0:T(8,128)(2,1)S(1)} %get-tuple-element.197), channel_id=1, source_target_pairs={{0,16},{2,18},{4,20},{6,22},{8,24},{10,26},{12,28},{14,30},{16,0},... | collective-permute-start | bytes 258056 | tf_op jit(solution)/shard_map/ppermute | solution.py:34
  60.3 0.8 combine.41
  61.1 1.6 %collective-permute-start.37 = (bf16[21,16,128]{2,1,0:T(8,128)(2,1)S(1)}, bf16[21,16,128]{2,1,0:T(8,128)(2,1)S(1)}, u32[]{:S(2)}, u32[]{:S(2)}) collective-permute-start(bf16[21,16,128]{2,1,0:T(8,128)(2,1)S(1)} %get-tuple-element.210), channel_id=1, source_target_pairs={{0,16},{2,18},{4,20},{6,22},{8,24},{10,26},{12,28},{14,30},{16,0},... | collective-permute-start | bytes 258056 | tf_op jit(solution)/shard_map/ppermute | solution.py:34
  62.7 0.8 combine.42
  63.6 1.6 %collective-permute-start.39 = (bf16[21,16,128]{2,1,0:T(8,128)(2,1)S(1)}, bf16[21,16,128]{2,1,0:T(8,128)(2,1)S(1)}, u32[]{:S(2)}, u32[]{:S(2)}) collective-permute-start(bf16[21,16,128]{2,1,0:T(8,128)(2,1)S(1)} %get-tuple-element.214), channel_id=1, source_target_pairs={{0,8},{2,10},{4,12},{6,14},{8,0},{10,2},{12,4},{14,6},{16,24},{18,... | collective-permute-start | bytes 258056 | tf_op jit(solution)/shard_map/ppermute | solution.py:34
  65.2 0.8 combine.43
  66.0 3.6 %collective-permute-start.41 = (bf16[21,16,128]{2,1,0:T(8,128)(2,1)S(1)}, bf16[21,16,128]{2,1,0:T(8,128)(2,1)S(1)}, u32[]{:S(2)}, u32[]{:S(2)}) collective-permute-start(bf16[21,16,128]{2,1,0:T(8,128)(2,1)S(1)} %get-tuple-element.218), channel_id=1, source_target_pairs={{0,16},{2,18},{4,20},{6,22},{8,24},{10,26},{12,28},{14,30},{16,0},... | collective-permute-start | bytes 258056 | tf_op jit(solution)/shard_map/ppermute | solution.py:34
  69.7 1.1 %combine.44 = (bf16[12,16,128]{2,1,0:T(8,128)(2,1)S(1)}, f32[12,16,128]{2,1,0:T(8,128)S(1)}) custom-call(s32[24,64]{1,0:T(8,128)S(1)} %make_plan.1.table, f32[21,16,128]{2,1,0:T(8,128)S(1)} %get-tuple-element.196.kept_in, bf16[21,16,128]{2,1,0:T(8,128)(2,1)S(1)} %collective-permute-done.32.received), custom_call_target="tpu_custom_call" | custom-call | bytes 411648 | tf_op jit(solution)/shard_map/combine/pallas_call | solution.py:20
  70.8 1.1 %combine.45 = (bf16[12,16,128]{2,1,0:T(8,128)(2,1)S(1)}, f32[12,16,128]{2,1,0:T(8,128)S(1)}) custom-call(s32[24,64]{1,0:T(8,128)S(1)} %make_plan.1.table, f32[21,16,128]{2,1,0:T(8,128)S(1)} %get-tuple-element.202.kept_in, bf16[21,16,128]{2,1,0:T(8,128)(2,1)S(1)} %collective-permute-done.37.received), custom_call_target="tpu_custom_call" | custom-call | bytes 411648 | tf_op jit(solution)/shard_map/combine/pallas_call | solution.py:20
  72.0 0.9 %collective-permute-start.38 = (bf16[12,16,128]{2,1,0:T(8,128)(2,1)S(1)}, bf16[12,16,128]{2,1,0:T(8,128)(2,1)S(1)}, u32[]{:S(2)}, u32[]{:S(2)}) collective-permute-start(bf16[12,16,128]{2,1,0:T(8,128)(2,1)S(1)} %get-tuple-element.213), channel_id=1, source_target_pairs={{0,2},{2,0},{4,6},{6,4},{8,10},{10,8},{12,14},{14,12},{16,18},{18,... | collective-permute-start | bytes 147464 | tf_op jit(solution)/shard_map/ppermute | solution.py:34
  72.8 1.2 %collective-permute-start.36 = (bf16[12,16,128]{2,1,0:T(8,128)(2,1)S(1)}, bf16[12,16,128]{2,1,0:T(8,128)(2,1)S(1)}, u32[]{:S(2)}, u32[]{:S(2)}) collective-permute-start(bf16[12,16,128]{2,1,0:T(8,128)(2,1)S(1)} %get-tuple-element.209), channel_id=1, source_target_pairs={{0,2},{2,0},{4,6},{6,4},{8,10},{10,8},{12,14},{14,12},{16,18},{18,... | collective-permute-start | bytes 147464 | tf_op jit(solution)/shard_map/ppermute | solution.py:34
  74.0 1.1 %combine.46 = (bf16[12,16,128]{2,1,0:T(8,128)(2,1)S(1)}, f32[12,16,128]{2,1,0:T(8,128)S(1)}) custom-call(s32[24,64]{1,0:T(8,128)S(1)} %make_plan.1.table, f32[21,16,128]{2,1,0:T(8,128)S(1)} %get-tuple-element.204.kept_in, bf16[21,16,128]{2,1,0:T(8,128)(2,1)S(1)} %collective-permute-done.39.received), custom_call_target="tpu_custom_call" | custom-call | bytes 411648 | tf_op jit(solution)/shard_map/combine/pallas_call | solution.py:20
  75.2 1.1 %combine.47 = (bf16[12,16,128]{2,1,0:T(8,128)(2,1)S(1)}, f32[12,16,128]{2,1,0:T(8,128)S(1)}) custom-call(s32[24,64]{1,0:T(8,128)S(1)} %make_plan.1.table, f32[21,16,128]{2,1,0:T(8,128)S(1)} %get-tuple-element.206.kept_in, bf16[21,16,128]{2,1,0:T(8,128)(2,1)S(1)} %collective-permute-done.41.received), custom_call_target="tpu_custom_call" | custom-call | bytes 411648 | tf_op jit(solution)/shard_map/combine/pallas_call | solution.py:20
  76.3 0.9 %collective-permute-start.42 = (bf16[12,16,128]{2,1,0:T(8,128)(2,1)S(1)}, bf16[12,16,128]{2,1,0:T(8,128)(2,1)S(1)}, u32[]{:S(2)}, u32[]{:S(2)}) collective-permute-start(bf16[12,16,128]{2,1,0:T(8,128)(2,1)S(1)} %get-tuple-element.221), channel_id=1, source_target_pairs={{0,2},{2,0},{4,6},{6,4},{8,10},{10,8},{12,14},{14,12},{16,18},{18,... | collective-permute-start | bytes 147464 | tf_op jit(solution)/shard_map/ppermute | solution.py:34
  77.3 1.1 %collective-permute-start.40 = (bf16[12,16,128]{2,1,0:T(8,128)(2,1)S(1)}, bf16[12,16,128]{2,1,0:T(8,128)(2,1)S(1)}, u32[]{:S(2)}, u32[]{:S(2)}) collective-permute-start(bf16[12,16,128]{2,1,0:T(8,128)(2,1)S(1)} %get-tuple-element.217), channel_id=1, source_target_pairs={{0,2},{2,0},{4,6},{6,4},{8,10},{10,8},{12,14},{14,12},{16,18},{18,... | collective-permute-start | bytes 147464 | tf_op jit(solution)/shard_map/ppermute | solution.py:34
  78.4 2.1 %collective-permute-done.42 = bf16[12,16,128]{2,1,0:T(8,128)(2,1)S(1)} collective-permute-done((bf16[12,16,128]{2,1,0:T(8,128)(2,1)S(1)}, bf16[12,16,128]{2,1,0:T(8,128)(2,1)S(1)}, u32[]{:S(2)}, u32[]{:S(2)}) %collective-permute-start.42) | collective-permute-done | bytes 49184 | tf_op jit(solution)/shard_map/ppermute | solution.py:34
  80.5 0.9 %collective-permute-done.40 = bf16[12,16,128]{2,1,0:T(8,128)(2,1)S(1)} collective-permute-done((bf16[12,16,128]{2,1,0:T(8,128)(2,1)S(1)}, bf16[12,16,128]{2,1,0:T(8,128)(2,1)S(1)}, u32[]{:S(2)}, u32[]{:S(2)}) %collective-permute-start.40) | collective-permute-done | bytes 49184 | tf_op jit(solution)/shard_map/ppermute | solution.py:34
  81.4 1.9 %finish.1 = f32[1,12,128,128]{3,2,1,0:T(8,128)} custom-call(s32[67]{0:T(128)S(1)} %concatenate.12.place, s32[24,64]{1,0:T(8,128)S(1)} %make_plan.1.table, f32[12,16,128]{2,1,0:T(8,128)S(1)} %get-tuple-element.222.refs_0_, bf16[12,16,128]{2,1,0:T(8,128)(2,1)S(1)} %get-tuple-element.223.refs_1_, f32[12,16,128]{2,1,0:T(8,128)S(1)} %get-tuple-element.224.refs_2_, ...), custom_call_target="tpu_custom_call" | custom-call | bytes 1382668 | tf_op jit(solution)/shard_map/finish/pallas_call | solution.py:20
  (37 shorter events, 0.2 us)
Async XLA Ops:
  0.0 6.9 %collective-permute-start.23 = (bf16[1,128,4096]{2,1,0:T(8,128)(2,1)}, bf16[1,128,4096]{2,1,0:T(8,128)(2,1)S(1)}, u32[]{:S(2)}, u32[]{:S(2)}) collective-permute-start(bf16[1,128,4096]{2,1,0:T(8,128)(2,1)} %bitcast.8), channel_id=1, source_target_pairs={{0,1},{1,0},{2,3},{3,2},{4,5},{5,4},{6,7},{7,6},{8,9},{9,8},{10,11... | collective-permute-start | bytes 3145736 | tf_op jit(solution)/shard_map/tokens/ppermute | solution.py:34
  1.2 1.2 %copy-start.1 = (bf16[128,4096]{1,0:T(8,128)(2,1)S(1)}, bf16[128,4096]{1,0:T(8,128)(2,1)}, u32[]{:S(2)}) copy-start(bf16[128,4096]{1,0:T(8,128)(2,1)} %param.9) | copy-start | bytes 3145732
  2.4 0.9 %copy-start.2 = (f32[1,4,128,128]{3,2,1,0:T(8,128)S(1)}, f32[1,4,128,128]{3,2,1,0:T(8,128)}, u32[]{:S(2)}) copy-start(f32[1,4,128,128]{3,2,1,0:T(8,128)} %masters) | copy-start | bytes 786436
  3.4 9.2 %copy-start = (bf16[128,14336]{1,0:T(8,128)(2,1)S(1)}, bf16[128,14336]{1,0:T(8,128)(2,1)}, u32[]{:S(2)}) copy-start(bf16[128,14336]{1,0:T(8,128)(2,1)} %grad.1) | copy-start | bytes 11010052
  4.3 5.3 %collective-permute-start.16 = (bf16[4,64,128]{2,1,0:T(8,128)(2,1)S(1)}, bf16[4,64,128]{2,1,0:T(8,128)(2,1)S(1)}, u32[]{:S(2)}, u32[]{:S(2)}) collective-permute-start(bf16[4,64,128]{2,1,0:T(8,128)(2,1)S(1)} %get-tuple-element.159), channel_id=1, source_target_pairs={{0,2},{2,0},{4,6},{6,4},{8,10},{10,8},{12,14},{14,12},{16,18},{18,... | collective-permute-start | bytes 196616 | tf_op jit(solution)/shard_map/weights/ppermute | solution.py:34
  7.8 8.4 %copy-start.3 = (s32[1,32]{1,0:T(1,128)S(1)}, s32[1,32]{1,0:T(1,128)}, u32[]{:S(2)}) copy-start(s32[1,32]{1,0:T(1,128)} %columns.1) | copy-start | bytes 388
  7.8 8.4 %copy-start.4 = (s32[2,64]{1,0:T(2,128)S(1)}, s32[2,64]{1,0:T(2,128)}, u32[]{:S(2)}) copy-start(s32[2,64]{1,0:T(2,128)} %constant.16.clone.found) | copy-start | bytes 1540
  7.8 8.4 %copy-start.5 = (s32[1,64]{1,0:T(1,128)S(1)}, s32[1,64]{1,0:T(1,128)}, u32[]{:S(2)}) copy-start(s32[1,64]{1,0:T(1,128)} %owners.1) | copy-start | bytes 772
  7.8 27.2 %collective-permute-start.24 = (bf16[32,128,128]{2,1,0:T(8,128)(2,1)S(1)}, bf16[32,128,128]{2,1,0:T(8,128)(2,1)S(1)}, u32[]{:S(2)}, u32[]{:S(2)}) collective-permute-start(bf16[32,128,128]{2,1,0:T(8,128)(2,1)S(1)} %select_rows.3.refs_4_), channel_id=1, source_target_pairs={{0,2},{2,0},{4,6},{6,4},{8,10},{10,8},{12,14},{14,12},{16,18},{18,... | collective-permute-start | bytes 3145736 | tf_op jit(solution)/shard_map/weights/ppermute | solution.py:34
  9.7 9.1 %collective-permute-start.17 = (bf16[8,64,128]{2,1,0:T(8,128)(2,1)S(1)}, bf16[8,64,128]{2,1,0:T(8,128)(2,1)S(1)}, u32[]{:S(2)}, u32[]{:S(2)}) collective-permute-start(bf16[8,64,128]{2,1,0:T(8,128)(2,1)S(1)} %constant_dynamic-update-slice_fusion), channel_id=1, source_target_pairs={{0,16},{2,18},{4,20},{6,22},{8,24},{10,26},{12,28},{14,30},{16,0},... | collective-permute-start | bytes 393224 | tf_op jit(solution)/shard_map/weights/ppermute | solution.py:34
  18.8 5.0 %collective-permute-start.18 = (bf16[8,64,128]{2,1,0:T(8,128)(2,1)S(1)}, bf16[8,64,128]{2,1,0:T(8,128)(2,1)S(1)}, u32[]{:S(2)}, u32[]{:S(2)}) collective-permute-start(bf16[8,64,128]{2,1,0:T(8,128)(2,1)S(1)} %constant_dynamic-update-slice_fusion), channel_id=1, source_target_pairs={{0,4},{2,6},{4,0},{6,2},{8,12},{10,14},{12,8},{14,10},{16,20},{18,... | collective-permute-start | bytes 393224 | tf_op jit(solution)/shard_map/weights/ppermute | solution.py:34
  20.3 5.0 %collective-permute-start.19 = (bf16[8,64,128]{2,1,0:T(8,128)(2,1)S(1)}, bf16[8,64,128]{2,1,0:T(8,128)(2,1)S(1)}, u32[]{:S(2)}, u32[]{:S(2)}) collective-permute-start(bf16[8,64,128]{2,1,0:T(8,128)(2,1)S(1)} %collective-permute-done.17), channel_id=1, source_target_pairs={{0,8},{2,10},{4,12},{6,14},{8,0},{10,2},{12,4},{14,6},{16,24},{18,... | collective-permute-start | bytes 393224 | tf_op jit(solution)/shard_map/weights/ppermute | solution.py:34
  25.3 6.7 %collective-permute-start.21 = (bf16[16,64,128]{2,1,0:T(8,128)(2,1)S(1)}, bf16[16,64,128]{2,1,0:T(8,128)(2,1)S(1)}, u32[]{:S(2)}, u32[]{:S(2)}) collective-permute-start(bf16[16,64,128]{2,1,0:T(8,128)(2,1)S(1)} %constant_dynamic-update-slice_fusion.4.refs_2_), channel_id=1, source_target_pairs={{0,4},{2,6},{4,0},{6,2},{8,12},{10,14},{12,8},{14,10},{16,20},{18,... | collective-permute-start | bytes 786440 | tf_op jit(solution)/shard_map/weights/ppermute | solution.py:34
  25.9 6.4 %collective-permute-start.20 = (bf16[16,64,128]{2,1,0:T(8,128)(2,1)S(1)}, bf16[16,64,128]{2,1,0:T(8,128)(2,1)S(1)}, u32[]{:S(2)}, u32[]{:S(2)}) collective-permute-start(bf16[16,64,128]{2,1,0:T(8,128)(2,1)S(1)} %constant_dynamic-update-slice_fusion.2.refs_0_), channel_id=1, source_target_pairs={{0,8},{2,10},{4,12},{6,14},{8,0},{10,2},{12,4},{14,6},{16,24},{18,... | collective-permute-start | bytes 786440 | tf_op jit(solution)/shard_map/weights/ppermute | solution.py:34
  26.8 12.7 %collective-permute-start.25 = (bf16[32,32,128]{2,1,0:T(8,128)(2,1)S(1)}, bf16[32,32,128]{2,1,0:T(8,128)(2,1)S(1)}, u32[]{:S(2)}, u32[]{:S(2)}) collective-permute-start(bf16[32,32,128]{2,1,0:T(8,128)(2,1)S(1)} %get-tuple-element.174), channel_id=1, source_target_pairs={{0,2},{2,0},{4,6},{6,4},{8,10},{10,8},{12,14},{14,12},{16,18},{18,... | collective-permute-start | bytes 786440 | tf_op jit(solution)/shard_map/upstream/ppermute | solution.py:34
  28.8 1.4 %collective-permute-start.22 = (s32[1]{0:T(128)}, s32[1]{0:T(128)}, u32[]{:S(2)}, u32[]{:S(2)}) collective-permute-start(s32[1]{0:T(128)} %bitcast.6), channel_id=1, source_target_pairs={{0,1},{1,0},{2,3},{3,2},{4,5},{5,4},{6,7},{7,6},{8,9},{9,8},{10,11... | collective-permute-start | bytes 20 | tf_op jit(solution)/shard_map/plan/ppermute | solution.py:34
  30.2 14.2 %collective-permute-start.26 = (bf16[32,32,128]{2,1,0:T(8,128)(2,1)S(1)}, bf16[32,32,128]{2,1,0:T(8,128)(2,1)S(1)}, u32[]{:S(2)}, u32[]{:S(2)}) collective-permute-start(bf16[32,32,128]{2,1,0:T(8,128)(2,1)S(1)} %get-tuple-element.176), channel_id=1, source_target_pairs={{0,2},{2,0},{4,6},{6,4},{8,10},{10,8},{12,14},{14,12},{16,18},{18,... | collective-permute-start | bytes 786440 | tf_op jit(solution)/shard_map/upstream/ppermute | solution.py:34
  40.8 8.1 %collective-permute-start.27 = (bf16[45,16,128]{2,1,0:T(8,128)(2,1)S(1)}, bf16[45,16,128]{2,1,0:T(8,128)(2,1)S(1)}, u32[]{:S(2)}, u32[]{:S(2)}) collective-permute-start(bf16[45,16,128]{2,1,0:T(8,128)(2,1)S(1)} %get-tuple-element.178), channel_id=1, source_target_pairs={{0,4},{2,6},{4,0},{6,2},{8,12},{10,14},{12,8},{14,10},{16,20},{18,... | collective-permute-start | bytes 552968 | tf_op jit(solution)/shard_map/ppermute | solution.py:34
  42.4 7.9 %collective-permute-start.31 = (bf16[45,16,128]{2,1,0:T(8,128)(2,1)S(1)}, bf16[45,16,128]{2,1,0:T(8,128)(2,1)S(1)}, u32[]{:S(2)}, u32[]{:S(2)}) collective-permute-start(bf16[45,16,128]{2,1,0:T(8,128)(2,1)S(1)} %get-tuple-element.188), channel_id=1, source_target_pairs={{0,8},{2,10},{4,12},{6,14},{8,0},{10,2},{12,4},{14,6},{16,24},{18,... | collective-permute-start | bytes 552968 | tf_op jit(solution)/shard_map/ppermute | solution.py:34
  45.7 6.0 %collective-permute-start.30 = (bf16[45,16,128]{2,1,0:T(8,128)(2,1)S(1)}, bf16[45,16,128]{2,1,0:T(8,128)(2,1)S(1)}, u32[]{:S(2)}, u32[]{:S(2)}) collective-permute-start(bf16[45,16,128]{2,1,0:T(8,128)(2,1)S(1)} %get-tuple-element.186), channel_id=1, source_target_pairs={{0,4},{2,6},{4,0},{6,2},{8,12},{10,14},{12,8},{14,10},{16,20},{18,... | collective-permute-start | bytes 552968 | tf_op jit(solution)/shard_map/ppermute | solution.py:34
  47.3 7.9 %collective-permute-start.29 = (bf16[45,16,128]{2,1,0:T(8,128)(2,1)S(1)}, bf16[45,16,128]{2,1,0:T(8,128)(2,1)S(1)}, u32[]{:S(2)}, u32[]{:S(2)}) collective-permute-start(bf16[45,16,128]{2,1,0:T(8,128)(2,1)S(1)} %get-tuple-element.185), channel_id=1, source_target_pairs={{0,8},{2,10},{4,12},{6,14},{8,0},{10,2},{12,4},{14,6},{16,24},{18,... | collective-permute-start | bytes 552968 | tf_op jit(solution)/shard_map/ppermute | solution.py:34
  49.8 8.3 %collective-permute-start.28 = (bf16[29,16,128]{2,1,0:T(8,128)(2,1)S(1)}, bf16[29,16,128]{2,1,0:T(8,128)(2,1)S(1)}, u32[]{:S(2)}, u32[]{:S(2)}) collective-permute-start(bf16[29,16,128]{2,1,0:T(8,128)(2,1)S(1)} %get-tuple-element.183), channel_id=1, source_target_pairs={{0,8},{2,10},{4,12},{6,14},{8,0},{10,2},{12,4},{14,6},{16,24},{18,... | collective-permute-start | bytes 356360 | tf_op jit(solution)/shard_map/ppermute | solution.py:34
  51.1 9.1 %collective-permute-start.35 = (bf16[29,16,128]{2,1,0:T(8,128)(2,1)S(1)}, bf16[29,16,128]{2,1,0:T(8,128)(2,1)S(1)}, u32[]{:S(2)}, u32[]{:S(2)}) collective-permute-start(bf16[29,16,128]{2,1,0:T(8,128)(2,1)S(1)} %get-tuple-element.200), channel_id=1, source_target_pairs={{0,4},{2,6},{4,0},{6,2},{8,12},{10,14},{12,8},{14,10},{16,20},{18,... | collective-permute-start | bytes 356360 | tf_op jit(solution)/shard_map/ppermute | solution.py:34
  52.6 10.1 %collective-permute-start.34 = (bf16[29,16,128]{2,1,0:T(8,128)(2,1)S(1)}, bf16[29,16,128]{2,1,0:T(8,128)(2,1)S(1)}, u32[]{:S(2)}, u32[]{:S(2)}) collective-permute-start(bf16[29,16,128]{2,1,0:T(8,128)(2,1)S(1)} %get-tuple-element.199), channel_id=1, source_target_pairs={{0,16},{2,18},{4,20},{6,22},{8,24},{10,26},{12,28},{14,30},{16,0},... | collective-permute-start | bytes 356360 | tf_op jit(solution)/shard_map/ppermute | solution.py:34
  56.1 9.1 %collective-permute-start.33 = (bf16[29,16,128]{2,1,0:T(8,128)(2,1)S(1)}, bf16[29,16,128]{2,1,0:T(8,128)(2,1)S(1)}, u32[]{:S(2)}, u32[]{:S(2)}) collective-permute-start(bf16[29,16,128]{2,1,0:T(8,128)(2,1)S(1)} %get-tuple-element.198), channel_id=1, source_target_pairs={{0,4},{2,6},{4,0},{6,2},{8,12},{10,14},{12,8},{14,10},{16,20},{18,... | collective-permute-start | bytes 356360 | tf_op jit(solution)/shard_map/ppermute | solution.py:34
  58.9 10.8 %collective-permute-start.32 = (bf16[21,16,128]{2,1,0:T(8,128)(2,1)S(1)}, bf16[21,16,128]{2,1,0:T(8,128)(2,1)S(1)}, u32[]{:S(2)}, u32[]{:S(2)}) collective-permute-start(bf16[21,16,128]{2,1,0:T(8,128)(2,1)S(1)} %get-tuple-element.197), channel_id=1, source_target_pairs={{0,16},{2,18},{4,20},{6,22},{8,24},{10,26},{12,28},{14,30},{16,0},... | collective-permute-start | bytes 258056 | tf_op jit(solution)/shard_map/ppermute | solution.py:34
  61.1 9.7 %collective-permute-start.37 = (bf16[21,16,128]{2,1,0:T(8,128)(2,1)S(1)}, bf16[21,16,128]{2,1,0:T(8,128)(2,1)S(1)}, u32[]{:S(2)}, u32[]{:S(2)}) collective-permute-start(bf16[21,16,128]{2,1,0:T(8,128)(2,1)S(1)} %get-tuple-element.210), channel_id=1, source_target_pairs={{0,16},{2,18},{4,20},{6,22},{8,24},{10,26},{12,28},{14,30},{16,0},... | collective-permute-start | bytes 258056 | tf_op jit(solution)/shard_map/ppermute | solution.py:34
  63.6 10.5 %collective-permute-start.39 = (bf16[21,16,128]{2,1,0:T(8,128)(2,1)S(1)}, bf16[21,16,128]{2,1,0:T(8,128)(2,1)S(1)}, u32[]{:S(2)}, u32[]{:S(2)}) collective-permute-start(bf16[21,16,128]{2,1,0:T(8,128)(2,1)S(1)} %get-tuple-element.214), channel_id=1, source_target_pairs={{0,8},{2,10},{4,12},{6,14},{8,0},{10,2},{12,4},{14,6},{16,24},{18,... | collective-permute-start | bytes 258056 | tf_op jit(solution)/shard_map/ppermute | solution.py:34
  66.0 9.2 %collective-permute-start.41 = (bf16[21,16,128]{2,1,0:T(8,128)(2,1)S(1)}, bf16[21,16,128]{2,1,0:T(8,128)(2,1)S(1)}, u32[]{:S(2)}, u32[]{:S(2)}) collective-permute-start(bf16[21,16,128]{2,1,0:T(8,128)(2,1)S(1)} %get-tuple-element.218), channel_id=1, source_target_pairs={{0,16},{2,18},{4,20},{6,22},{8,24},{10,26},{12,28},{14,30},{16,0},... | collective-permute-start | bytes 258056 | tf_op jit(solution)/shard_map/ppermute | solution.py:34
  72.0 6.5 %collective-permute-start.38 = (bf16[12,16,128]{2,1,0:T(8,128)(2,1)S(1)}, bf16[12,16,128]{2,1,0:T(8,128)(2,1)S(1)}, u32[]{:S(2)}, u32[]{:S(2)}) collective-permute-start(bf16[12,16,128]{2,1,0:T(8,128)(2,1)S(1)} %get-tuple-element.213), channel_id=1, source_target_pairs={{0,2},{2,0},{4,6},{6,4},{8,10},{10,8},{12,14},{14,12},{16,18},{18,... | collective-permute-start | bytes 147464 | tf_op jit(solution)/shard_map/ppermute | solution.py:34
  72.8 5.6 %collective-permute-start.36 = (bf16[12,16,128]{2,1,0:T(8,128)(2,1)S(1)}, bf16[12,16,128]{2,1,0:T(8,128)(2,1)S(1)}, u32[]{:S(2)}, u32[]{:S(2)}) collective-permute-start(bf16[12,16,128]{2,1,0:T(8,128)(2,1)S(1)} %get-tuple-element.209), channel_id=1, source_target_pairs={{0,2},{2,0},{4,6},{6,4},{8,10},{10,8},{12,14},{14,12},{16,18},{18,... | collective-permute-start | bytes 147464 | tf_op jit(solution)/shard_map/ppermute | solution.py:34
  76.3 4.2 %collective-permute-start.42 = (bf16[12,16,128]{2,1,0:T(8,128)(2,1)S(1)}, bf16[12,16,128]{2,1,0:T(8,128)(2,1)S(1)}, u32[]{:S(2)}, u32[]{:S(2)}) collective-permute-start(bf16[12,16,128]{2,1,0:T(8,128)(2,1)S(1)} %get-tuple-element.221), channel_id=1, source_target_pairs={{0,2},{2,0},{4,6},{6,4},{8,10},{10,8},{12,14},{14,12},{16,18},{18,... | collective-permute-start | bytes 147464 | tf_op jit(solution)/shard_map/ppermute | solution.py:34
  77.3 4.1 %collective-permute-start.40 = (bf16[12,16,128]{2,1,0:T(8,128)(2,1)S(1)}, bf16[12,16,128]{2,1,0:T(8,128)(2,1)S(1)}, u32[]{:S(2)}, u32[]{:S(2)}) collective-permute-start(bf16[12,16,128]{2,1,0:T(8,128)(2,1)S(1)} %get-tuple-element.217), channel_id=1, source_target_pairs={{0,2},{2,0},{4,6},{6,4},{8,10},{10,8},{12,14},{14,12},{16,18},{18,... | collective-permute-start | bytes 147464 | tf_op jit(solution)/shard_map/ppermute | solution.py:34

commit v4 on v3

--- a/solution.py
+++ b/solution.py
@@ -42,20 +42,12 @@
     return parts
 
 
-def split_masters(place, masters, kept, sent):
-    half = kept.shape[1]
+def split_masters(masters, tokens, low, high):
+    del tokens
+    half = low.shape[1]
     for block in range(masters.shape[1]):
         turned = masters[0, block].T.astype(BF16)
-
-        @pl.when(place[0] == 0)
-        def _():
-            kept[block] = turned[:half]
-            sent[block] = turned[half:]
-
-        @pl.when(place[0] != 0)
-        def _():
-            kept[block] = turned[half:]
-            sent[block] = turned[:half]
+        low[block], high[block] = turned[:half], turned[half:]
 
 
 def split_upstream(place, grad, kept, *refs):
@@ -82,7 +74,7 @@
 
 
 def select_rows(first, place, *refs):
-    sources, before, chosen = refs[: 1 if first == 0 else -2], refs[-2], refs[-1]
+    sources, before, chosen = refs[:-1], None, refs[-1]
     side = chosen.shape[2]
     per_shard = sources[0].shape[2] // side
     for k in range(chosen.shape[0]):
@@ -149,8 +141,12 @@
         slope[k, :half], slope[k, half:] = slopes(total[first, :half], total[first, half:])
 
 
-def other_part(rows, names, start, table, slope, other_tokens, other_up, grad, *refs):
-    outs, total = refs[:-1], refs[-1]
+def scalar(table, row):
+    return jnp.max(table[pl.ds(row, 1), :].astype(F32)).astype(jnp.int32)
+
+
+def other_part(rows, steps, start, table, slope, other_tokens, other_up, grad, *refs):
+    outs, total, ordered = refs[: 2 * len(steps)], refs[2 * len(steps)], refs[2 * len(steps) + 1 :]
     places, height, half = other_up.shape[0], other_up.shape[1], grad.shape[1] // 2
     gate, up = pl.ds(start, height), pl.ds(half + start, height)
     for k in range(places):
@@ -158,47 +154,30 @@
         total[k, :height] = grad[k, gate] + result[:height]
         total[k, height:] = grad[k, up] + result[height:]
     first = 0
-    for n, name in enumerate(names):
+    for n, (order, step) in enumerate(steps):
         sent, kept = outs[2 * n], outs[2 * n + 1]
         room, size = sent.shape[0], sent.shape[1]
         for block in range(2 * places):
             which, k = divmod(block, places)
-            value = total[k, pl.ds(which * height + first, size), :]
-            sent[jnp.minimum(table[rows[name, "sent"], block], room - 1)] = value.astype(BF16)
-            kept[jnp.minimum(table[rows[name, "kept"], block], room - 1)] = value
+            ordered[n][table[rows[order, "at"], block]] = total[k, pl.ds(which * height + first, size), :]
+        sent[...] = ordered[n][pl.ds(table[rows[step, "sent"], 0], room)].astype(BF16)
+        kept[...] = ordered[n][pl.ds(table[rows[step, "kept"], 0], room)]
         first += size
 
 
-def combine(sent_row, kept_row, table, kept_in, received, sent, kept):
-    room = sent.shape[0]
-    for r in range(kept_in.shape[0] - 1):
-        value = kept_in[r] + received[r].astype(F32)
-        sent[jnp.minimum(table[sent_row, r], room - 1)] = value.astype(BF16)
-        kept[jnp.minimum(table[kept_row, r], room - 1)] = value
-
-
-def combine_last(sent_row, kept_row, count_row, table, kept_in, received, sent, kept):
-    def step(r, _):
-        value = kept_in[r] + received[r].astype(F32)
-        away = table[sent_row, r]
-
-        @pl.when(away >= 0)
-        def _():
-            sent[jnp.minimum(away, sent.shape[0] - 1)] = value.astype(BF16)
-
-        @pl.when(away < 0)
-        def _():
-            kept[jnp.minimum(table[kept_row, r], kept.shape[0] - 1)] = value
-
-        return 0
-
-    lax.fori_loop(0, jnp.minimum(table[count_row, 0], kept_in.shape[0]), step, 0)
-
-
-def finish(count_row, place, table, *refs):
+def combine(sent_row, kept_row, pieces, table, *refs):
+    kept_in, received, (sent, kept, total) = refs[:pieces], refs[pieces : 2 * pieces], refs[2 * pieces :]
+    count, room, start = kept_in[0].shape[0], sent.shape[0], 0
+    for mine, other in zip(kept_in, received):
+        total[:count, start : start + mine.shape[1]] = mine[...] + other[...].astype(F32)
+        start += mine.shape[1]
+    sent[...] = total[pl.ds(jnp.minimum(scalar(table, sent_row), count), room)].astype(BF16)
+    kept[...] = total[pl.ds(jnp.minimum(scalar(table, kept_row), count), room)]
+
+
+def finish(count_row, pair_row, table, *refs):
     ends, out = refs[:-1], refs[-1]
-    count = table[count_row, 0]
-    swapped = place[0] != 0
+    count, swapped = scalar(table, count_row), scalar(table, pair_row) != 0
     for slot in range(out.shape[1]):
         mine = jnp.concatenate([end[slot] for end in ends[0::2]], axis=0)
         other = jnp.concatenate([end[slot] for end in ends[1::2]], axis=0).astype(F32)
@@ -211,27 +190,25 @@
     bits = owner_count.bit_length() - 1
     if bits == 4:
         y, near, far = 1, 2, 3
-        parts = ((1, (y, near, far)), (1, (near, y, far))), ((1, (y, far, near)), (1, (near, y, far)))
-        turns = tuple((part, 0) for part in range(2)) + tuple((piece, n) for n in range(1, 4) for piece in range(4))
+        parts = ((1, (near, y, far)), (1, (y, far, near))), ((1, (y, near, far)), (1, (near, far, y)))
+        turns = tuple(((part,), 0) for part in range(2)) + tuple(((piece,), n) for n in range(1, 4) for piece in range(4))
         return 0, (y, near), (far,), parts, turns
     pair, ends, rest = bits - 2, (0, bits - 1), tuple(range(1, bits - 2))
     parts = ((2, (*ends, *rest)),), ((2, (*ends[::-1], *rest)),)
-    return pair, ends, rest, parts, tuple((piece, n) for n in range(bits) for piece in range(2))
+    return pair, ends, rest, parts, tuple(((piece,), n) for n in range(bits) for piece in range(2))
+
+
+def orders_of(axes):
+    return list(dict.fromkeys((*order, axes[0]) for part in axes[3] for _, order in part))
 
 
 def steps_of(axes):
-    pair, _, _, parts, _ = axes
-    steps = {}
-    for part in parts:
-        for _, order in part:
-            order = (*order, pair)
-            for n, bit in enumerate(order):
-                steps[tuple(sorted(order[:n])), bit] = None
-    return list(steps)
+    return list(dict.fromkeys((tuple(sorted(o[:n])), bit) for o in orders_of(axes) for n, bit in enumerate(o)))
 
 
 def rows_of(axes):
-    names = ["order", "first", "last", "end", "fits"]
+    names = ["order", "first", "end", "pair", "fits"]
+    names += [(order, "at") for order in orders_of(axes)]
     names += [(step, kind) for step in steps_of(axes) for kind in ("sent", "kept")]
     return {name: n for n, name in enumerate(names)}
 
@@ -249,59 +226,47 @@
         kept = jnp.where((across == down)[:size, :size], row.astype(F32), 0.0)
         return jnp.sum(kept, axis=1, keepdims=True).astype(jnp.int32)
 
-    owner_col, column_col = as_column(owner_row), as_column(column_row)
-    before = across < down
-    differs_row, differs_col = owner_row ^ me, owner_col ^ me
-
-    def alive(differs, done):
-        return (differs & sum(1 << b for b in done)) == 0
-
     def number(mask):
         return jnp.where(mask, 1.0, 0.0)
 
-    def rank(mask_row):
-        return jnp.sum(jnp.where(before, number(mask_row), 0.0), axis=1, keepdims=True)
-
-    def turned(column):
-        return jnp.sum(jnp.where(across == down, column, 0.0), axis=0, keepdims=True)
-
     def write(name, row):
-        table[pl.ds(rows[name], 1), :] = row.astype(jnp.int32)
-
-    def going(done, bit):
-        live, away = alive(differs_row, done), ((differs_row >> bit) & 1) == 1
-        return rank(jnp.logical_and(live, away)), rank(jnp.logical_and(live, jnp.logical_not(away)))
-
+        table[pl.ds(rows[name], 1), :] = jnp.broadcast_to(row, (1, count)).astype(jnp.int32)
+
+    owner_col, column_col = as_column(owner_row), as_column(column_row)
     table[...] = jnp.zeros(table.shape, jnp.int32)
-    table[pl.ds(rows["order"], 1), :] = (found[0:1, :] ^ me) * own_blocks + found[1:2, :]
+    write("order", (found[0:1, :] ^ me) * own_blocks + found[1:2, :])
     same = column_row == column_col
     place_at = lax.broadcasted_iota(jnp.int32, (places, places), 0).astype(F32)
     first = jnp.min(jnp.where(same, place_at, float(places)), axis=0, keepdims=True)
     table[pl.ds(rows["first"], 1), :places] = first.astype(jnp.int32)
-    full, at_most, everything = float(count), None, ()
+    write("pair", jnp.full((1, 1), (me >> pair) & 1, jnp.int32))
+    for order in orders_of(axes):
+
+        def key(owner):
+            return sum(((owner >> bit) & 1) << n for n, bit in enumerate(order[::-1]))
+
+        ahead = key(owner_col) < key(owner_row)
+        ahead = jnp.logical_or(ahead, jnp.logical_and(key(owner_col) == key(owner_row), down < across))
+        write((order, "at"), jnp.sum(number(ahead), axis=0, keepdims=True))
+
+    def alive(done):
+        return ((owner_row ^ me) & sum(1 << b for b in done)) == 0
+
     for step in steps_of(axes):
         done, bit = step
-        sent, kept = going(done, bit)
-        if not done:
-            write((step, "sent"), turned(sent))
-            write((step, "kept"), turned(kept))
-            continue
-        live = rank(alive(differs_row, done))
-        hit = jnp.logical_and(alive(differs_col, done), live == across.astype(F32))
-        if bit == pair:
-            sent, everything = jnp.where(((differs_col >> bit) & 1) == 1, sent, -1.0), done
-        for kind, values in (("sent", sent), ("kept", kept)):
-            write((step, kind), full + jnp.sum(jnp.where(hit, values - full, 0.0), axis=0, keepdims=True))
+        low = jnp.logical_and(alive(done), ((owner_row >> bit) & 1) == 0)
+        total, mine = jnp.sum(number(low), axis=1, keepdims=True), ((me >> bit) & 1).astype(F32)
+        write((step, "sent"), total * (1.0 - mine))
+        write((step, "kept"), total * mine)
+    everything = alive((*axes[1], *axes[2], pair))
+    write("end", jnp.sum(number(everything), axis=1, keepdims=True))
+    over = jnp.zeros((1, 1), F32)
     for done, most in usual.items():
         mask = sum(1 << b for b in done)
         group = (owner_row & mask) == (owner_col & mask)
-        over = jnp.max(jnp.sum(number(group), axis=1, keepdims=True), axis=0, keepdims=True) - most
-        at_most = over if at_most is None else jnp.maximum(at_most, over)
-    for name, done in (("last", everything), ("end", (*everything, pair))):
-        total = jnp.sum(number(alive(differs_row, done)), axis=1, keepdims=True)
-        write(name, jnp.broadcast_to(total, (1, count)))
-    fits = jnp.zeros((1, 1), F32) if at_most is None else at_most
-    write("fits", jnp.broadcast_to(number(fits <= 0.0), (1, count)))
+        taken = jnp.max(jnp.sum(number(group), axis=1, keepdims=True), axis=0, keepdims=True)
+        over = jnp.maximum(over, taken - most)
+    write("fits", number(over <= 0.0))
 
 
 def local(tokens, hidden_grad, masters, block_row, block_col, owners):
@@ -321,21 +286,17 @@
         return jax.ShapeDtypeStruct(shape, dtype)
 
     with jax.named_scope("tokens"):
-        shape = [struct((places, token_count, side), BF16)]
-        near = call(functools.partial(select_rows, 0), "select_rows", shape, [SMEM, VMEM], [place, tokens[None]])[0]
-        first_chosen, others = near, spread(tokens)[1:]
-        if others:
-            near = call(
-                functools.partial(select_rows, 1), "select_rows", shape, [SMEM] + [VMEM] * (len(others) + 1),
-                [place, *others, near],
-            )[0]
-        own_chosen = near
-        masters, _ = lax.optimization_barrier((masters, first_chosen))
+        own_chosen = call(
+            functools.partial(select_rows, 0), "select_rows", [struct((places, token_count, side), BF16)],
+            [SMEM] + [VMEM] * lax.axis_size("tensor").bit_length(), [place, *spread(tokens)],
+        )[0]
 
     with jax.named_scope("weights"):
-        kept, sent = call(
-            split_masters, "split_masters", [struct((own_blocks, half, side), BF16)] * 2, [SMEM, VMEM], [place, masters]
+        low, high = call(
+            split_masters, "split_masters", [struct((own_blocks, half, side), BF16)] * 2, [VMEM] * 2, [masters, tokens]
         )
+        upper = ((me >> pair) & 1) == 1
+        kept, sent = jnp.where(upper, high, low), jnp.where(upper, low, high)
         entries = [(0, b) for b in range(own_blocks)]
 
         def moved(found, bit):
@@ -408,29 +369,31 @@
         )[0]
 
     def reduce(load, table, slope, other_chosen, other_up, grad):
-        held, got, orders, firsts, start = [], [], [], [], 0
+        orders, firsts, start = [], [], 0
         for part in parts:
             firsts.append((len(orders), start))
             orders += [(*order, pair) for _, order in part]
             start += sum(share for share, _ in part) * quarter
-        turn = None
-        for at, n in turns:
+        state, turn = {}, None
+        for group, n in turns:
+            order = orders[group[0]]
             if n == 0:
+                (at,) = group
                 part, up, (piece, start) = parts[at], other_up[at], firsts[at]
-                steps = [((), order[0]) for _, order in part]
-                shapes = [(load(step[1:]) + 1, share * quarter, side) for step, (share, _) in zip(steps, part)]
+                steps = [((*order, pair), ((), order[0])) for _, order in part]
+                shapes = [(load(order[:1]), share * quarter, side) for share, order in part]
                 body, spec = functools.partial(other_part, rows, steps, start), [SMEM] + [VMEM] * 4
                 args, scratch = [table, slope, other_chosen, up, grad], [pltpu.VMEM((places, 2 * up.shape[1], side), F32)]
+                scratch += [pltpu.VMEM((block_count + room, *rest_of), F32) for room, *rest_of in shapes]
+                made = [(piece + i,) for i in range(len(part))]
             else:
-                piece, order = at, orders[at]
+                joined = [state.pop(key) for key in sorted(state) if set(key) <= set(group)]
                 step = tuple(sorted(order[:n])), order[n]
-                where = rows[step, "sent"], rows[step, "kept"]
-                if order[n] == pair:
-                    body, room = functools.partial(combine_last, *where, rows["last"]), capacity
-                else:
-                    body, room = functools.partial(combine, *where), load(order[: n + 1]) + 1
-                shapes = [(room, *held[piece].shape[1:])]
-                spec, args, scratch = [SMEM] + [VMEM] * 2, [table, held[piece], got[piece]], []
+                body = functools.partial(combine, rows[step, "sent"], rows[step, "kept"], len(joined))
+                room, was, height = load(order[: n + 1]), joined[0][0].shape[0], sum(k.shape[1] for k, _ in joined)
+                shapes, spec = [(room, height, side)], [VMEM] * (1 + 2 * len(joined))
+                args = [table, *(k for k, _ in joined), *(g for _, g in joined)]
+                scratch, made = [pltpu.VMEM((was + room, height, side), F32)], [group]
             if turn is not None:
                 args[-1], _ = lax.optimization_barrier((args[-1], turn))
             outs = call(
@@ -438,18 +401,16 @@
                 spec, args, 0 if n else work // 4, scratch,
             )
             turn = outs[1]
-            if n == 0:
-                held, got = held + [None] * len(part), got + [None] * len(part)
-            for i, (sent, kept) in enumerate(zip(outs[0::2], outs[1::2])):
-                held[piece + i], got[piece + i] = kept, swap(sent, "dp", orders[piece + i][n])
-        return [end for both in zip(held, got) for end in both]
+            for key, sent, kept in zip(made, outs[0::2], outs[1::2]):
+                state[key] = kept, swap(sent, "dp", orders[key[0]][n])
+        return [end for key in sorted(state) for end in state[key]]
 
     operands = (table, slope, other_chosen, other_up, grad)
     ends = reduce(load_of, *operands)
     ends = lax.cond(fits[0] == 1, lambda ends, operands: ends, lambda ends, operands: reduce(most_of, *operands), ends, operands)
     return call(
-        functools.partial(finish, rows["end"]), "finish", [struct((1, capacity, side, side), F32)],
-        [SMEM, SMEM] + [VMEM] * len(ends), [place, table, *ends],
+        functools.partial(finish, rows["end"], rows["pair"]), "finish", [struct((1, capacity, side, side), F32)],
+        [VMEM] * (1 + len(ends)), [table, *ends],
     )[0]
 
 

time: 83.8 us -> 77.1 us (0.920)
  Pallas kernels: 27.7 us -> 16.5 us
  local copies, waits for them, and re-layouts: 2.7 us -> 5.57 us
  starting transfers between devices: 36.2 us -> 38.2 us
    pallas_call x22 -> x21, Pallas kernels: 27.7 us -> 16.5 us  [call(): pl.pallas_call(body, name=name, out_shape=tuple(outs), in_specs=in_specs,...]
    unnamed x15 -> x16, local copies, waits for them, and re-layouts: 1.37 us -> 4.25 us
    ppermute x27, starting transfers between devices: 36.2 us -> 38.2 us  [swap(): return lax.ppermute(value, axis, [(i, i ^ 1 << bit) for i in range(size)])]
  transfers between devices with their start and end apart: 27 -> 27, of which waited for: 10 -> 13; matrix products, arithmetic and copies ran while one was open for 2% -> 2% of each run, Pallas kernels for 31% -> 20%
where the time goes in v4:
time: 77.1 us; the launch traced here: 76.9 us
  starting transfers between devices  38.2 us (50%)
  Pallas kernels  16.5 us (21%)
  waiting for transfers between devices  15 us (19%)
  local copies, waits for them, and re-layouts  5.57 us (7%)
  between operations  1.58 us (2%)
    ppermute x27, starting transfers between devices, swap(): return lax.ppermute(value, axis, [(i, i ^ 1 << bit) for i in range(size)])  38.2 us
    pallas_call x21, Pallas kernels, call(): pl.pallas_call(body, name=name, out_shape=tuple(outs), in_specs=in_specs,...  16.5 us
    ppermute x27, waiting for transfers between devices, swap(): return lax.ppermute(value, axis, [(i, i ^ 1 << bit) for i in range(size)])  15 us
    unnamed x16, local copies, waits for them, and re-layouts  4.25 us
  transfers between devices with their start and end apart: 27, of which 13 were waited for; matrix products, arithmetic and copies ran while one was open for 2% of the time, Pallas kernels for 20%

profile of v4, /device:TPU:0, one launch (start us, length us, event | category | flops | bytes accessed | tf_op | source)
XLA Modules:
  0.0 76.9 jit_solution(745503928269252624)
XLA Ops:
  0.0 0.5 collective-permute-start.23
  0.5 1.2 %copy-done = bf16[128,4096]{1,0:T(8,128)(2,1)S(1)} copy-done((bf16[128,4096]{1,0:T(8,128)(2,1)S(1)}, bf16[128,4096]{1,0:T(8,128)(2,1)}, u32[]{:S(2)}) %copy-start) | copy-done | bytes 1048600
  1.7 0.9 %copy-done.3 = f32[1,4,128,128]{3,2,1,0:T(8,128)S(1)} copy-done((f32[1,4,128,128]{3,2,1,0:T(8,128)S(1)}, f32[1,4,128,128]{3,2,1,0:T(8,128)}, u32[]{:S(2)}) %copy-start.3) | copy-done | bytes 262168
  2.6 0.1 split_masters.1
  2.8 2.6 %collective-permute-start.16 = (bf16[4,64,128]{2,1,0:T(8,128)(2,1)S(1)}, bf16[4,64,128]{2,1,0:T(8,128)(2,1)S(1)}, u32[]{:S(2)}, u32[]{:S(2)}) collective-permute-start(bf16[4,64,128]{2,1,0:T(8,128)(2,1)S(1)} %get-tuple-element.229), channel_id=1, source_target_pairs={{0,2},{2,0},{4,6},{6,4},{8,10},{10,8},{12,14},{14,12},{16,18},{18,... | collective-permute-start | bytes 196616 | tf_op jit(solution)/shard_map/weights/ppermute | solution.py:34
  5.3 0.7 concatenate.12.place
  6.1 1.2 %select_rows.1.refs_4_ = bf16[32,128,128]{2,1,0:T(8,128)(2,1)S(1)} custom-call(s32[67]{0:T(128)S(1)} %concatenate.12.place, bf16[1,128,4096]{2,1,0:T(8,128)(2,1)S(1)} %bitcast.9, bf16[1,128,4096]{2,1,0:T(8,128)(2,1)S(1)} %collective-permute-done.23.refs_1_), custom_call_target="tpu_custom_call" | custom-call | bytes 3145996 | tf_op jit(solution)/shard_map/tokens/select_rows/pallas_call | solution.py:20
  7.3 0.3 collective-permute-start.24
  7.7 0.4 collective-permute-done.16
  8.1 2.9 %collective-permute-start.17 = (bf16[8,64,128]{2,1,0:T(8,128)(2,1)S(1)}, bf16[8,64,128]{2,1,0:T(8,128)(2,1)S(1)}, u32[]{:S(2)}, u32[]{:S(2)}) collective-permute-start(bf16[8,64,128]{2,1,0:T(8,128)(2,1)S(1)} %pad_maximum_fusion), channel_id=1, source_target_pairs={{0,16},{2,18},{4,20},{6,22},{8,24},{10,26},{12,28},{14,30},{16,0},... | collective-permute-start | bytes 393224 | tf_op jit(solution)/shard_map/weights/ppermute | solution.py:34
  11.0 2.0 %copy-done.2 = bf16[128,14336]{1,0:T(8,128)(2,1)S(1)} copy-done((bf16[128,14336]{1,0:T(8,128)(2,1)S(1)}, bf16[128,14336]{1,0:T(8,128)(2,1)}, u32[]{:S(2)}) %copy-start.2) | copy-done | bytes 3670040
  13.0 3.6 %split_upstream.1 = (bf16[32,64,128]{2,1,0:T(8,128)(2,1)S(1)}, bf16[32,32,128]{2,1,0:T(8,128)(2,1)S(1)}, bf16[32,32,128]{2,1,0:T(8,128)(2,1)S(1)}) custom-call(s32[67]{0:T(128)S(1)} %concatenate.12.place, bf16[128,14336]{1,0:T(8,128)(2,1)S(1)} %copy-done.2), custom_call_target="tpu_custom_call" | custom-call | bytes 4718860 | tf_op jit(solution)/shard_map/weights/split_upstream/pallas_call | solution.py:20
  16.7 0.8 %make_plan.1.table = s32[32,64]{1,0:T(8,128)S(1)} custom-call(s32[67]{0:T(128)S(1)} %concatenate.12.place, s32[1,64]{1,0:T(1,128)S(1)} %copy-done.6, s32[1,32]{1,0:T(1,128)S(1)} %copy-done.4, s32[2,64]{1,0:T(2,128)S(1)} %copy-done.5), custom_call_target="tpu_custom_call" | custom-call | bytes 9356 | tf_op jit(solution)/shard_map/plan/make_plan/pallas_call | solution.py:20
  17.5 1.6 %collective-permute-start.18 = (bf16[8,64,128]{2,1,0:T(8,128)(2,1)S(1)}, bf16[8,64,128]{2,1,0:T(8,128)(2,1)S(1)}, u32[]{:S(2)}, u32[]{:S(2)}) collective-permute-start(bf16[8,64,128]{2,1,0:T(8,128)(2,1)S(1)} %pad_maximum_fusion), channel_id=1, source_target_pairs={{0,4},{2,6},{4,0},{6,2},{8,12},{10,14},{12,8},{14,10},{16,20},{18,... | collective-permute-start | bytes 393224 | tf_op jit(solution)/shard_map/weights/ppermute | solution.py:34
  19.1 1.6 %collective-permute-start.19 = (bf16[8,64,128]{2,1,0:T(8,128)(2,1)S(1)}, bf16[8,64,128]{2,1,0:T(8,128)(2,1)S(1)}, u32[]{:S(2)}, u32[]{:S(2)}) collective-permute-start(bf16[8,64,128]{2,1,0:T(8,128)(2,1)S(1)} %collective-permute-done.17), channel_id=1, source_target_pairs={{0,8},{2,10},{4,12},{6,14},{8,0},{10,2},{12,4},{14,6},{16,24},{18,... | collective-permute-start | bytes 393224 | tf_op jit(solution)/shard_map/weights/ppermute | solution.py:34
  20.7 1.8 %collective-permute-done.18 = bf16[8,64,128]{2,1,0:T(8,128)(2,1)S(1)} collective-permute-done((bf16[8,64,128]{2,1,0:T(8,128)(2,1)S(1)}, bf16[8,64,128]{2,1,0:T(8,128)(2,1)S(1)}, u32[]{:S(2)}, u32[]{:S(2)}) %collective-permute-start.18) | collective-permute-done | bytes 131104 | tf_op jit(solution)/shard_map/weights/ppermute | solution.py:34
  22.5 1.5 %collective-permute-done.19 = bf16[8,64,128]{2,1,0:T(8,128)(2,1)S(1)} collective-permute-done((bf16[8,64,128]{2,1,0:T(8,128)(2,1)S(1)}, bf16[8,64,128]{2,1,0:T(8,128)(2,1)S(1)}, u32[]{:S(2)}, u32[]{:S(2)}) %collective-permute-start.19) | collective-permute-done | bytes 131104 | tf_op jit(solution)/shard_map/weights/ppermute | solution.py:34
  24.1 0.6 collective-permute-start.21
  24.7 1.6 %collective-permute-start.20 = (bf16[16,64,128]{2,1,0:T(8,128)(2,1)S(1)}, bf16[16,64,128]{2,1,0:T(8,128)(2,1)S(1)}, u32[]{:S(2)}, u32[]{:S(2)}) collective-permute-start(bf16[16,64,128]{2,1,0:T(8,128)(2,1)S(1)} %constant_dynamic-update-slice_fusion.refs_0_), channel_id=1, source_target_pairs={{0,8},{2,10},{4,12},{6,14},{8,0},{10,2},{12,4},{14,6},{16,24},{18,... | collective-permute-start | bytes 786440 | tf_op jit(solution)/shard_map/weights/ppermute | solution.py:34
  26.3 1.5 %collective-permute-start.25 = (bf16[32,32,128]{2,1,0:T(8,128)(2,1)S(1)}, bf16[32,32,128]{2,1,0:T(8,128)(2,1)S(1)}, u32[]{:S(2)}, u32[]{:S(2)}) collective-permute-start(bf16[32,32,128]{2,1,0:T(8,128)(2,1)S(1)} %get-tuple-element.172), channel_id=1, source_target_pairs={{0,2},{2,0},{4,6},{6,4},{8,10},{10,8},{12,14},{14,12},{16,18},{18,... | collective-permute-start | bytes 786440 | tf_op jit(solution)/shard_map/upstream/ppermute | solution.py:34
  27.8 0.5 slice.4
  28.3 1.2 %collective-permute-done.22 = s32[1]{0:T(128)} collective-permute-done((s32[1]{0:T(128)}, s32[1]{0:T(128)}, u32[]{:S(2)}, u32[]{:S(2)}) %collective-permute-start.22) | collective-permute-done | bytes 36 | tf_op jit(solution)/shard_map/plan/ppermute | solution.py:34
  29.5 0.5 collective-permute-start.26
  31.4 2.8 %own_part.1 = (bf16[32,128,128]{2,1,0:T(8,128)(2,1)S(1)}, f32[32,128,128]{2,1,0:T(8,128)S(1)}) custom-call(s32[32,64]{1,0:T(8,128)S(1)} %make_plan.1.table, bf16[16,64,128]{2,1,0:T(8,128)(2,1)S(1)} %constant_dynamic-update-slice_fusion.refs_0_, bf16[16,64,128]{2,1,0:T(8,128)(2,1)S(1)} %collective-permute-done.20.refs_1_, ...), custom_call_target="tpu_custom_call" | custom-call | flops 268435456 | bytes 5775360 | tf_op jit(solution)/shard_map/own_tokens/own_part/pallas_call | solution.py:20
  34.2 2.3 %other_slopes.1.slope = f32[32,128,128]{2,1,0:T(8,128)S(1)} custom-call(s32[32,64]{1,0:T(8,128)S(1)} %make_plan.1.table, bf16[32,128,128]{2,1,0:T(8,128)(2,1)S(1)} %get-tuple-element.171.weights, bf16[32,128,128]{2,1,0:T(8,128)(2,1)S(1)} %collective-permute-done.24.other_tokens), custom_call_target="tpu_custom_call" | custom-call | flops 134217728 | bytes 4202496 | tf_op jit(solution)/shard_map/other_tokens/other_slopes/pallas_call | solution.py:20
  36.4 2.6 %collective-permute-done.25.other_up = bf16[32,32,128]{2,1,0:T(8,128)(2,1)S(1)} collective-permute-done((bf16[32,32,128]{2,1,0:T(8,128)(2,1)S(1)}, bf16[32,32,128]{2,1,0:T(8,128)(2,1)S(1)}, u32[]{:S(2)}, u32[]{:S(2)}) %collective-permute-start.25) | collective-permute-done | bytes 262176 | tf_op jit(solution)/shard_map/upstream/ppermute | solution.py:34
  39.0 1.4 %other_part.6 = (bf16[44,16,128]{2,1,0:T(8,128)(2,1)S(1)}, f32[44,16,128]{2,1,0:T(8,128)S(1)}, bf16[44,16,128]{2,1,0:T(8,128)(2,1)S(1)}, f32[44,16,128]{2,1,0:T(8,128)S(1)}) custom-call(s32[32,64]{1,0:T(8,128)S(1)} %make_plan.1.table, f32[32,128,128]{2,1,0:T(8,128)S(1)} %other_slopes.1.slope, bf16[32,128,128]{2,1,0:T(8,128)(2,1)S(1)} %collective-permute-done.24.other_tokens, ...), custom_call_target="tpu_custom_call" | custom-call | flops 67108864 | bytes 6594560 | tf_op jit(solution)/shard_map/other_part/pallas_call | solution.py:20
  40.4 1.6 %collective-permute-start.27 = (bf16[44,16,128]{2,1,0:T(8,128)(2,1)S(1)}, bf16[44,16,128]{2,1,0:T(8,128)(2,1)S(1)}, u32[]{:S(2)}, u32[]{:S(2)}) collective-permute-start(bf16[44,16,128]{2,1,0:T(8,128)(2,1)S(1)} %get-tuple-element.176), channel_id=1, source_target_pairs={{0,8},{2,10},{4,12},{6,14},{8,0},{10,2},{12,4},{14,6},{16,24},{18,... | collective-permute-start | bytes 540680 | tf_op jit(solution)/shard_map/ppermute | solution.py:34
  42.0 1.5 %collective-permute-start.31 = (bf16[44,16,128]{2,1,0:T(8,128)(2,1)S(1)}, bf16[44,16,128]{2,1,0:T(8,128)(2,1)S(1)}, u32[]{:S(2)}, u32[]{:S(2)}) collective-permute-start(bf16[44,16,128]{2,1,0:T(8,128)(2,1)S(1)} %get-tuple-element.186), channel_id=1, source_target_pairs={{0,4},{2,6},{4,0},{6,2},{8,12},{10,14},{12,8},{14,10},{16,20},{18,... | collective-permute-start | bytes 540680 | tf_op jit(solution)/shard_map/ppermute | solution.py:34
  43.5 0.4 collective-permute-done.26.other_up
  43.9 1.4 %other_part.7 = (bf16[44,16,128]{2,1,0:T(8,128)(2,1)S(1)}, f32[44,16,128]{2,1,0:T(8,128)S(1)}, bf16[44,16,128]{2,1,0:T(8,128)(2,1)S(1)}, f32[44,16,128]{2,1,0:T(8,128)S(1)}) custom-call(s32[32,64]{1,0:T(8,128)S(1)} %make_plan.1.table, f32[32,128,128]{2,1,0:T(8,128)S(1)} %other_slopes.1.slope, bf16[32,128,128]{2,1,0:T(8,128)(2,1)S(1)} %collective-permute-done.24.other_tokens, ...), custom_call_target="tpu_custom_call" | custom-call | flops 67108864 | bytes 6594560 | tf_op jit(solution)/shard_map/other_part/pallas_call | solution.py:20
  45.3 1.6 %collective-permute-start.30 = (bf16[44,16,128]{2,1,0:T(8,128)(2,1)S(1)}, bf16[44,16,128]{2,1,0:T(8,128)(2,1)S(1)}, u32[]{:S(2)}, u32[]{:S(2)}) collective-permute-start(bf16[44,16,128]{2,1,0:T(8,128)(2,1)S(1)} %get-tuple-element.184), channel_id=1, source_target_pairs={{0,4},{2,6},{4,0},{6,2},{8,12},{10,14},{12,8},{14,10},{16,20},{18,... | collective-permute-start | bytes 540680 | tf_op jit(solution)/shard_map/ppermute | solution.py:34
  46.9 1.6 %collective-permute-start.29 = (bf16[44,16,128]{2,1,0:T(8,128)(2,1)S(1)}, bf16[44,16,128]{2,1,0:T(8,128)(2,1)S(1)}, u32[]{:S(2)}, u32[]{:S(2)}) collective-permute-start(bf16[44,16,128]{2,1,0:T(8,128)(2,1)S(1)} %get-tuple-element.183), channel_id=1, source_target_pairs={{0,8},{2,10},{4,12},{6,14},{8,0},{10,2},{12,4},{14,6},{16,24},{18,... | collective-permute-start | bytes 540680 | tf_op jit(solution)/shard_map/ppermute | solution.py:34
  48.5 0.2 combine.36
  48.6 0.6 collective-permute-start.28
  49.2 0.2 combine.37
  49.4 2.6 %collective-permute-start.35 = (bf16[28,16,128]{2,1,0:T(8,128)(2,1)S(1)}, bf16[28,16,128]{2,1,0:T(8,128)(2,1)S(1)}, u32[]{:S(2)}, u32[]{:S(2)}) collective-permute-start(bf16[28,16,128]{2,1,0:T(8,128)(2,1)S(1)} %get-tuple-element.198), channel_id=1, source_target_pairs={{0,16},{2,18},{4,20},{6,22},{8,24},{10,26},{12,28},{14,30},{16,0},... | collective-permute-start | bytes 344072 | tf_op jit(solution)/shard_map/ppermute | solution.py:34
  52.0 0.6 collective-permute-done.30.refs_1_
  52.6 0.2 combine.38
  52.8 1.5 %collective-permute-start.34 = (bf16[28,16,128]{2,1,0:T(8,128)(2,1)S(1)}, bf16[28,16,128]{2,1,0:T(8,128)(2,1)S(1)}, u32[]{:S(2)}, u32[]{:S(2)}) collective-permute-start(bf16[28,16,128]{2,1,0:T(8,128)(2,1)S(1)} %get-tuple-element.197), channel_id=1, source_target_pairs={{0,8},{2,10},{4,12},{6,14},{8,0},{10,2},{12,4},{14,6},{16,24},{18,... | collective-permute-start | bytes 344072 | tf_op jit(solution)/shard_map/ppermute | solution.py:34
  54.3 0.3 collective-permute-done.29.refs_1_
  54.5 0.2 combine.39
  54.7 3.3 %collective-permute-start.33 = (bf16[28,16,128]{2,1,0:T(8,128)(2,1)S(1)}, bf16[28,16,128]{2,1,0:T(8,128)(2,1)S(1)}, u32[]{:S(2)}, u32[]{:S(2)}) collective-permute-start(bf16[28,16,128]{2,1,0:T(8,128)(2,1)S(1)} %get-tuple-element.196), channel_id=1, source_target_pairs={{0,16},{2,18},{4,20},{6,22},{8,24},{10,26},{12,28},{14,30},{16,0},... | collective-permute-start | bytes 344072 | tf_op jit(solution)/shard_map/ppermute | solution.py:34
  57.9 0.1 combine.40
  58.2 0.1 combine.41
  58.3 2.5 %collective-permute-start.37 = (bf16[20,16,128]{2,1,0:T(8,128)(2,1)S(1)}, bf16[20,16,128]{2,1,0:T(8,128)(2,1)S(1)}, u32[]{:S(2)}, u32[]{:S(2)}) collective-permute-start(bf16[20,16,128]{2,1,0:T(8,128)(2,1)S(1)} %get-tuple-element.208), channel_id=1, source_target_pairs={{0,8},{2,10},{4,12},{6,14},{8,0},{10,2},{12,4},{14,6},{16,24},{18,... | collective-permute-start | bytes 245768 | tf_op jit(solution)/shard_map/ppermute | solution.py:34
  60.9 0.1 combine.42
  61.0 3.0 %collective-permute-start.39 = (bf16[20,16,128]{2,1,0:T(8,128)(2,1)S(1)}, bf16[20,16,128]{2,1,0:T(8,128)(2,1)S(1)}, u32[]{:S(2)}, u32[]{:S(2)}) collective-permute-start(bf16[20,16,128]{2,1,0:T(8,128)(2,1)S(1)} %get-tuple-element.212), channel_id=1, source_target_pairs={{0,16},{2,18},{4,20},{6,22},{8,24},{10,26},{12,28},{14,30},{16,0},... | collective-permute-start | bytes 245768 | tf_op jit(solution)/shard_map/ppermute | solution.py:34
  64.0 2.1 %collective-permute-done.33.refs_1_ = bf16[28,16,128]{2,1,0:T(8,128)(2,1)S(1)} collective-permute-done((bf16[28,16,128]{2,1,0:T(8,128)(2,1)S(1)}, bf16[28,16,128]{2,1,0:T(8,128)(2,1)S(1)}, u32[]{:S(2)}, u32[]{:S(2)}) %collective-permute-start.33) | collective-permute-done | bytes 114720 | tf_op jit(solution)/shard_map/ppermute | solution.py:34
  66.1 0.1 combine.43
  66.3 0.5 collective-permute-start.41
  66.7 1.3 %collective-permute-done.32.refs_1_ = bf16[20,16,128]{2,1,0:T(8,128)(2,1)S(1)} collective-permute-done((bf16[20,16,128]{2,1,0:T(8,128)(2,1)S(1)}, bf16[20,16,128]{2,1,0:T(8,128)(2,1)S(1)}, u32[]{:S(2)}, u32[]{:S(2)}) %collective-permute-start.32) | collective-permute-done | bytes 81952 | tf_op jit(solution)/shard_map/ppermute | solution.py:34
  68.0 0.1 combine.44
  68.2 0.1 combine.45
  68.3 0.6 collective-permute-start.38
  68.9 1.5 %collective-permute-start.36 = (bf16[12,16,128]{2,1,0:T(8,128)(2,1)S(1)}, bf16[12,16,128]{2,1,0:T(8,128)(2,1)S(1)}, u32[]{:S(2)}, u32[]{:S(2)}) collective-permute-start(bf16[12,16,128]{2,1,0:T(8,128)(2,1)S(1)} %get-tuple-element.207), channel_id=1, source_target_pairs={{0,2},{2,0},{4,6},{6,4},{8,10},{10,8},{12,14},{14,12},{16,18},{18,... | collective-permute-start | bytes 147464 | tf_op jit(solution)/shard_map/ppermute | solution.py:34
  70.4 0.1 combine.46
  70.6 0.2 collective-permute-done.41.refs_1_
  70.8 0.1 combine.47
  70.9 0.5 collective-permute-start.42
  71.5 1.5 %collective-permute-start.40 = (bf16[12,16,128]{2,1,0:T(8,128)(2,1)S(1)}, bf16[12,16,128]{2,1,0:T(8,128)(2,1)S(1)}, u32[]{:S(2)}, u32[]{:S(2)}) collective-permute-start(bf16[12,16,128]{2,1,0:T(8,128)(2,1)S(1)} %get-tuple-element.215), channel_id=1, source_target_pairs={{0,2},{2,0},{4,6},{6,4},{8,10},{10,8},{12,14},{14,12},{16,18},{18,... | collective-permute-start | bytes 147464 | tf_op jit(solution)/shard_map/ppermute | solution.py:34
  73.0 2.0 %collective-permute-done.42 = bf16[12,16,128]{2,1,0:T(8,128)(2,1)S(1)} collective-permute-done((bf16[12,16,128]{2,1,0:T(8,128)(2,1)S(1)}, bf16[12,16,128]{2,1,0:T(8,128)(2,1)S(1)}, u32[]{:S(2)}, u32[]{:S(2)}) %collective-permute-start.42) | collective-permute-done | bytes 49184 | tf_op jit(solution)/shard_map/ppermute | solution.py:34
  75.1 0.5 collective-permute-done.40
  75.6 1.3 %finish.1 = f32[1,12,128,128]{3,2,1,0:T(8,128)} custom-call(s32[32,64]{1,0:T(8,128)S(1)} %make_plan.1.table, f32[12,16,128]{2,1,0:T(8,128)S(1)} %get-tuple-element.220.refs_0_, bf16[12,16,128]{2,1,0:T(8,128)(2,1)S(1)} %get-tuple-element.221.refs_1_, f32[12,16,128]{2,1,0:T(8,128)S(1)} %get-tuple-element.222.refs_2_, ...), custom_call_target="tpu_custom_call" | custom-call | bytes 1384448 | tf_op jit(solution)/shard_map/finish/pallas_call | solution.py:20
  (38 shorter events, 0.3 us)
Async XLA Ops:
  0.0 6.1 %collective-permute-start.23 = (bf16[1,128,4096]{2,1,0:T(8,128)(2,1)}, bf16[1,128,4096]{2,1,0:T(8,128)(2,1)S(1)}, u32[]{:S(2)}, u32[]{:S(2)}) collective-permute-start(bf16[1,128,4096]{2,1,0:T(8,128)(2,1)} %bitcast.8), channel_id=1, source_target_pairs={{0,1},{1,0},{2,3},{3,2},{4,5},{5,4},{6,7},{7,6},{8,9},{9,8},{10,11... | collective-permute-start | bytes 3145736 | tf_op jit(solution)/shard_map/tokens/ppermute | solution.py:34
  0.5 1.2 %copy-start = (bf16[128,4096]{1,0:T(8,128)(2,1)S(1)}, bf16[128,4096]{1,0:T(8,128)(2,1)}, u32[]{:S(2)}) copy-start(bf16[128,4096]{1,0:T(8,128)(2,1)} %tokens.1) | copy-start | bytes 3145732
  1.7 0.9 %copy-start.3 = (f32[1,4,128,128]{3,2,1,0:T(8,128)S(1)}, f32[1,4,128,128]{3,2,1,0:T(8,128)}, u32[]{:S(2)}) copy-start(f32[1,4,128,128]{3,2,1,0:T(8,128)} %masters.1) | copy-start | bytes 786436
  2.6 3.4 %copy-start.1 = (bf16[128,4096]{1,0:T(8,128)(2,1)S(1)}, bf16[128,4096]{1,0:T(8,128)(2,1)}, u32[]{:S(2)}) copy-start(bf16[128,4096]{1,0:T(8,128)(2,1)} %tokens.1) | copy-start | bytes 3145732
  2.8 5.3 %collective-permute-start.16 = (bf16[4,64,128]{2,1,0:T(8,128)(2,1)S(1)}, bf16[4,64,128]{2,1,0:T(8,128)(2,1)S(1)}, u32[]{:S(2)}, u32[]{:S(2)}) collective-permute-start(bf16[4,64,128]{2,1,0:T(8,128)(2,1)S(1)} %get-tuple-element.229), channel_id=1, source_target_pairs={{0,2},{2,0},{4,6},{6,4},{8,10},{10,8},{12,14},{14,12},{16,18},{18,... | collective-permute-start | bytes 196616 | tf_op jit(solution)/shard_map/weights/ppermute | solution.py:34
  7.3 9.4 %copy-start.4 = (s32[1,32]{1,0:T(1,128)S(1)}, s32[1,32]{1,0:T(1,128)}, u32[]{:S(2)}) copy-start(s32[1,32]{1,0:T(1,128)} %columns.1) | copy-start | bytes 388
  7.3 9.4 %copy-start.5 = (s32[2,64]{1,0:T(2,128)S(1)}, s32[2,64]{1,0:T(2,128)}, u32[]{:S(2)}) copy-start(s32[2,64]{1,0:T(2,128)} %constant.16.clone.found) | copy-start | bytes 1540
  7.3 9.4 %copy-start.6 = (s32[1,64]{1,0:T(1,128)S(1)}, s32[1,64]{1,0:T(1,128)}, u32[]{:S(2)}) copy-start(s32[1,64]{1,0:T(1,128)} %owners.1) | copy-start | bytes 772
  7.3 26.8 %collective-permute-start.24 = (bf16[32,128,128]{2,1,0:T(8,128)(2,1)S(1)}, bf16[32,128,128]{2,1,0:T(8,128)(2,1)S(1)}, u32[]{:S(2)}, u32[]{:S(2)}) collective-permute-start(bf16[32,128,128]{2,1,0:T(8,128)(2,1)S(1)} %select_rows.1.refs_4_), channel_id=1, source_target_pairs={{0,2},{2,0},{4,6},{6,4},{8,10},{10,8},{12,14},{14,12},{16,18},{18,... | collective-permute-start | bytes 3145736 | tf_op jit(solution)/shard_map/weights/ppermute | solution.py:34
  8.1 9.4 %collective-permute-start.17 = (bf16[8,64,128]{2,1,0:T(8,128)(2,1)S(1)}, bf16[8,64,128]{2,1,0:T(8,128)(2,1)S(1)}, u32[]{:S(2)}, u32[]{:S(2)}) collective-permute-start(bf16[8,64,128]{2,1,0:T(8,128)(2,1)S(1)} %pad_maximum_fusion), channel_id=1, source_target_pairs={{0,16},{2,18},{4,20},{6,22},{8,24},{10,26},{12,28},{14,30},{16,0},... | collective-permute-start | bytes 393224 | tf_op jit(solution)/shard_map/weights/ppermute | solution.py:34
  11.0 2.0 %copy-start.2 = (bf16[128,14336]{1,0:T(8,128)(2,1)S(1)}, bf16[128,14336]{1,0:T(8,128)(2,1)}, u32[]{:S(2)}) copy-start(bf16[128,14336]{1,0:T(8,128)(2,1)} %grad.1) | copy-start | bytes 11010052
  17.5 5.0 %collective-permute-start.18 = (bf16[8,64,128]{2,1,0:T(8,128)(2,1)S(1)}, bf16[8,64,128]{2,1,0:T(8,128)(2,1)S(1)}, u32[]{:S(2)}, u32[]{:S(2)}) collective-permute-start(bf16[8,64,128]{2,1,0:T(8,128)(2,1)S(1)} %pad_maximum_fusion), channel_id=1, source_target_pairs={{0,4},{2,6},{4,0},{6,2},{8,12},{10,14},{12,8},{14,10},{16,20},{18,... | collective-permute-start | bytes 393224 | tf_op jit(solution)/shard_map/weights/ppermute | solution.py:34
  19.1 5.0 %collective-permute-start.19 = (bf16[8,64,128]{2,1,0:T(8,128)(2,1)S(1)}, bf16[8,64,128]{2,1,0:T(8,128)(2,1)S(1)}, u32[]{:S(2)}, u32[]{:S(2)}) collective-permute-start(bf16[8,64,128]{2,1,0:T(8,128)(2,1)S(1)} %collective-permute-done.17), channel_id=1, source_target_pairs={{0,8},{2,10},{4,12},{6,14},{8,0},{10,2},{12,4},{14,6},{16,24},{18,... | collective-permute-start | bytes 393224 | tf_op jit(solution)/shard_map/weights/ppermute | solution.py:34
  24.1 7.3 %collective-permute-start.21 = (bf16[16,64,128]{2,1,0:T(8,128)(2,1)S(1)}, bf16[16,64,128]{2,1,0:T(8,128)(2,1)S(1)}, u32[]{:S(2)}, u32[]{:S(2)}) collective-permute-start(bf16[16,64,128]{2,1,0:T(8,128)(2,1)S(1)} %constant_dynamic-update-slice_fusion.2.refs_2_), channel_id=1, source_target_pairs={{0,4},{2,6},{4,0},{6,2},{8,12},{10,14},{12,8},{14,10},{16,20},{18,... | collective-permute-start | bytes 786440 | tf_op jit(solution)/shard_map/weights/ppermute | solution.py:34
  24.7 6.7 %collective-permute-start.20 = (bf16[16,64,128]{2,1,0:T(8,128)(2,1)S(1)}, bf16[16,64,128]{2,1,0:T(8,128)(2,1)S(1)}, u32[]{:S(2)}, u32[]{:S(2)}) collective-permute-start(bf16[16,64,128]{2,1,0:T(8,128)(2,1)S(1)} %constant_dynamic-update-slice_fusion.refs_0_), channel_id=1, source_target_pairs={{0,8},{2,10},{4,12},{6,14},{8,0},{10,2},{12,4},{14,6},{16,24},{18,... | collective-permute-start | bytes 786440 | tf_op jit(solution)/shard_map/weights/ppermute | solution.py:34
  26.3 12.7 %collective-permute-start.25 = (bf16[32,32,128]{2,1,0:T(8,128)(2,1)S(1)}, bf16[32,32,128]{2,1,0:T(8,128)(2,1)S(1)}, u32[]{:S(2)}, u32[]{:S(2)}) collective-permute-start(bf16[32,32,128]{2,1,0:T(8,128)(2,1)S(1)} %get-tuple-element.172), channel_id=1, source_target_pairs={{0,2},{2,0},{4,6},{6,4},{8,10},{10,8},{12,14},{14,12},{16,18},{18,... | collective-permute-start | bytes 786440 | tf_op jit(solution)/shard_map/upstream/ppermute | solution.py:34
  28.3 1.2 %collective-permute-start.22 = (s32[1]{0:T(128)}, s32[1]{0:T(128)}, u32[]{:S(2)}, u32[]{:S(2)}) collective-permute-start(s32[1]{0:T(128)} %bitcast.5), channel_id=1, source_target_pairs={{0,1},{1,0},{2,3},{3,2},{4,5},{5,4},{6,7},{7,6},{8,9},{9,8},{10,11... | collective-permute-start | bytes 20 | tf_op jit(solution)/shard_map/plan/ppermute | solution.py:34
  29.5 14.4 %collective-permute-start.26 = (bf16[32,32,128]{2,1,0:T(8,128)(2,1)S(1)}, bf16[32,32,128]{2,1,0:T(8,128)(2,1)S(1)}, u32[]{:S(2)}, u32[]{:S(2)}) collective-permute-start(bf16[32,32,128]{2,1,0:T(8,128)(2,1)S(1)} %get-tuple-element.174), channel_id=1, source_target_pairs={{0,2},{2,0},{4,6},{6,4},{8,10},{10,8},{12,14},{14,12},{16,18},{18,... | collective-permute-start | bytes 786440 | tf_op jit(solution)/shard_map/upstream/ppermute | solution.py:34
  40.4 8.1 %collective-permute-start.27 = (bf16[44,16,128]{2,1,0:T(8,128)(2,1)S(1)}, bf16[44,16,128]{2,1,0:T(8,128)(2,1)S(1)}, u32[]{:S(2)}, u32[]{:S(2)}) collective-permute-start(bf16[44,16,128]{2,1,0:T(8,128)(2,1)S(1)} %get-tuple-element.176), channel_id=1, source_target_pairs={{0,8},{2,10},{4,12},{6,14},{8,0},{10,2},{12,4},{14,6},{16,24},{18,... | collective-permute-start | bytes 540680 | tf_op jit(solution)/shard_map/ppermute | solution.py:34
  42.0 7.2 %collective-permute-start.31 = (bf16[44,16,128]{2,1,0:T(8,128)(2,1)S(1)}, bf16[44,16,128]{2,1,0:T(8,128)(2,1)S(1)}, u32[]{:S(2)}, u32[]{:S(2)}) collective-permute-start(bf16[44,16,128]{2,1,0:T(8,128)(2,1)S(1)} %get-tuple-element.186), channel_id=1, source_target_pairs={{0,4},{2,6},{4,0},{6,2},{8,12},{10,14},{12,8},{14,10},{16,20},{18,... | collective-permute-start | bytes 540680 | tf_op jit(solution)/shard_map/ppermute | solution.py:34
  45.3 7.3 %collective-permute-start.30 = (bf16[44,16,128]{2,1,0:T(8,128)(2,1)S(1)}, bf16[44,16,128]{2,1,0:T(8,128)(2,1)S(1)}, u32[]{:S(2)}, u32[]{:S(2)}) collective-permute-start(bf16[44,16,128]{2,1,0:T(8,128)(2,1)S(1)} %get-tuple-element.184), channel_id=1, source_target_pairs={{0,4},{2,6},{4,0},{6,2},{8,12},{10,14},{12,8},{14,10},{16,20},{18,... | collective-permute-start | bytes 540680 | tf_op jit(solution)/shard_map/ppermute | solution.py:34
  46.9 7.6 %collective-permute-start.29 = (bf16[44,16,128]{2,1,0:T(8,128)(2,1)S(1)}, bf16[44,16,128]{2,1,0:T(8,128)(2,1)S(1)}, u32[]{:S(2)}, u32[]{:S(2)}) collective-permute-start(bf16[44,16,128]{2,1,0:T(8,128)(2,1)S(1)} %get-tuple-element.183), channel_id=1, source_target_pairs={{0,8},{2,10},{4,12},{6,14},{8,0},{10,2},{12,4},{14,6},{16,24},{18,... | collective-permute-start | bytes 540680 | tf_op jit(solution)/shard_map/ppermute | solution.py:34
  48.6 9.3 %collective-permute-start.28 = (bf16[28,16,128]{2,1,0:T(8,128)(2,1)S(1)}, bf16[28,16,128]{2,1,0:T(8,128)(2,1)S(1)}, u32[]{:S(2)}, u32[]{:S(2)}) collective-permute-start(bf16[28,16,128]{2,1,0:T(8,128)(2,1)S(1)} %get-tuple-element.181), channel_id=1, source_target_pairs={{0,4},{2,6},{4,0},{6,2},{8,12},{10,14},{12,8},{14,10},{16,20},{18,... | collective-permute-start | bytes 344072 | tf_op jit(solution)/shard_map/ppermute | solution.py:34
  49.4 8.8 %collective-permute-start.35 = (bf16[28,16,128]{2,1,0:T(8,128)(2,1)S(1)}, bf16[28,16,128]{2,1,0:T(8,128)(2,1)S(1)}, u32[]{:S(2)}, u32[]{:S(2)}) collective-permute-start(bf16[28,16,128]{2,1,0:T(8,128)(2,1)S(1)} %get-tuple-element.198), channel_id=1, source_target_pairs={{0,16},{2,18},{4,20},{6,22},{8,24},{10,26},{12,28},{14,30},{16,0},... | collective-permute-start | bytes 344072 | tf_op jit(solution)/shard_map/ppermute | solution.py:34
  52.8 8.1 %collective-permute-start.34 = (bf16[28,16,128]{2,1,0:T(8,128)(2,1)S(1)}, bf16[28,16,128]{2,1,0:T(8,128)(2,1)S(1)}, u32[]{:S(2)}, u32[]{:S(2)}) collective-permute-start(bf16[28,16,128]{2,1,0:T(8,128)(2,1)S(1)} %get-tuple-element.197), channel_id=1, source_target_pairs={{0,8},{2,10},{4,12},{6,14},{8,0},{10,2},{12,4},{14,6},{16,24},{18,... | collective-permute-start | bytes 344072 | tf_op jit(solution)/shard_map/ppermute | solution.py:34
  54.7 11.4 %collective-permute-start.33 = (bf16[28,16,128]{2,1,0:T(8,128)(2,1)S(1)}, bf16[28,16,128]{2,1,0:T(8,128)(2,1)S(1)}, u32[]{:S(2)}, u32[]{:S(2)}) collective-permute-start(bf16[28,16,128]{2,1,0:T(8,128)(2,1)S(1)} %get-tuple-element.196), channel_id=1, source_target_pairs={{0,16},{2,18},{4,20},{6,22},{8,24},{10,26},{12,28},{14,30},{16,0},... | collective-permute-start | bytes 344072 | tf_op jit(solution)/shard_map/ppermute | solution.py:34
  58.1 9.9 %collective-permute-start.32 = (bf16[20,16,128]{2,1,0:T(8,128)(2,1)S(1)}, bf16[20,16,128]{2,1,0:T(8,128)(2,1)S(1)}, u32[]{:S(2)}, u32[]{:S(2)}) collective-permute-start(bf16[20,16,128]{2,1,0:T(8,128)(2,1)S(1)} %get-tuple-element.195), channel_id=1, source_target_pairs={{0,16},{2,18},{4,20},{6,22},{8,24},{10,26},{12,28},{14,30},{16,0},... | collective-permute-start | bytes 245768 | tf_op jit(solution)/shard_map/ppermute | solution.py:34
  58.3 9.8 %collective-permute-start.37 = (bf16[20,16,128]{2,1,0:T(8,128)(2,1)S(1)}, bf16[20,16,128]{2,1,0:T(8,128)(2,1)S(1)}, u32[]{:S(2)}, u32[]{:S(2)}) collective-permute-start(bf16[20,16,128]{2,1,0:T(8,128)(2,1)S(1)} %get-tuple-element.208), channel_id=1, source_target_pairs={{0,8},{2,10},{4,12},{6,14},{8,0},{10,2},{12,4},{14,6},{16,24},{18,... | collective-permute-start | bytes 245768 | tf_op jit(solution)/shard_map/ppermute | solution.py:34
  61.0 9.4 %collective-permute-start.39 = (bf16[20,16,128]{2,1,0:T(8,128)(2,1)S(1)}, bf16[20,16,128]{2,1,0:T(8,128)(2,1)S(1)}, u32[]{:S(2)}, u32[]{:S(2)}) collective-permute-start(bf16[20,16,128]{2,1,0:T(8,128)(2,1)S(1)} %get-tuple-element.212), channel_id=1, source_target_pairs={{0,16},{2,18},{4,20},{6,22},{8,24},{10,26},{12,28},{14,30},{16,0},... | collective-permute-start | bytes 245768 | tf_op jit(solution)/shard_map/ppermute | solution.py:34
  66.3 4.5 %collective-permute-start.41 = (bf16[20,16,128]{2,1,0:T(8,128)(2,1)S(1)}, bf16[20,16,128]{2,1,0:T(8,128)(2,1)S(1)}, u32[]{:S(2)}, u32[]{:S(2)}) collective-permute-start(bf16[20,16,128]{2,1,0:T(8,128)(2,1)S(1)} %get-tuple-element.216), channel_id=1, source_target_pairs={{0,4},{2,6},{4,0},{6,2},{8,12},{10,14},{12,8},{14,10},{16,20},{18,... | collective-permute-start | bytes 245768 | tf_op jit(solution)/shard_map/ppermute | solution.py:34
  68.3 4.7 %collective-permute-start.38 = (bf16[12,16,128]{2,1,0:T(8,128)(2,1)S(1)}, bf16[12,16,128]{2,1,0:T(8,128)(2,1)S(1)}, u32[]{:S(2)}, u32[]{:S(2)}) collective-permute-start(bf16[12,16,128]{2,1,0:T(8,128)(2,1)S(1)} %get-tuple-element.211), channel_id=1, source_target_pairs={{0,2},{2,0},{4,6},{6,4},{8,10},{10,8},{12,14},{14,12},{16,18},{18,... | collective-permute-start | bytes 147464 | tf_op jit(solution)/shard_map/ppermute | solution.py:34
  68.9 4.1 %collective-permute-start.36 = (bf16[12,16,128]{2,1,0:T(8,128)(2,1)S(1)}, bf16[12,16,128]{2,1,0:T(8,128)(2,1)S(1)}, u32[]{:S(2)}, u32[]{:S(2)}) collective-permute-start(bf16[12,16,128]{2,1,0:T(8,128)(2,1)S(1)} %get-tuple-element.207), channel_id=1, source_target_pairs={{0,2},{2,0},{4,6},{6,4},{8,10},{10,8},{12,14},{14,12},{16,18},{18,... | collective-permute-start | bytes 147464 | tf_op jit(solution)/shard_map/ppermute | solution.py:34
  70.9 4.2 %collective-permute-start.42 = (bf16[12,16,128]{2,1,0:T(8,128)(2,1)S(1)}, bf16[12,16,128]{2,1,0:T(8,128)(2,1)S(1)}, u32[]{:S(2)}, u32[]{:S(2)}) collective-permute-start(bf16[12,16,128]{2,1,0:T(8,128)(2,1)S(1)} %get-tuple-element.219), channel_id=1, source_target_pairs={{0,2},{2,0},{4,6},{6,4},{8,10},{10,8},{12,14},{14,12},{16,18},{18,... | collective-permute-start | bytes 147464 | tf_op jit(solution)/shard_map/ppermute | solution.py:34
  71.5 4.1 %collective-permute-start.40 = (bf16[12,16,128]{2,1,0:T(8,128)(2,1)S(1)}, bf16[12,16,128]{2,1,0:T(8,128)(2,1)S(1)}, u32[]{:S(2)}, u32[]{:S(2)}) collective-permute-start(bf16[12,16,128]{2,1,0:T(8,128)(2,1)S(1)} %get-tuple-element.215), channel_id=1, source_target_pairs={{0,2},{2,0},{4,6},{6,4},{8,10},{10,8},{12,14},{14,12},{16,18},{18,... | collective-permute-start | bytes 147464 | tf_op jit(solution)/shard_map/ppermute | solution.py:34

commit v5 on v4

--- a/solution.py
+++ b/solution.py
@@ -145,14 +145,17 @@
     return jnp.max(table[pl.ds(row, 1), :].astype(F32)).astype(jnp.int32)
 
 
-def other_part(rows, steps, start, table, slope, other_tokens, other_up, grad, *refs):
-    outs, total, ordered = refs[: 2 * len(steps)], refs[2 * len(steps)], refs[2 * len(steps) + 1 :]
+def other_part(rows, steps, start, plan, slope, other_tokens, other_up, grad, *refs):
+    outs, (table, arrived, total, *ordered) = refs[: 2 * len(steps)], refs[2 * len(steps) :]
+    copy = pltpu.make_async_copy(plan, table, arrived)
+    copy.start()
     places, height, half = other_up.shape[0], other_up.shape[1], grad.shape[1] // 2
     gate, up = pl.ds(start, height), pl.ds(half + start, height)
     for k in range(places):
         result = term(other_up[k], slope[k, gate], slope[k, up], other_tokens[k])
         total[k, :height] = grad[k, gate] + result[:height]
         total[k, height:] = grad[k, up] + result[height:]
+    copy.wait()
     first = 0
     for n, (order, step) in enumerate(steps):
         sent, kept = outs[2 * n], outs[2 * n + 1]
@@ -190,7 +193,7 @@
     bits = owner_count.bit_length() - 1
     if bits == 4:
         y, near, far = 1, 2, 3
-        parts = ((1, (near, y, far)), (1, (y, far, near))), ((1, (y, near, far)), (1, (near, far, y)))
+        parts = ((1, (near, y, far)), (1, (y, far, near))), ((1, (near, y, far)), (1, (y, near, far)))
         turns = tuple(((part,), 0) for part in range(2)) + tuple(((piece,), n) for n in range(1, 4) for piece in range(4))
         return 0, (y, near), (far,), parts, turns
     pair, ends, rest = bits - 2, (0, bits - 1), tuple(range(1, bits - 2))
@@ -213,13 +216,13 @@
     return {name: n for n, name in enumerate(names)}
 
 
-def make_plan(axes, usual, own_blocks, place, owners, columns, found, table):
-    pair, rows = axes[0], rows_of(axes)
-    count, places = owners.shape[1], columns.shape[1]
+def make_plan(axes, usual, own_blocks, place, columns, found, *refs):
+    pair, rows, owners, table = axes[0], rows_of(axes), refs[:-1], refs[-1]
+    count, places = owners[0].shape[1], columns.shape[1]
     me = place[2]
     across = lax.broadcasted_iota(jnp.int32, (count, count), 1)
     down = lax.broadcasted_iota(jnp.int32, (count, count), 0)
-    owner_row, column_row = owners[...], columns[...]
+    owner_row, column_row = owners[0][...], columns[...]
 
     def as_column(row):
         size = row.shape[1]
@@ -261,11 +264,13 @@
     everything = alive((*axes[1], *axes[2], pair))
     write("end", jnp.sum(number(everything), axis=1, keepdims=True))
     over = jnp.zeros((1, 1), F32)
-    for done, most in usual.items():
-        mask = sum(1 << b for b in done)
-        group = (owner_row & mask) == (owner_col & mask)
-        taken = jnp.max(jnp.sum(number(group), axis=1, keepdims=True), axis=0, keepdims=True)
-        over = jnp.maximum(over, taken - most)
+    for row in [part[n : n + 1, :] for part in owners for n in range(part.shape[0])]:
+        column = as_column(row)
+        for done, most in usual.items():
+            mask = sum(1 << b for b in done)
+            group = (row & mask) == (column & mask)
+            taken = jnp.max(jnp.sum(number(group), axis=1, keepdims=True), axis=0, keepdims=True)
+            over = jnp.maximum(over, taken - most)
     write("fits", number(over <= 0.0))
 
 
@@ -286,6 +291,7 @@
         return jax.ShapeDtypeStruct(shape, dtype)
 
     with jax.named_scope("tokens"):
+        all_owners = [part.reshape(-1, block_count) for part in spread(owners)]
         own_chosen = call(
             functools.partial(select_rows, 0), "select_rows", [struct((places, token_count, side), BF16)],
             [SMEM] + [VMEM] * lax.axis_size("tensor").bit_length(), [place, *spread(tokens)],
@@ -338,18 +344,14 @@
         usual = {done: load_of(done) for done in settled if load_of(done) < most_of(done)}
         table = call(
             functools.partial(make_plan, axes, usual, own_blocks), "make_plan",
-            [struct((-(-len(rows) // 8) * 8, block_count), jnp.int32)], [SMEM] + [VMEM] * 3,
-            [later, owners, block_col, jnp.asarray(found)],
+            [struct((-(-len(rows) // 8) * 8, block_count), jnp.int32)], [SMEM] + [VMEM] * (2 + len(all_owners)),
+            [later, block_col, jnp.asarray(found), *all_owners],
         )[0]
-        fits = table[rows["fits"], :1]
-        for bit in range(lax.axis_size("tensor").bit_length() - 1):
-            fits = jnp.minimum(fits, swap(fits, "tensor", bit))
 
     with jax.named_scope("weights"):
         near_a, near_b, table = lax.optimization_barrier((near_a, near_b, table))
         a0, b0 = jnp.concatenate([current, near_a], 0), jnp.concatenate([far, near_b], 0)
         a1, b1 = swap(a0, "dp", bit_b), swap(b0, "dp", bit_a)
-        a1, b1, fits = lax.optimization_barrier((a1, b1, fits))
 
     with jax.named_scope("upstream"):
         other_up = [swap(sent, "dp", pair) for sent in sent_up]
@@ -382,8 +384,10 @@
                 part, up, (piece, start) = parts[at], other_up[at], firsts[at]
                 steps = [((*order, pair), ((), order[0])) for _, order in part]
                 shapes = [(load(order[:1]), share * quarter, side) for share, order in part]
-                body, spec = functools.partial(other_part, rows, steps, start), [SMEM] + [VMEM] * 4
-                args, scratch = [table, slope, other_chosen, up, grad], [pltpu.VMEM((places, 2 * up.shape[1], side), F32)]
+                body, spec = functools.partial(other_part, rows, steps, start), [VMEM] * 5
+                args = [table, slope, other_chosen, up, grad]
+                scratch = [pltpu.SMEM(table.shape, jnp.int32), pltpu.SemaphoreType.DMA]
+                scratch += [pltpu.VMEM((places, 2 * up.shape[1], side), F32)]
                 scratch += [pltpu.VMEM((block_count + room, *rest_of), F32) for room, *rest_of in shapes]
                 made = [(piece + i,) for i in range(len(part))]
             else:
@@ -407,7 +411,7 @@
 
     operands = (table, slope, other_chosen, other_up, grad)
     ends = reduce(load_of, *operands)
-    ends = lax.cond(fits[0] == 1, lambda ends, operands: ends, lambda ends, operands: reduce(most_of, *operands), ends, operands)
+    ends = lax.cond(table[rows["fits"], 0] == 1, lambda ends, operands: ends, lambda ends, operands: reduce(most_of, *operands), ends, operands)
     return call(
         functools.partial(finish, rows["end"], rows["pair"]), "finish", [struct((1, capacity, side, side), F32)],
         [VMEM] * (1 + len(ends)), [table, *ends],

time: 77.1 us -> 74.7 us (0.969)
  starting transfers between devices: 38.2 us -> 33.6 us
  waiting for transfers between devices: 15 us -> 18.7 us
  Pallas kernels: 16.5 us -> 15.5 us
    ppermute x27, starting transfers between devices: 38.2 us -> 33.6 us  [swap(): return lax.ppermute(value, axis, [(i, i ^ 1 << bit) for i in range(size)])]
    ppermute x27, waiting for transfers between devices: 15 us -> 18.7 us  [swap(): return lax.ppermute(value, axis, [(i, i ^ 1 << bit) for i in range(size)])]
    pallas_call x21, Pallas kernels: 16.5 us -> 15.5 us  [call(): pl.pallas_call(body, name=name, out_shape=tuple(outs), in_specs=in_specs,...]
  transfers between devices with their start and end apart: 27 -> 27, of which waited for: 13 -> 15; matrix products, arithmetic and copies ran while one was open for 2% -> 2% of each run, Pallas kernels for 20% -> 19%
where the time goes in v5:
time: 74.7 us; the launch traced here: 74.4 us
  starting transfers between devices  33.6 us (45%)
  waiting for transfers between devices  18.7 us (25%)
  Pallas kernels  15.5 us (21%)
  local copies, waits for them, and re-layouts  5.57 us (7%)
  between operations  0.96 us (1%)
    ppermute x27, starting transfers between devices, swap(): return lax.ppermute(value, axis, [(i, i ^ 1 << bit) for i in range(size)])  33.6 us
    ppermute x27, waiting for transfers between devices, swap(): return lax.ppermute(value, axis, [(i, i ^ 1 << bit) for i in range(size)])  18.7 us
    pallas_call x21, Pallas kernels, call(): pl.pallas_call(body, name=name, out_shape=tuple(outs), in_specs=in_specs,...  15.5 us
    unnamed x16, local copies, waits for them, and re-layouts  4.26 us
  transfers between devices with their start and end apart: 27, of which 15 were waited for; matrix products, arithmetic and copies ran while one was open for 2% of the time, Pallas kernels for 19%

profile of v5, /device:TPU:0, one launch (start us, length us, event | category | flops | bytes accessed | tf_op | source)
XLA Modules:
  0.0 74.4 jit_solution(16253962940568067418)
XLA Ops:
  0.0 0.5 collective-permute-start.23
  0.5 1.2 %copy-done = bf16[128,4096]{1,0:T(8,128)(2,1)S(1)} copy-done((bf16[128,4096]{1,0:T(8,128)(2,1)S(1)}, bf16[128,4096]{1,0:T(8,128)(2,1)}, u32[]{:S(2)}) %copy-start) | copy-done | bytes 1048600
  1.7 0.9 %copy-done.3 = f32[1,4,128,128]{3,2,1,0:T(8,128)S(1)} copy-done((f32[1,4,128,128]{3,2,1,0:T(8,128)S(1)}, f32[1,4,128,128]{3,2,1,0:T(8,128)}, u32[]{:S(2)}) %copy-start.3) | copy-done | bytes 262168
  2.8 2.6 %collective-permute-start.16 = (bf16[4,64,128]{2,1,0:T(8,128)(2,1)S(1)}, bf16[4,64,128]{2,1,0:T(8,128)(2,1)S(1)}, u32[]{:S(2)}, u32[]{:S(2)}) collective-permute-start(bf16[4,64,128]{2,1,0:T(8,128)(2,1)S(1)} %get-tuple-element.223), channel_id=1, source_target_pairs={{0,2},{2,0},{4,6},{6,4},{8,10},{10,8},{12,14},{14,12},{16,18},{18,... | collective-permute-start | bytes 196616 | tf_op jit(solution)/shard_map/weights/ppermute | solution.py:34
  5.3 0.7 %concatenate.12.place = s32[67]{0:T(128)S(1)} concatenate(s32[1]{0:T(128)} %bitcast, s32[1]{0:T(128)} %bitcast.1, s32[1]{0:T(128)} %bitcast.2, s32[32]{0:T(128)} %bitcast.14, s32[32]{0:T(128)} %bitcast.11), dimensions={0} | concatenate | bytes 536 | tf_op jit(solution)/shard_map/concatenate | solution.py:288
  6.1 1.2 %select_rows.1.refs_4_ = bf16[32,128,128]{2,1,0:T(8,128)(2,1)S(1)} custom-call(s32[67]{0:T(128)S(1)} %concatenate.12.place, bf16[1,128,4096]{2,1,0:T(8,128)(2,1)S(1)} %bitcast.10, bf16[1,128,4096]{2,1,0:T(8,128)(2,1)S(1)} %collective-permute-done.23.refs_1_), custom_call_target="tpu_custom_call" | custom-call | bytes 3145996 | tf_op jit(solution)/shard_map/tokens/select_rows/pallas_call | solution.py:20
  7.3 0.3 collective-permute-start.24
  7.6 0.5 collective-permute-done.16
  8.1 2.9 %collective-permute-start.17 = (bf16[8,64,128]{2,1,0:T(8,128)(2,1)S(1)}, bf16[8,64,128]{2,1,0:T(8,128)(2,1)S(1)}, u32[]{:S(2)}, u32[]{:S(2)}) collective-permute-start(bf16[8,64,128]{2,1,0:T(8,128)(2,1)S(1)} %pad_maximum_fusion), channel_id=1, source_target_pairs={{0,16},{2,18},{4,20},{6,22},{8,24},{10,26},{12,28},{14,30},{16,0},... | collective-permute-start | bytes 393224 | tf_op jit(solution)/shard_map/weights/ppermute | solution.py:34
  11.0 2.0 %copy-done.2 = bf16[128,14336]{1,0:T(8,128)(2,1)S(1)} copy-done((bf16[128,14336]{1,0:T(8,128)(2,1)S(1)}, bf16[128,14336]{1,0:T(8,128)(2,1)}, u32[]{:S(2)}) %copy-start.2) | copy-done | bytes 3670040
  13.1 3.6 %split_upstream.1 = (bf16[32,64,128]{2,1,0:T(8,128)(2,1)S(1)}, bf16[32,32,128]{2,1,0:T(8,128)(2,1)S(1)}, bf16[32,32,128]{2,1,0:T(8,128)(2,1)S(1)}) custom-call(s32[67]{0:T(128)S(1)} %concatenate.12.place, bf16[128,14336]{1,0:T(8,128)(2,1)S(1)} %copy-done.2), custom_call_target="tpu_custom_call" | custom-call | bytes 4718860 | tf_op jit(solution)/shard_map/weights/split_upstream/pallas_call | solution.py:20
  16.7 0.8 %make_plan.1.table.plan = s32[24,64]{1,0:T(8,128)S(1)} custom-call(s32[67]{0:T(128)S(1)} %concatenate.12.place, s32[1,32]{1,0:T(1,128)S(1)} %copy-done.4, s32[2,64]{1,0:T(2,128)S(1)} %copy-done.5, s32[1,64]{1,0:T(1,128)S(1)} %copy-done.6, s32[1,64]{1,0:T(1,128)S(1)} %bitcast.13), custom_call_target="tpu_custom_call" | custom-call | bytes 7564 | tf_op jit(solution)/shard_map/plan/make_plan/pallas_call | solution.py:20
  17.6 1.6 %collective-permute-start.18 = (bf16[8,64,128]{2,1,0:T(8,128)(2,1)S(1)}, bf16[8,64,128]{2,1,0:T(8,128)(2,1)S(1)}, u32[]{:S(2)}, u32[]{:S(2)}) collective-permute-start(bf16[8,64,128]{2,1,0:T(8,128)(2,1)S(1)} %pad_maximum_fusion), channel_id=1, source_target_pairs={{0,4},{2,6},{4,0},{6,2},{8,12},{10,14},{12,8},{14,10},{16,20},{18,... | collective-permute-start | bytes 393224 | tf_op jit(solution)/shard_map/weights/ppermute | solution.py:34
  19.2 1.6 %collective-permute-start.19 = (bf16[8,64,128]{2,1,0:T(8,128)(2,1)S(1)}, bf16[8,64,128]{2,1,0:T(8,128)(2,1)S(1)}, u32[]{:S(2)}, u32[]{:S(2)}) collective-permute-start(bf16[8,64,128]{2,1,0:T(8,128)(2,1)S(1)} %collective-permute-done.17), channel_id=1, source_target_pairs={{0,8},{2,10},{4,12},{6,14},{8,0},{10,2},{12,4},{14,6},{16,24},{18,... | collective-permute-start | bytes 393224 | tf_op jit(solution)/shard_map/weights/ppermute | solution.py:34
  20.8 2.8 %collective-permute-done.18 = bf16[8,64,128]{2,1,0:T(8,128)(2,1)S(1)} collective-permute-done((bf16[8,64,128]{2,1,0:T(8,128)(2,1)S(1)}, bf16[8,64,128]{2,1,0:T(8,128)(2,1)S(1)}, u32[]{:S(2)}, u32[]{:S(2)}) %collective-permute-start.18) | collective-permute-done | bytes 131104 | tf_op jit(solution)/shard_map/weights/ppermute | solution.py:34
  23.5 1.2 %collective-permute-done.19 = bf16[8,64,128]{2,1,0:T(8,128)(2,1)S(1)} collective-permute-done((bf16[8,64,128]{2,1,0:T(8,128)(2,1)S(1)}, bf16[8,64,128]{2,1,0:T(8,128)(2,1)S(1)}, u32[]{:S(2)}, u32[]{:S(2)}) %collective-permute-start.19) | collective-permute-done | bytes 131104 | tf_op jit(solution)/shard_map/weights/ppermute | solution.py:34
  24.8 0.6 collective-permute-start.22
  25.4 1.6 %collective-permute-start.21 = (bf16[16,64,128]{2,1,0:T(8,128)(2,1)S(1)}, bf16[16,64,128]{2,1,0:T(8,128)(2,1)S(1)}, u32[]{:S(2)}, u32[]{:S(2)}) collective-permute-start(bf16[16,64,128]{2,1,0:T(8,128)(2,1)S(1)} %constant_dynamic-update-slice_fusion.refs_0_), channel_id=1, source_target_pairs={{0,8},{2,10},{4,12},{6,14},{8,0},{10,2},{12,4},{14,6},{16,24},{18,... | collective-permute-start | bytes 786440 | tf_op jit(solution)/shard_map/weights/ppermute | solution.py:34
  27.0 1.5 %collective-permute-start.25 = (bf16[32,32,128]{2,1,0:T(8,128)(2,1)S(1)}, bf16[32,32,128]{2,1,0:T(8,128)(2,1)S(1)}, u32[]{:S(2)}, u32[]{:S(2)}) collective-permute-start(bf16[32,32,128]{2,1,0:T(8,128)(2,1)S(1)} %get-tuple-element.166), channel_id=1, source_target_pairs={{0,2},{2,0},{4,6},{6,4},{8,10},{10,8},{12,14},{14,12},{16,18},{18,... | collective-permute-start | bytes 786440 | tf_op jit(solution)/shard_map/upstream/ppermute | solution.py:34
  28.5 0.5 collective-permute-start.26
  29.1 3.4 %collective-permute-done.22.refs_3_ = bf16[16,64,128]{2,1,0:T(8,128)(2,1)S(1)} collective-permute-done((bf16[16,64,128]{2,1,0:T(8,128)(2,1)S(1)}, bf16[16,64,128]{2,1,0:T(8,128)(2,1)S(1)}, u32[]{:S(2)}, u32[]{:S(2)}) %collective-permute-start.22) | collective-permute-done | bytes 262176 | tf_op jit(solution)/shard_map/weights/ppermute | solution.py:34
  32.5 0.4 collective-permute-done.21.refs_1_
  32.9 2.7 %own_part.1 = (bf16[32,128,128]{2,1,0:T(8,128)(2,1)S(1)}, f32[32,128,128]{2,1,0:T(8,128)S(1)}) custom-call(s32[24,64]{1,0:T(8,128)S(1)} %make_plan.1.table.plan, bf16[16,64,128]{2,1,0:T(8,128)(2,1)S(1)} %constant_dynamic-update-slice_fusion.refs_0_, bf16[16,64,128]{2,1,0:T(8,128)(2,1)S(1)} %collective-permute-done.21.refs_1_, ...), custom_call_target="tpu_custom_call" | custom-call | flops 268435456 | bytes 5773312 | tf_op jit(solution)/shard_map/own_tokens/own_part/pallas_call | solution.py:20
  35.6 2.2 %other_slopes.1.slope = f32[32,128,128]{2,1,0:T(8,128)S(1)} custom-call(s32[24,64]{1,0:T(8,128)S(1)} %make_plan.1.table.plan, bf16[32,128,128]{2,1,0:T(8,128)(2,1)S(1)} %get-tuple-element.165.weights, bf16[32,128,128]{2,1,0:T(8,128)(2,1)S(1)} %collective-permute-done.24.other_tokens), custom_call_target="tpu_custom_call" | custom-call | flops 134217728 | bytes 4200448 | tf_op jit(solution)/shard_map/other_tokens/other_slopes/pallas_call | solution.py:20
  37.8 1.2 %collective-permute-done.25.other_up = bf16[32,32,128]{2,1,0:T(8,128)(2,1)S(1)} collective-permute-done((bf16[32,32,128]{2,1,0:T(8,128)(2,1)S(1)}, bf16[32,32,128]{2,1,0:T(8,128)(2,1)S(1)}, u32[]{:S(2)}, u32[]{:S(2)}) %collective-permute-start.25) | collective-permute-done | bytes 262176 | tf_op jit(solution)/shard_map/upstream/ppermute | solution.py:34
  39.0 0.9 %other_part.6 = (bf16[44,16,128]{2,1,0:T(8,128)(2,1)S(1)}, f32[44,16,128]{2,1,0:T(8,128)S(1)}, bf16[44,16,128]{2,1,0:T(8,128)(2,1)S(1)}, f32[44,16,128]{2,1,0:T(8,128)S(1)}) custom-call(s32[24,64]{1,0:T(8,128)S(1)} %make_plan.1.table.plan, f32[32,128,128]{2,1,0:T(8,128)S(1)} %other_slopes.1.slope, ...), custom_call_target="tpu_custom_call" | custom-call | flops 67108864 | bytes 6592512 | tf_op jit(solution)/shard_map/other_part/pallas_call | solution.py:20
  39.9 1.6 %collective-permute-start.27 = (bf16[44,16,128]{2,1,0:T(8,128)(2,1)S(1)}, bf16[44,16,128]{2,1,0:T(8,128)(2,1)S(1)}, u32[]{:S(2)}, u32[]{:S(2)}) collective-permute-start(bf16[44,16,128]{2,1,0:T(8,128)(2,1)S(1)} %get-tuple-element.170), channel_id=1, source_target_pairs={{0,8},{2,10},{4,12},{6,14},{8,0},{10,2},{12,4},{14,6},{16,24},{18,... | collective-permute-start | bytes 540680 | tf_op jit(solution)/shard_map/ppermute | solution.py:34
  41.6 1.5 %collective-permute-start.31 = (bf16[44,16,128]{2,1,0:T(8,128)(2,1)S(1)}, bf16[44,16,128]{2,1,0:T(8,128)(2,1)S(1)}, u32[]{:S(2)}, u32[]{:S(2)}) collective-permute-start(bf16[44,16,128]{2,1,0:T(8,128)(2,1)S(1)} %get-tuple-element.180), channel_id=1, source_target_pairs={{0,4},{2,6},{4,0},{6,2},{8,12},{10,14},{12,8},{14,10},{16,20},{18,... | collective-permute-start | bytes 540680 | tf_op jit(solution)/shard_map/ppermute | solution.py:34
  43.1 0.8 %collective-permute-done.26.other_up = bf16[32,32,128]{2,1,0:T(8,128)(2,1)S(1)} collective-permute-done((bf16[32,32,128]{2,1,0:T(8,128)(2,1)S(1)}, bf16[32,32,128]{2,1,0:T(8,128)(2,1)S(1)}, u32[]{:S(2)}, u32[]{:S(2)}) %collective-permute-start.26) | collective-permute-done | bytes 262176 | tf_op jit(solution)/shard_map/upstream/ppermute | solution.py:34
  43.9 0.9 %other_part.7 = (bf16[44,16,128]{2,1,0:T(8,128)(2,1)S(1)}, f32[44,16,128]{2,1,0:T(8,128)S(1)}, bf16[44,16,128]{2,1,0:T(8,128)(2,1)S(1)}, f32[44,16,128]{2,1,0:T(8,128)S(1)}) custom-call(s32[24,64]{1,0:T(8,128)S(1)} %make_plan.1.table.plan, f32[32,128,128]{2,1,0:T(8,128)S(1)} %other_slopes.1.slope, ...), custom_call_target="tpu_custom_call" | custom-call | flops 67108864 | bytes 6592512 | tf_op jit(solution)/shard_map/other_part/pallas_call | solution.py:20
  44.8 1.6 %collective-permute-start.30 = (bf16[44,16,128]{2,1,0:T(8,128)(2,1)S(1)}, bf16[44,16,128]{2,1,0:T(8,128)(2,1)S(1)}, u32[]{:S(2)}, u32[]{:S(2)}) collective-permute-start(bf16[44,16,128]{2,1,0:T(8,128)(2,1)S(1)} %get-tuple-element.178), channel_id=1, source_target_pairs={{0,8},{2,10},{4,12},{6,14},{8,0},{10,2},{12,4},{14,6},{16,24},{18,... | collective-permute-start | bytes 540680 | tf_op jit(solution)/shard_map/ppermute | solution.py:34
  46.5 1.5 %collective-permute-start.29 = (bf16[44,16,128]{2,1,0:T(8,128)(2,1)S(1)}, bf16[44,16,128]{2,1,0:T(8,128)(2,1)S(1)}, u32[]{:S(2)}, u32[]{:S(2)}) collective-permute-start(bf16[44,16,128]{2,1,0:T(8,128)(2,1)S(1)} %get-tuple-element.177), channel_id=1, source_target_pairs={{0,4},{2,6},{4,0},{6,2},{8,12},{10,14},{12,8},{14,10},{16,20},{18,... | collective-permute-start | bytes 540680 | tf_op jit(solution)/shard_map/ppermute | solution.py:34
  48.0 0.2 combine.36
  48.2 0.6 collective-permute-start.28
  48.7 0.2 combine.37
  48.9 2.7 %collective-permute-start.35 = (bf16[28,16,128]{2,1,0:T(8,128)(2,1)S(1)}, bf16[28,16,128]{2,1,0:T(8,128)(2,1)S(1)}, u32[]{:S(2)}, u32[]{:S(2)}) collective-permute-start(bf16[28,16,128]{2,1,0:T(8,128)(2,1)S(1)} %get-tuple-element.192), channel_id=1, source_target_pairs={{0,16},{2,18},{4,20},{6,22},{8,24},{10,26},{12,28},{14,30},{16,0},... | collective-permute-start | bytes 344072 | tf_op jit(solution)/shard_map/ppermute | solution.py:34
  51.6 0.2 combine.38
  51.7 1.6 %collective-permute-start.34 = (bf16[28,16,128]{2,1,0:T(8,128)(2,1)S(1)}, bf16[28,16,128]{2,1,0:T(8,128)(2,1)S(1)}, u32[]{:S(2)}, u32[]{:S(2)}) collective-permute-start(bf16[28,16,128]{2,1,0:T(8,128)(2,1)S(1)} %get-tuple-element.191), channel_id=1, source_target_pairs={{0,4},{2,6},{4,0},{6,2},{8,12},{10,14},{12,8},{14,10},{16,20},{18,... | collective-permute-start | bytes 344072 | tf_op jit(solution)/shard_map/ppermute | solution.py:34
  53.3 0.6 collective-permute-done.29.refs_1_
  53.9 0.2 combine.39
  54.0 0.3 collective-permute-start.33
  54.3 1.4 %collective-permute-done.28.refs_1_ = bf16[28,16,128]{2,1,0:T(8,128)(2,1)S(1)} collective-permute-done((bf16[28,16,128]{2,1,0:T(8,128)(2,1)S(1)}, bf16[28,16,128]{2,1,0:T(8,128)(2,1)S(1)}, u32[]{:S(2)}, u32[]{:S(2)}) %collective-permute-start.28) | collective-permute-done | bytes 114720 | tf_op jit(solution)/shard_map/ppermute | solution.py:34
  55.8 0.1 combine.40
  55.9 2.7 %collective-permute-start.32 = (bf16[20,16,128]{2,1,0:T(8,128)(2,1)S(1)}, bf16[20,16,128]{2,1,0:T(8,128)(2,1)S(1)}, u32[]{:S(2)}, u32[]{:S(2)}) collective-permute-start(bf16[20,16,128]{2,1,0:T(8,128)(2,1)S(1)} %get-tuple-element.189), channel_id=1, source_target_pairs={{0,16},{2,18},{4,20},{6,22},{8,24},{10,26},{12,28},{14,30},{16,0},... | collective-permute-start | bytes 245768 | tf_op jit(solution)/shard_map/ppermute | solution.py:34
  58.6 0.1 combine.41
  58.7 0.5 collective-permute-start.37
  59.3 0.1 combine.42
  59.4 0.4 collective-permute-start.39
  59.8 1.8 %collective-permute-done.33.refs_1_ = bf16[28,16,128]{2,1,0:T(8,128)(2,1)S(1)} collective-permute-done((bf16[28,16,128]{2,1,0:T(8,128)(2,1)S(1)}, bf16[28,16,128]{2,1,0:T(8,128)(2,1)S(1)}, u32[]{:S(2)}, u32[]{:S(2)}) %collective-permute-start.33) | collective-permute-done | bytes 114720 | tf_op jit(solution)/shard_map/ppermute | solution.py:34
  61.7 0.1 combine.43
  61.8 0.8 %collective-permute-start.41 = (bf16[20,16,128]{2,1,0:T(8,128)(2,1)S(1)}, bf16[20,16,128]{2,1,0:T(8,128)(2,1)S(1)}, u32[]{:S(2)}, u32[]{:S(2)}) collective-permute-start(bf16[20,16,128]{2,1,0:T(8,128)(2,1)S(1)} %get-tuple-element.210), channel_id=1, source_target_pairs={{0,16},{2,18},{4,20},{6,22},{8,24},{10,26},{12,28},{14,30},{16,0},... | collective-permute-start | bytes 245768 | tf_op jit(solution)/shard_map/ppermute | solution.py:34
  62.6 1.7 %collective-permute-done.32.refs_1_ = bf16[20,16,128]{2,1,0:T(8,128)(2,1)S(1)} collective-permute-done((bf16[20,16,128]{2,1,0:T(8,128)(2,1)S(1)}, bf16[20,16,128]{2,1,0:T(8,128)(2,1)S(1)}, u32[]{:S(2)}, u32[]{:S(2)}) %collective-permute-start.32) | collective-permute-done | bytes 81952 | tf_op jit(solution)/shard_map/ppermute | solution.py:34
  64.3 0.1 combine.44
  64.4 0.1 combine.45
  64.6 0.6 collective-permute-start.38
  65.2 1.5 %collective-permute-start.36 = (bf16[12,16,128]{2,1,0:T(8,128)(2,1)S(1)}, bf16[12,16,128]{2,1,0:T(8,128)(2,1)S(1)}, u32[]{:S(2)}, u32[]{:S(2)}) collective-permute-start(bf16[12,16,128]{2,1,0:T(8,128)(2,1)S(1)} %get-tuple-element.201), channel_id=1, source_target_pairs={{0,2},{2,0},{4,6},{6,4},{8,10},{10,8},{12,14},{14,12},{16,18},{18,... | collective-permute-start | bytes 147464 | tf_op jit(solution)/shard_map/ppermute | solution.py:34
  66.7 0.7 collective-permute-done.39.refs_1_
  67.5 0.7 collective-permute-done.41.refs_1_
  68.4 0.6 collective-permute-start.42
  69.0 1.5 %collective-permute-start.40 = (bf16[12,16,128]{2,1,0:T(8,128)(2,1)S(1)}, bf16[12,16,128]{2,1,0:T(8,128)(2,1)S(1)}, u32[]{:S(2)}, u32[]{:S(2)}) collective-permute-start(bf16[12,16,128]{2,1,0:T(8,128)(2,1)S(1)} %get-tuple-element.209), channel_id=1, source_target_pairs={{0,2},{2,0},{4,6},{6,4},{8,10},{10,8},{12,14},{14,12},{16,18},{18,... | collective-permute-start | bytes 147464 | tf_op jit(solution)/shard_map/ppermute | solution.py:34
  70.5 0.5 slice.3
  71.7 0.9 %collective-permute-done.42 = bf16[12,16,128]{2,1,0:T(8,128)(2,1)S(1)} collective-permute-done((bf16[12,16,128]{2,1,0:T(8,128)(2,1)S(1)}, bf16[12,16,128]{2,1,0:T(8,128)(2,1)S(1)}, u32[]{:S(2)}, u32[]{:S(2)}) %collective-permute-start.42) | collective-permute-done | bytes 49184 | tf_op jit(solution)/shard_map/ppermute | solution.py:34
  72.6 0.5 collective-permute-done.40
  73.2 1.3 %finish.1 = f32[1,12,128,128]{3,2,1,0:T(8,128)} custom-call(s32[24,64]{1,0:T(8,128)S(1)} %make_plan.1.table.plan, f32[12,16,128]{2,1,0:T(8,128)S(1)} %get-tuple-element.214.refs_0_, bf16[12,16,128]{2,1,0:T(8,128)(2,1)S(1)} %get-tuple-element.215.refs_1_, f32[12,16,128]{2,1,0:T(8,128)S(1)} %get-tuple-element.216.refs_2_, ...), custom_call_target="tpu_custom_call" | custom-call | bytes 1382400 | tf_op jit(solution)/shard_map/finish/pallas_call | solution.py:20
  (38 shorter events, 0.6 us)
Async XLA Ops:
  0.0 6.1 %collective-permute-start.23 = (bf16[1,128,4096]{2,1,0:T(8,128)(2,1)}, bf16[1,128,4096]{2,1,0:T(8,128)(2,1)S(1)}, u32[]{:S(2)}, u32[]{:S(2)}) collective-permute-start(bf16[1,128,4096]{2,1,0:T(8,128)(2,1)} %bitcast.9), channel_id=1, source_target_pairs={{0,1},{1,0},{2,3},{3,2},{4,5},{5,4},{6,7},{7,6},{8,9},{9,8},{10,11... | collective-permute-start | bytes 3145736 | tf_op jit(solution)/shard_map/tokens/ppermute | solution.py:34
  0.5 1.2 %copy-start = (bf16[128,4096]{1,0:T(8,128)(2,1)S(1)}, bf16[128,4096]{1,0:T(8,128)(2,1)}, u32[]{:S(2)}) copy-start(bf16[128,4096]{1,0:T(8,128)(2,1)} %tokens.1) | copy-start | bytes 3145732
  1.7 0.9 %copy-start.3 = (f32[1,4,128,128]{3,2,1,0:T(8,128)S(1)}, f32[1,4,128,128]{3,2,1,0:T(8,128)}, u32[]{:S(2)}) copy-start(f32[1,4,128,128]{3,2,1,0:T(8,128)} %masters.1) | copy-start | bytes 786436
  2.6 3.5 %copy-start.1 = (bf16[128,4096]{1,0:T(8,128)(2,1)S(1)}, bf16[128,4096]{1,0:T(8,128)(2,1)}, u32[]{:S(2)}) copy-start(bf16[128,4096]{1,0:T(8,128)(2,1)} %tokens.1) | copy-start | bytes 3145732
  2.7 8.3 %copy-start.6 = (s32[1,64]{1,0:T(1,128)S(1)}, s32[1,64]{1,0:T(1,128)}, u32[]{:S(2)}) copy-start(s32[1,64]{1,0:T(1,128)} %refs_0_.1) | copy-start | bytes 772
  2.8 5.3 %collective-permute-start.16 = (bf16[4,64,128]{2,1,0:T(8,128)(2,1)S(1)}, bf16[4,64,128]{2,1,0:T(8,128)(2,1)S(1)}, u32[]{:S(2)}, u32[]{:S(2)}) collective-permute-start(bf16[4,64,128]{2,1,0:T(8,128)(2,1)S(1)} %get-tuple-element.223), channel_id=1, source_target_pairs={{0,2},{2,0},{4,6},{6,4},{8,10},{10,8},{12,14},{14,12},{16,18},{18,... | collective-permute-start | bytes 196616 | tf_op jit(solution)/shard_map/weights/ppermute | solution.py:34
  7.3 9.4 %copy-start.4 = (s32[1,32]{1,0:T(1,128)S(1)}, s32[1,32]{1,0:T(1,128)}, u32[]{:S(2)}) copy-start(s32[1,32]{1,0:T(1,128)} %columns.1) | copy-start | bytes 388
  7.3 9.4 %copy-start.5 = (s32[2,64]{1,0:T(2,128)S(1)}, s32[2,64]{1,0:T(2,128)}, u32[]{:S(2)}) copy-start(s32[2,64]{1,0:T(2,128)} %constant.16.clone.found) | copy-start | bytes 1540
  7.3 28.3 %collective-permute-start.24 = (bf16[32,128,128]{2,1,0:T(8,128)(2,1)S(1)}, bf16[32,128,128]{2,1,0:T(8,128)(2,1)S(1)}, u32[]{:S(2)}, u32[]{:S(2)}) collective-permute-start(bf16[32,128,128]{2,1,0:T(8,128)(2,1)S(1)} %select_rows.1.refs_4_), channel_id=1, source_target_pairs={{0,2},{2,0},{4,6},{6,4},{8,10},{10,8},{12,14},{14,12},{16,18},{18,... | collective-permute-start | bytes 3145736 | tf_op jit(solution)/shard_map/weights/ppermute | solution.py:34
  8.1 9.4 %collective-permute-start.17 = (bf16[8,64,128]{2,1,0:T(8,128)(2,1)S(1)}, bf16[8,64,128]{2,1,0:T(8,128)(2,1)S(1)}, u32[]{:S(2)}, u32[]{:S(2)}) collective-permute-start(bf16[8,64,128]{2,1,0:T(8,128)(2,1)S(1)} %pad_maximum_fusion), channel_id=1, source_target_pairs={{0,16},{2,18},{4,20},{6,22},{8,24},{10,26},{12,28},{14,30},{16,0},... | collective-permute-start | bytes 393224 | tf_op jit(solution)/shard_map/weights/ppermute | solution.py:34
  11.0 5.7 %collective-permute-start.20 = (s32[1,1,64]{2,1,0:T(1,128)S(1)}, s32[1,1,64]{2,1,0:T(1,128)S(1)}, u32[]{:S(2)}, u32[]{:S(2)}) collective-permute-start(s32[1,1,64]{2,1,0:T(1,128)S(1)} %bitcast.12), channel_id=1, source_target_pairs={{0,1},{1,0},{2,3},{3,2},{4,5},{5,4},{6,7},{7,6},{8,9},{9,8},{10,11... | collective-permute-start | bytes 776 | tf_op jit(solution)/shard_map/tokens/ppermute | solution.py:34
  11.0 2.0 %copy-start.2 = (bf16[128,14336]{1,0:T(8,128)(2,1)S(1)}, bf16[128,14336]{1,0:T(8,128)(2,1)}, u32[]{:S(2)}) copy-start(bf16[128,14336]{1,0:T(8,128)(2,1)} %grad.1) | copy-start | bytes 11010052
  17.6 6.0 %collective-permute-start.18 = (bf16[8,64,128]{2,1,0:T(8,128)(2,1)S(1)}, bf16[8,64,128]{2,1,0:T(8,128)(2,1)S(1)}, u32[]{:S(2)}, u32[]{:S(2)}) collective-permute-start(bf16[8,64,128]{2,1,0:T(8,128)(2,1)S(1)} %pad_maximum_fusion), channel_id=1, source_target_pairs={{0,4},{2,6},{4,0},{6,2},{8,12},{10,14},{12,8},{14,10},{16,20},{18,... | collective-permute-start | bytes 393224 | tf_op jit(solution)/shard_map/weights/ppermute | solution.py:34
  19.2 5.6 %collective-permute-start.19 = (bf16[8,64,128]{2,1,0:T(8,128)(2,1)S(1)}, bf16[8,64,128]{2,1,0:T(8,128)(2,1)S(1)}, u32[]{:S(2)}, u32[]{:S(2)}) collective-permute-start(bf16[8,64,128]{2,1,0:T(8,128)(2,1)S(1)} %collective-permute-done.17), channel_id=1, source_target_pairs={{0,8},{2,10},{4,12},{6,14},{8,0},{10,2},{12,4},{14,6},{16,24},{18,... | collective-permute-start | bytes 393224 | tf_op jit(solution)/shard_map/weights/ppermute | solution.py:34
  24.8 7.7 %collective-permute-start.22 = (bf16[16,64,128]{2,1,0:T(8,128)(2,1)S(1)}, bf16[16,64,128]{2,1,0:T(8,128)(2,1)S(1)}, u32[]{:S(2)}, u32[]{:S(2)}) collective-permute-start(bf16[16,64,128]{2,1,0:T(8,128)(2,1)S(1)} %constant_dynamic-update-slice_fusion.2.refs_2_), channel_id=1, source_target_pairs={{0,4},{2,6},{4,0},{6,2},{8,12},{10,14},{12,8},{14,10},{16,20},{18,... | collective-permute-start | bytes 786440 | tf_op jit(solution)/shard_map/weights/ppermute | solution.py:34
  25.4 7.5 %collective-permute-start.21 = (bf16[16,64,128]{2,1,0:T(8,128)(2,1)S(1)}, bf16[16,64,128]{2,1,0:T(8,128)(2,1)S(1)}, u32[]{:S(2)}, u32[]{:S(2)}) collective-permute-start(bf16[16,64,128]{2,1,0:T(8,128)(2,1)S(1)} %constant_dynamic-update-slice_fusion.refs_0_), channel_id=1, source_target_pairs={{0,8},{2,10},{4,12},{6,14},{8,0},{10,2},{12,4},{14,6},{16,24},{18,... | collective-permute-start | bytes 786440 | tf_op jit(solution)/shard_map/weights/ppermute | solution.py:34
  27.0 12.0 %collective-permute-start.25 = (bf16[32,32,128]{2,1,0:T(8,128)(2,1)S(1)}, bf16[32,32,128]{2,1,0:T(8,128)(2,1)S(1)}, u32[]{:S(2)}, u32[]{:S(2)}) collective-permute-start(bf16[32,32,128]{2,1,0:T(8,128)(2,1)S(1)} %get-tuple-element.166), channel_id=1, source_target_pairs={{0,2},{2,0},{4,6},{6,4},{8,10},{10,8},{12,14},{14,12},{16,18},{18,... | collective-permute-start | bytes 786440 | tf_op jit(solution)/shard_map/upstream/ppermute | solution.py:34
  28.5 15.4 %collective-permute-start.26 = (bf16[32,32,128]{2,1,0:T(8,128)(2,1)S(1)}, bf16[32,32,128]{2,1,0:T(8,128)(2,1)S(1)}, u32[]{:S(2)}, u32[]{:S(2)}) collective-permute-start(bf16[32,32,128]{2,1,0:T(8,128)(2,1)S(1)} %get-tuple-element.168), channel_id=1, source_target_pairs={{0,2},{2,0},{4,6},{6,4},{8,10},{10,8},{12,14},{14,12},{16,18},{18,... | collective-permute-start | bytes 786440 | tf_op jit(solution)/shard_map/upstream/ppermute | solution.py:34
  39.9 8.1 %collective-permute-start.27 = (bf16[44,16,128]{2,1,0:T(8,128)(2,1)S(1)}, bf16[44,16,128]{2,1,0:T(8,128)(2,1)S(1)}, u32[]{:S(2)}, u32[]{:S(2)}) collective-permute-start(bf16[44,16,128]{2,1,0:T(8,128)(2,1)S(1)} %get-tuple-element.170), channel_id=1, source_target_pairs={{0,8},{2,10},{4,12},{6,14},{8,0},{10,2},{12,4},{14,6},{16,24},{18,... | collective-permute-start | bytes 540680 | tf_op jit(solution)/shard_map/ppermute | solution.py:34
  41.6 7.2 %collective-permute-start.31 = (bf16[44,16,128]{2,1,0:T(8,128)(2,1)S(1)}, bf16[44,16,128]{2,1,0:T(8,128)(2,1)S(1)}, u32[]{:S(2)}, u32[]{:S(2)}) collective-permute-start(bf16[44,16,128]{2,1,0:T(8,128)(2,1)S(1)} %get-tuple-element.180), channel_id=1, source_target_pairs={{0,4},{2,6},{4,0},{6,2},{8,12},{10,14},{12,8},{14,10},{16,20},{18,... | collective-permute-start | bytes 540680 | tf_op jit(solution)/shard_map/ppermute | solution.py:34
  44.8 6.7 %collective-permute-start.30 = (bf16[44,16,128]{2,1,0:T(8,128)(2,1)S(1)}, bf16[44,16,128]{2,1,0:T(8,128)(2,1)S(1)}, u32[]{:S(2)}, u32[]{:S(2)}) collective-permute-start(bf16[44,16,128]{2,1,0:T(8,128)(2,1)S(1)} %get-tuple-element.178), channel_id=1, source_target_pairs={{0,8},{2,10},{4,12},{6,14},{8,0},{10,2},{12,4},{14,6},{16,24},{18,... | collective-permute-start | bytes 540680 | tf_op jit(solution)/shard_map/ppermute | solution.py:34
  46.5 7.4 %collective-permute-start.29 = (bf16[44,16,128]{2,1,0:T(8,128)(2,1)S(1)}, bf16[44,16,128]{2,1,0:T(8,128)(2,1)S(1)}, u32[]{:S(2)}, u32[]{:S(2)}) collective-permute-start(bf16[44,16,128]{2,1,0:T(8,128)(2,1)S(1)} %get-tuple-element.177), channel_id=1, source_target_pairs={{0,4},{2,6},{4,0},{6,2},{8,12},{10,14},{12,8},{14,10},{16,20},{18,... | collective-permute-start | bytes 540680 | tf_op jit(solution)/shard_map/ppermute | solution.py:34
  48.2 7.6 %collective-permute-start.28 = (bf16[28,16,128]{2,1,0:T(8,128)(2,1)S(1)}, bf16[28,16,128]{2,1,0:T(8,128)(2,1)S(1)}, u32[]{:S(2)}, u32[]{:S(2)}) collective-permute-start(bf16[28,16,128]{2,1,0:T(8,128)(2,1)S(1)} %get-tuple-element.175), channel_id=1, source_target_pairs={{0,4},{2,6},{4,0},{6,2},{8,12},{10,14},{12,8},{14,10},{16,20},{18,... | collective-permute-start | bytes 344072 | tf_op jit(solution)/shard_map/ppermute | solution.py:34
  48.9 9.7 %collective-permute-start.35 = (bf16[28,16,128]{2,1,0:T(8,128)(2,1)S(1)}, bf16[28,16,128]{2,1,0:T(8,128)(2,1)S(1)}, u32[]{:S(2)}, u32[]{:S(2)}) collective-permute-start(bf16[28,16,128]{2,1,0:T(8,128)(2,1)S(1)} %get-tuple-element.192), channel_id=1, source_target_pairs={{0,16},{2,18},{4,20},{6,22},{8,24},{10,26},{12,28},{14,30},{16,0},... | collective-permute-start | bytes 344072 | tf_op jit(solution)/shard_map/ppermute | solution.py:34
  51.7 7.5 %collective-permute-start.34 = (bf16[28,16,128]{2,1,0:T(8,128)(2,1)S(1)}, bf16[28,16,128]{2,1,0:T(8,128)(2,1)S(1)}, u32[]{:S(2)}, u32[]{:S(2)}) collective-permute-start(bf16[28,16,128]{2,1,0:T(8,128)(2,1)S(1)} %get-tuple-element.191), channel_id=1, source_target_pairs={{0,4},{2,6},{4,0},{6,2},{8,12},{10,14},{12,8},{14,10},{16,20},{18,... | collective-permute-start | bytes 344072 | tf_op jit(solution)/shard_map/ppermute | solution.py:34
  54.0 7.6 %collective-permute-start.33 = (bf16[28,16,128]{2,1,0:T(8,128)(2,1)S(1)}, bf16[28,16,128]{2,1,0:T(8,128)(2,1)S(1)}, u32[]{:S(2)}, u32[]{:S(2)}) collective-permute-start(bf16[28,16,128]{2,1,0:T(8,128)(2,1)S(1)} %get-tuple-element.190), channel_id=1, source_target_pairs={{0,8},{2,10},{4,12},{6,14},{8,0},{10,2},{12,4},{14,6},{16,24},{18,... | collective-permute-start | bytes 344072 | tf_op jit(solution)/shard_map/ppermute | solution.py:34
  55.9 8.4 %collective-permute-start.32 = (bf16[20,16,128]{2,1,0:T(8,128)(2,1)S(1)}, bf16[20,16,128]{2,1,0:T(8,128)(2,1)S(1)}, u32[]{:S(2)}, u32[]{:S(2)}) collective-permute-start(bf16[20,16,128]{2,1,0:T(8,128)(2,1)S(1)} %get-tuple-element.189), channel_id=1, source_target_pairs={{0,16},{2,18},{4,20},{6,22},{8,24},{10,26},{12,28},{14,30},{16,0},... | collective-permute-start | bytes 245768 | tf_op jit(solution)/shard_map/ppermute | solution.py:34
  58.7 5.7 %collective-permute-start.37 = (bf16[20,16,128]{2,1,0:T(8,128)(2,1)S(1)}, bf16[20,16,128]{2,1,0:T(8,128)(2,1)S(1)}, u32[]{:S(2)}, u32[]{:S(2)}) collective-permute-start(bf16[20,16,128]{2,1,0:T(8,128)(2,1)S(1)} %get-tuple-element.202), channel_id=1, source_target_pairs={{0,8},{2,10},{4,12},{6,14},{8,0},{10,2},{12,4},{14,6},{16,24},{18,... | collective-permute-start | bytes 245768 | tf_op jit(solution)/shard_map/ppermute | solution.py:34
  59.4 8.0 %collective-permute-start.39 = (bf16[20,16,128]{2,1,0:T(8,128)(2,1)S(1)}, bf16[20,16,128]{2,1,0:T(8,128)(2,1)S(1)}, u32[]{:S(2)}, u32[]{:S(2)}) collective-permute-start(bf16[20,16,128]{2,1,0:T(8,128)(2,1)S(1)} %get-tuple-element.206), channel_id=1, source_target_pairs={{0,16},{2,18},{4,20},{6,22},{8,24},{10,26},{12,28},{14,30},{16,0},... | collective-permute-start | bytes 245768 | tf_op jit(solution)/shard_map/ppermute | solution.py:34
  61.8 6.5 %collective-permute-start.41 = (bf16[20,16,128]{2,1,0:T(8,128)(2,1)S(1)}, bf16[20,16,128]{2,1,0:T(8,128)(2,1)S(1)}, u32[]{:S(2)}, u32[]{:S(2)}) collective-permute-start(bf16[20,16,128]{2,1,0:T(8,128)(2,1)S(1)} %get-tuple-element.210), channel_id=1, source_target_pairs={{0,16},{2,18},{4,20},{6,22},{8,24},{10,26},{12,28},{14,30},{16,0},... | collective-permute-start | bytes 245768 | tf_op jit(solution)/shard_map/ppermute | solution.py:34
  64.6 7.1 %collective-permute-start.38 = (bf16[12,16,128]{2,1,0:T(8,128)(2,1)S(1)}, bf16[12,16,128]{2,1,0:T(8,128)(2,1)S(1)}, u32[]{:S(2)}, u32[]{:S(2)}) collective-permute-start(bf16[12,16,128]{2,1,0:T(8,128)(2,1)S(1)} %get-tuple-element.205), channel_id=1, source_target_pairs={{0,2},{2,0},{4,6},{6,4},{8,10},{10,8},{12,14},{14,12},{16,18},{18,... | collective-permute-start | bytes 147464 | tf_op jit(solution)/shard_map/ppermute | solution.py:34
  65.2 6.5 %collective-permute-start.36 = (bf16[12,16,128]{2,1,0:T(8,128)(2,1)S(1)}, bf16[12,16,128]{2,1,0:T(8,128)(2,1)S(1)}, u32[]{:S(2)}, u32[]{:S(2)}) collective-permute-start(bf16[12,16,128]{2,1,0:T(8,128)(2,1)S(1)} %get-tuple-element.201), channel_id=1, source_target_pairs={{0,2},{2,0},{4,6},{6,4},{8,10},{10,8},{12,14},{14,12},{16,18},{18,... | collective-permute-start | bytes 147464 | tf_op jit(solution)/shard_map/ppermute | solution.py:34
  68.4 4.2 %collective-permute-start.42 = (bf16[12,16,128]{2,1,0:T(8,128)(2,1)S(1)}, bf16[12,16,128]{2,1,0:T(8,128)(2,1)S(1)}, u32[]{:S(2)}, u32[]{:S(2)}) collective-permute-start(bf16[12,16,128]{2,1,0:T(8,128)(2,1)S(1)} %get-tuple-element.213), channel_id=1, source_target_pairs={{0,2},{2,0},{4,6},{6,4},{8,10},{10,8},{12,14},{14,12},{16,18},{18,... | collective-permute-start | bytes 147464 | tf_op jit(solution)/shard_map/ppermute | solution.py:34
  69.0 4.1 %collective-permute-start.40 = (bf16[12,16,128]{2,1,0:T(8,128)(2,1)S(1)}, bf16[12,16,128]{2,1,0:T(8,128)(2,1)S(1)}, u32[]{:S(2)}, u32[]{:S(2)}) collective-permute-start(bf16[12,16,128]{2,1,0:T(8,128)(2,1)S(1)} %get-tuple-element.209), channel_id=1, source_target_pairs={{0,2},{2,0},{4,6},{6,4},{8,10},{10,8},{12,14},{14,12},{16,18},{18,... | collective-permute-start | bytes 147464 | tf_op jit(solution)/shard_map/ppermute | solution.py:34

commit v6 on v5

--- a/solution.py
+++ b/solution.py
@@ -131,10 +131,13 @@
         grad[k] = term(own_up[k], *slopes(total[first, :half], total[first, half:]), own_tokens[k])
 
 
-def other_slopes(rows, table, weights, other_tokens, slope, total):
+def other_slopes(rows, plan, weights, other_tokens, slope, table, arrived, total):
     places, half = weights.shape[0], weights.shape[1] // 2
+    copy = pltpu.make_async_copy(plan, table, arrived)
+    copy.start()
     for k in range(places):
         total[k] = project(weights[k], other_tokens[k])
+    copy.wait()
     add_duplicates(rows["first"], table, total)
     for k in range(places):
         first = table[rows["first"], k]
@@ -337,7 +340,7 @@
             return min(block_count, (owner_count >> len(done)) * capacity)
 
         def load_of(done):
-            return min(most_of(done), (block_count >> len(done)) + capacity)
+            return min(most_of(done), (block_count >> len(done)) + capacity + (len(done) < 3))
 
         rows = rows_of(axes)
         settled = [tuple(sorted((*done, bit))) for done, bit in steps_of(axes)]
@@ -366,8 +369,8 @@
     with jax.named_scope("other_tokens"):
         slope = call(
             functools.partial(other_slopes, rows), "other_slopes", [struct((places, side, token_count), F32)],
-            [SMEM, VMEM, VMEM], [table, weights, other_chosen], work // 2,
-            [pltpu.VMEM((places, side, token_count), F32)],
+            [VMEM] * 3, [table, weights, other_chosen], work // 2,
+            [pltpu.SMEM(table.shape, jnp.int32), pltpu.SemaphoreType.DMA, pltpu.VMEM((places, side, token_count), F32)],
         )[0]
 
     def reduce(load, table, slope, other_chosen, other_up, grad):

time: 74.7 us -> 74.9 us (level)
  waiting for transfers between devices: 18.7 us -> 19.8 us
    ppermute x27, waiting for transfers between devices: 18.7 us -> 19.8 us  [swap(): return lax.ppermute(value, axis, [(i, i ^ 1 << bit) for i in range(size)])]
  transfers between devices with their start and end apart: 27 -> 27, of which waited for: 15 -> 15; matrix products, arithmetic and copies ran while one was open for 2% -> 2% of each run, Pallas kernels for 19% -> 18%
where the time goes in v6:
time: 74.9 us; the launch traced here: 74.6 us
  starting transfers between devices  33.4 us (45%)
  waiting for transfers between devices  19.8 us (26%)
  Pallas kernels  14.8 us (20%)
  local copies, waits for them, and re-layouts  5.57 us (7%)
  between operations  0.96 us (1%)
    ppermute x27, starting transfers between devices, swap(): return lax.ppermute(value, axis, [(i, i ^ 1 << bit) for i in range(size)])  33.4 us
    ppermute x27, waiting for transfers between devices, swap(): return lax.ppermute(value, axis, [(i, i ^ 1 << bit) for i in range(size)])  19.8 us
    pallas_call x21, Pallas kernels, call(): pl.pallas_call(body, name=name, out_shape=tuple(outs), in_specs=in_specs,...  14.8 us
    unnamed x16, local copies, waits for them, and re-layouts  4.26 us
  transfers between devices with their start and end apart: 27, of which 15 were waited for; matrix products, arithmetic and copies ran while one was open for 2% of the time, Pallas kernels for 18%

profile of v6, /device:TPU:0, one launch (start us, length us, event | category | flops | bytes accessed | tf_op | source)
XLA Modules:
  0.0 74.6 jit_solution(3113009125401854689)
XLA Ops:
  0.0 0.5 collective-permute-start.23
  0.5 1.2 %copy-done = bf16[128,4096]{1,0:T(8,128)(2,1)S(1)} copy-done((bf16[128,4096]{1,0:T(8,128)(2,1)S(1)}, bf16[128,4096]{1,0:T(8,128)(2,1)}, u32[]{:S(2)}) %copy-start) | copy-done | bytes 1048600
  1.7 0.9 %copy-done.3 = f32[1,4,128,128]{3,2,1,0:T(8,128)S(1)} copy-done((f32[1,4,128,128]{3,2,1,0:T(8,128)S(1)}, f32[1,4,128,128]{3,2,1,0:T(8,128)}, u32[]{:S(2)}) %copy-start.3) | copy-done | bytes 262168
  2.8 2.6 %collective-permute-start.16 = (bf16[4,64,128]{2,1,0:T(8,128)(2,1)S(1)}, bf16[4,64,128]{2,1,0:T(8,128)(2,1)S(1)}, u32[]{:S(2)}, u32[]{:S(2)}) collective-permute-start(bf16[4,64,128]{2,1,0:T(8,128)(2,1)S(1)} %get-tuple-element.223), channel_id=1, source_target_pairs={{0,2},{2,0},{4,6},{6,4},{8,10},{10,8},{12,14},{14,12},{16,18},{18,... | collective-permute-start | bytes 196616 | tf_op jit(solution)/shard_map/weights/ppermute | solution.py:34
  5.3 0.7 concatenate.12.place
  6.1 1.2 %select_rows.1.refs_4_ = bf16[32,128,128]{2,1,0:T(8,128)(2,1)S(1)} custom-call(s32[67]{0:T(128)S(1)} %concatenate.12.place, bf16[1,128,4096]{2,1,0:T(8,128)(2,1)S(1)} %bitcast.10, bf16[1,128,4096]{2,1,0:T(8,128)(2,1)S(1)} %collective-permute-done.23.refs_1_), custom_call_target="tpu_custom_call" | custom-call | bytes 3145996 | tf_op jit(solution)/shard_map/tokens/select_rows/pallas_call | solution.py:20
  7.3 0.3 collective-permute-start.24
  7.6 0.5 collective-permute-done.16
  8.1 2.9 %collective-permute-start.17 = (bf16[8,64,128]{2,1,0:T(8,128)(2,1)S(1)}, bf16[8,64,128]{2,1,0:T(8,128)(2,1)S(1)}, u32[]{:S(2)}, u32[]{:S(2)}) collective-permute-start(bf16[8,64,128]{2,1,0:T(8,128)(2,1)S(1)} %pad_maximum_fusion), channel_id=1, source_target_pairs={{0,16},{2,18},{4,20},{6,22},{8,24},{10,26},{12,28},{14,30},{16,0},... | collective-permute-start | bytes 393224 | tf_op jit(solution)/shard_map/weights/ppermute | solution.py:34
  11.0 2.0 %copy-done.2 = bf16[128,14336]{1,0:T(8,128)(2,1)S(1)} copy-done((bf16[128,14336]{1,0:T(8,128)(2,1)S(1)}, bf16[128,14336]{1,0:T(8,128)(2,1)}, u32[]{:S(2)}) %copy-start.2) | copy-done | bytes 3670040
  13.1 3.6 %split_upstream.1 = (bf16[32,64,128]{2,1,0:T(8,128)(2,1)S(1)}, bf16[32,32,128]{2,1,0:T(8,128)(2,1)S(1)}, bf16[32,32,128]{2,1,0:T(8,128)(2,1)S(1)}) custom-call(s32[67]{0:T(128)S(1)} %concatenate.12.place, bf16[128,14336]{1,0:T(8,128)(2,1)S(1)} %copy-done.2), custom_call_target="tpu_custom_call" | custom-call | bytes 4718860 | tf_op jit(solution)/shard_map/weights/split_upstream/pallas_call | solution.py:20
  16.7 0.8 %make_plan.1.table.plan = s32[24,64]{1,0:T(8,128)S(1)} custom-call(s32[67]{0:T(128)S(1)} %concatenate.12.place, s32[1,32]{1,0:T(1,128)S(1)} %copy-done.4, s32[2,64]{1,0:T(2,128)S(1)} %copy-done.5, s32[1,64]{1,0:T(1,128)S(1)} %copy-done.6, s32[1,64]{1,0:T(1,128)S(1)} %bitcast.13), custom_call_target="tpu_custom_call" | custom-call | bytes 7564 | tf_op jit(solution)/shard_map/plan/make_plan/pallas_call | solution.py:20
  17.6 1.6 %collective-permute-start.18 = (bf16[8,64,128]{2,1,0:T(8,128)(2,1)S(1)}, bf16[8,64,128]{2,1,0:T(8,128)(2,1)S(1)}, u32[]{:S(2)}, u32[]{:S(2)}) collective-permute-start(bf16[8,64,128]{2,1,0:T(8,128)(2,1)S(1)} %pad_maximum_fusion), channel_id=1, source_target_pairs={{0,4},{2,6},{4,0},{6,2},{8,12},{10,14},{12,8},{14,10},{16,20},{18,... | collective-permute-start | bytes 393224 | tf_op jit(solution)/shard_map/weights/ppermute | solution.py:34
  19.2 1.6 %collective-permute-start.19 = (bf16[8,64,128]{2,1,0:T(8,128)(2,1)S(1)}, bf16[8,64,128]{2,1,0:T(8,128)(2,1)S(1)}, u32[]{:S(2)}, u32[]{:S(2)}) collective-permute-start(bf16[8,64,128]{2,1,0:T(8,128)(2,1)S(1)} %collective-permute-done.17), channel_id=1, source_target_pairs={{0,8},{2,10},{4,12},{6,14},{8,0},{10,2},{12,4},{14,6},{16,24},{18,... | collective-permute-start | bytes 393224 | tf_op jit(solution)/shard_map/weights/ppermute | solution.py:34
  20.8 2.8 %collective-permute-done.18 = bf16[8,64,128]{2,1,0:T(8,128)(2,1)S(1)} collective-permute-done((bf16[8,64,128]{2,1,0:T(8,128)(2,1)S(1)}, bf16[8,64,128]{2,1,0:T(8,128)(2,1)S(1)}, u32[]{:S(2)}, u32[]{:S(2)}) %collective-permute-start.18) | collective-permute-done | bytes 131104 | tf_op jit(solution)/shard_map/weights/ppermute | solution.py:34
  23.5 1.2 %collective-permute-done.19 = bf16[8,64,128]{2,1,0:T(8,128)(2,1)S(1)} collective-permute-done((bf16[8,64,128]{2,1,0:T(8,128)(2,1)S(1)}, bf16[8,64,128]{2,1,0:T(8,128)(2,1)S(1)}, u32[]{:S(2)}, u32[]{:S(2)}) %collective-permute-start.19) | collective-permute-done | bytes 131104 | tf_op jit(solution)/shard_map/weights/ppermute | solution.py:34
  24.8 0.6 collective-permute-start.22
  25.4 1.6 %collective-permute-start.21 = (bf16[16,64,128]{2,1,0:T(8,128)(2,1)S(1)}, bf16[16,64,128]{2,1,0:T(8,128)(2,1)S(1)}, u32[]{:S(2)}, u32[]{:S(2)}) collective-permute-start(bf16[16,64,128]{2,1,0:T(8,128)(2,1)S(1)} %constant_dynamic-update-slice_fusion.refs_0_), channel_id=1, source_target_pairs={{0,8},{2,10},{4,12},{6,14},{8,0},{10,2},{12,4},{14,6},{16,24},{18,... | collective-permute-start | bytes 786440 | tf_op jit(solution)/shard_map/weights/ppermute | solution.py:34
  27.0 1.5 %collective-permute-start.25 = (bf16[32,32,128]{2,1,0:T(8,128)(2,1)S(1)}, bf16[32,32,128]{2,1,0:T(8,128)(2,1)S(1)}, u32[]{:S(2)}, u32[]{:S(2)}) collective-permute-start(bf16[32,32,128]{2,1,0:T(8,128)(2,1)S(1)} %get-tuple-element.166), channel_id=1, source_target_pairs={{0,2},{2,0},{4,6},{6,4},{8,10},{10,8},{12,14},{14,12},{16,18},{18,... | collective-permute-start | bytes 786440 | tf_op jit(solution)/shard_map/upstream/ppermute | solution.py:34
  28.5 0.5 collective-permute-start.26
  29.1 3.4 %collective-permute-done.22.refs_3_ = bf16[16,64,128]{2,1,0:T(8,128)(2,1)S(1)} collective-permute-done((bf16[16,64,128]{2,1,0:T(8,128)(2,1)S(1)}, bf16[16,64,128]{2,1,0:T(8,128)(2,1)S(1)}, u32[]{:S(2)}, u32[]{:S(2)}) %collective-permute-start.22) | collective-permute-done | bytes 262176 | tf_op jit(solution)/shard_map/weights/ppermute | solution.py:34
  32.5 0.4 collective-permute-done.21.refs_1_
  32.9 2.7 %own_part.1 = (bf16[32,128,128]{2,1,0:T(8,128)(2,1)S(1)}, f32[32,128,128]{2,1,0:T(8,128)S(1)}) custom-call(s32[24,64]{1,0:T(8,128)S(1)} %make_plan.1.table.plan, bf16[16,64,128]{2,1,0:T(8,128)(2,1)S(1)} %constant_dynamic-update-slice_fusion.refs_0_, bf16[16,64,128]{2,1,0:T(8,128)(2,1)S(1)} %collective-permute-done.21.refs_1_, ...), custom_call_target="tpu_custom_call" | custom-call | flops 268435456 | bytes 5773312 | tf_op jit(solution)/shard_map/own_tokens/own_part/pallas_call | solution.py:20
  35.6 1.5 %other_slopes.1.slope = f32[32,128,128]{2,1,0:T(8,128)S(1)} custom-call(s32[24,64]{1,0:T(8,128)S(1)} %make_plan.1.table.plan, bf16[32,128,128]{2,1,0:T(8,128)(2,1)S(1)} %get-tuple-element.165.weights, bf16[32,128,128]{2,1,0:T(8,128)(2,1)S(1)} %collective-permute-done.24.other_tokens), custom_call_target="tpu_custom_call" | custom-call | flops 134217728 | bytes 4200448 | tf_op jit(solution)/shard_map/other_tokens/other_slopes/pallas_call | solution.py:20
  37.1 1.9 %collective-permute-done.25.other_up = bf16[32,32,128]{2,1,0:T(8,128)(2,1)S(1)} collective-permute-done((bf16[32,32,128]{2,1,0:T(8,128)(2,1)S(1)}, bf16[32,32,128]{2,1,0:T(8,128)(2,1)S(1)}, u32[]{:S(2)}, u32[]{:S(2)}) %collective-permute-start.25) | collective-permute-done | bytes 262176 | tf_op jit(solution)/shard_map/upstream/ppermute | solution.py:34
  39.0 0.9 %other_part.6 = (bf16[45,16,128]{2,1,0:T(8,128)(2,1)S(1)}, f32[45,16,128]{2,1,0:T(8,128)S(1)}, bf16[45,16,128]{2,1,0:T(8,128)(2,1)S(1)}, f32[45,16,128]{2,1,0:T(8,128)S(1)}) custom-call(s32[24,64]{1,0:T(8,128)S(1)} %make_plan.1.table.plan, f32[32,128,128]{2,1,0:T(8,128)S(1)} %other_slopes.1.slope, ...), custom_call_target="tpu_custom_call" | custom-call | flops 67108864 | bytes 6617088 | tf_op jit(solution)/shard_map/other_part/pallas_call | solution.py:20
  39.9 1.6 %collective-permute-start.27 = (bf16[45,16,128]{2,1,0:T(8,128)(2,1)S(1)}, bf16[45,16,128]{2,1,0:T(8,128)(2,1)S(1)}, u32[]{:S(2)}, u32[]{:S(2)}) collective-permute-start(bf16[45,16,128]{2,1,0:T(8,128)(2,1)S(1)} %get-tuple-element.170), channel_id=1, source_target_pairs={{0,8},{2,10},{4,12},{6,14},{8,0},{10,2},{12,4},{14,6},{16,24},{18,... | collective-permute-start | bytes 552968 | tf_op jit(solution)/shard_map/ppermute | solution.py:34
  41.6 1.5 %collective-permute-start.31 = (bf16[45,16,128]{2,1,0:T(8,128)(2,1)S(1)}, bf16[45,16,128]{2,1,0:T(8,128)(2,1)S(1)}, u32[]{:S(2)}, u32[]{:S(2)}) collective-permute-start(bf16[45,16,128]{2,1,0:T(8,128)(2,1)S(1)} %get-tuple-element.180), channel_id=1, source_target_pairs={{0,4},{2,6},{4,0},{6,2},{8,12},{10,14},{12,8},{14,10},{16,20},{18,... | collective-permute-start | bytes 552968 | tf_op jit(solution)/shard_map/ppermute | solution.py:34
  43.1 0.8 %collective-permute-done.26.other_up = bf16[32,32,128]{2,1,0:T(8,128)(2,1)S(1)} collective-permute-done((bf16[32,32,128]{2,1,0:T(8,128)(2,1)S(1)}, bf16[32,32,128]{2,1,0:T(8,128)(2,1)S(1)}, u32[]{:S(2)}, u32[]{:S(2)}) %collective-permute-start.26) | collective-permute-done | bytes 262176 | tf_op jit(solution)/shard_map/upstream/ppermute | solution.py:34
  43.9 0.9 %other_part.7 = (bf16[45,16,128]{2,1,0:T(8,128)(2,1)S(1)}, f32[45,16,128]{2,1,0:T(8,128)S(1)}, bf16[45,16,128]{2,1,0:T(8,128)(2,1)S(1)}, f32[45,16,128]{2,1,0:T(8,128)S(1)}) custom-call(s32[24,64]{1,0:T(8,128)S(1)} %make_plan.1.table.plan, f32[32,128,128]{2,1,0:T(8,128)S(1)} %other_slopes.1.slope, ...), custom_call_target="tpu_custom_call" | custom-call | flops 67108864 | bytes 6617088 | tf_op jit(solution)/shard_map/other_part/pallas_call | solution.py:20
  44.8 1.6 %collective-permute-start.30 = (bf16[45,16,128]{2,1,0:T(8,128)(2,1)S(1)}, bf16[45,16,128]{2,1,0:T(8,128)(2,1)S(1)}, u32[]{:S(2)}, u32[]{:S(2)}) collective-permute-start(bf16[45,16,128]{2,1,0:T(8,128)(2,1)S(1)} %get-tuple-element.178), channel_id=1, source_target_pairs={{0,8},{2,10},{4,12},{6,14},{8,0},{10,2},{12,4},{14,6},{16,24},{18,... | collective-permute-start | bytes 552968 | tf_op jit(solution)/shard_map/ppermute | solution.py:34
  46.5 1.5 %collective-permute-start.29 = (bf16[45,16,128]{2,1,0:T(8,128)(2,1)S(1)}, bf16[45,16,128]{2,1,0:T(8,128)(2,1)S(1)}, u32[]{:S(2)}, u32[]{:S(2)}) collective-permute-start(bf16[45,16,128]{2,1,0:T(8,128)(2,1)S(1)} %get-tuple-element.177), channel_id=1, source_target_pairs={{0,4},{2,6},{4,0},{6,2},{8,12},{10,14},{12,8},{14,10},{16,20},{18,... | collective-permute-start | bytes 552968 | tf_op jit(solution)/shard_map/ppermute | solution.py:34
  48.0 0.2 combine.36
  48.2 0.6 collective-permute-start.28
  48.7 0.2 combine.37
  48.9 2.7 %collective-permute-start.35 = (bf16[29,16,128]{2,1,0:T(8,128)(2,1)S(1)}, bf16[29,16,128]{2,1,0:T(8,128)(2,1)S(1)}, u32[]{:S(2)}, u32[]{:S(2)}) collective-permute-start(bf16[29,16,128]{2,1,0:T(8,128)(2,1)S(1)} %get-tuple-element.192), channel_id=1, source_target_pairs={{0,16},{2,18},{4,20},{6,22},{8,24},{10,26},{12,28},{14,30},{16,0},... | collective-permute-start | bytes 356360 | tf_op jit(solution)/shard_map/ppermute | solution.py:34
  51.6 0.2 combine.38
  51.7 1.6 %collective-permute-start.34 = (bf16[29,16,128]{2,1,0:T(8,128)(2,1)S(1)}, bf16[29,16,128]{2,1,0:T(8,128)(2,1)S(1)}, u32[]{:S(2)}, u32[]{:S(2)}) collective-permute-start(bf16[29,16,128]{2,1,0:T(8,128)(2,1)S(1)} %get-tuple-element.191), channel_id=1, source_target_pairs={{0,4},{2,6},{4,0},{6,2},{8,12},{10,14},{12,8},{14,10},{16,20},{18,... | collective-permute-start | bytes 356360 | tf_op jit(solution)/shard_map/ppermute | solution.py:34
  53.3 0.8 %collective-permute-done.29.refs_1_ = bf16[45,16,128]{2,1,0:T(8,128)(2,1)S(1)} collective-permute-done((bf16[45,16,128]{2,1,0:T(8,128)(2,1)S(1)}, bf16[45,16,128]{2,1,0:T(8,128)(2,1)S(1)}, u32[]{:S(2)}, u32[]{:S(2)}) %collective-permute-start.29) | collective-permute-done | bytes 184352 | tf_op jit(solution)/shard_map/ppermute | solution.py:34
  54.1 0.2 combine.39
  54.2 0.2 collective-permute-start.33
  54.4 1.6 %collective-permute-done.28.refs_1_ = bf16[29,16,128]{2,1,0:T(8,128)(2,1)S(1)} collective-permute-done((bf16[29,16,128]{2,1,0:T(8,128)(2,1)S(1)}, bf16[29,16,128]{2,1,0:T(8,128)(2,1)S(1)}, u32[]{:S(2)}, u32[]{:S(2)}) %collective-permute-start.28) | collective-permute-done | bytes 118816 | tf_op jit(solution)/shard_map/ppermute | solution.py:34
  56.0 0.1 combine.40
  56.1 2.7 %collective-permute-start.32 = (bf16[20,16,128]{2,1,0:T(8,128)(2,1)S(1)}, bf16[20,16,128]{2,1,0:T(8,128)(2,1)S(1)}, u32[]{:S(2)}, u32[]{:S(2)}) collective-permute-start(bf16[20,16,128]{2,1,0:T(8,128)(2,1)S(1)} %get-tuple-element.189), channel_id=1, source_target_pairs={{0,16},{2,18},{4,20},{6,22},{8,24},{10,26},{12,28},{14,30},{16,0},... | collective-permute-start | bytes 245768 | tf_op jit(solution)/shard_map/ppermute | solution.py:34
  58.8 0.1 combine.41
  58.9 0.5 collective-permute-start.37
  59.5 0.1 combine.42
  59.6 0.4 collective-permute-start.39
  60.1 2.0 %collective-permute-done.33.refs_1_ = bf16[29,16,128]{2,1,0:T(8,128)(2,1)S(1)} collective-permute-done((bf16[29,16,128]{2,1,0:T(8,128)(2,1)S(1)}, bf16[29,16,128]{2,1,0:T(8,128)(2,1)S(1)}, u32[]{:S(2)}, u32[]{:S(2)}) %collective-permute-start.33) | collective-permute-done | bytes 118816 | tf_op jit(solution)/shard_map/ppermute | solution.py:34
  62.0 0.1 combine.43
  62.2 0.7 collective-permute-start.41
  62.8 1.6 %collective-permute-done.32.refs_1_ = bf16[20,16,128]{2,1,0:T(8,128)(2,1)S(1)} collective-permute-done((bf16[20,16,128]{2,1,0:T(8,128)(2,1)S(1)}, bf16[20,16,128]{2,1,0:T(8,128)(2,1)S(1)}, u32[]{:S(2)}, u32[]{:S(2)}) %collective-permute-start.32) | collective-permute-done | bytes 81952 | tf_op jit(solution)/shard_map/ppermute | solution.py:34
  64.4 0.1 combine.44
  64.6 0.1 combine.45
  64.7 0.6 collective-permute-start.38
  65.3 1.5 %collective-permute-start.36 = (bf16[12,16,128]{2,1,0:T(8,128)(2,1)S(1)}, bf16[12,16,128]{2,1,0:T(8,128)(2,1)S(1)}, u32[]{:S(2)}, u32[]{:S(2)}) collective-permute-start(bf16[12,16,128]{2,1,0:T(8,128)(2,1)S(1)} %get-tuple-element.201), channel_id=1, source_target_pairs={{0,2},{2,0},{4,6},{6,4},{8,10},{10,8},{12,14},{14,12},{16,18},{18,... | collective-permute-start | bytes 147464 | tf_op jit(solution)/shard_map/ppermute | solution.py:34
  66.8 0.8 %collective-permute-done.39.refs_1_ = bf16[20,16,128]{2,1,0:T(8,128)(2,1)S(1)} collective-permute-done((bf16[20,16,128]{2,1,0:T(8,128)(2,1)S(1)}, bf16[20,16,128]{2,1,0:T(8,128)(2,1)S(1)}, u32[]{:S(2)}, u32[]{:S(2)}) %collective-permute-start.39) | collective-permute-done | bytes 81952 | tf_op jit(solution)/shard_map/ppermute | solution.py:34
  67.7 0.7 collective-permute-done.41.refs_1_
  68.6 0.6 collective-permute-start.42
  69.2 1.5 %collective-permute-start.40 = (bf16[12,16,128]{2,1,0:T(8,128)(2,1)S(1)}, bf16[12,16,128]{2,1,0:T(8,128)(2,1)S(1)}, u32[]{:S(2)}, u32[]{:S(2)}) collective-permute-start(bf16[12,16,128]{2,1,0:T(8,128)(2,1)S(1)} %get-tuple-element.209), channel_id=1, source_target_pairs={{0,2},{2,0},{4,6},{6,4},{8,10},{10,8},{12,14},{14,12},{16,18},{18,... | collective-permute-start | bytes 147464 | tf_op jit(solution)/shard_map/ppermute | solution.py:34
  70.7 0.5 slice.3
  71.9 0.9 %collective-permute-done.42 = bf16[12,16,128]{2,1,0:T(8,128)(2,1)S(1)} collective-permute-done((bf16[12,16,128]{2,1,0:T(8,128)(2,1)S(1)}, bf16[12,16,128]{2,1,0:T(8,128)(2,1)S(1)}, u32[]{:S(2)}, u32[]{:S(2)}) %collective-permute-start.42) | collective-permute-done | bytes 49184 | tf_op jit(solution)/shard_map/ppermute | solution.py:34
  72.8 0.5 collective-permute-done.40
  73.3 1.3 %finish.1 = f32[1,12,128,128]{3,2,1,0:T(8,128)} custom-call(s32[24,64]{1,0:T(8,128)S(1)} %make_plan.1.table.plan, f32[12,16,128]{2,1,0:T(8,128)S(1)} %get-tuple-element.214.refs_0_, bf16[12,16,128]{2,1,0:T(8,128)(2,1)S(1)} %get-tuple-element.215.refs_1_, f32[12,16,128]{2,1,0:T(8,128)S(1)} %get-tuple-element.216.refs_2_, ...), custom_call_target="tpu_custom_call" | custom-call | bytes 1382400 | tf_op jit(solution)/shard_map/finish/pallas_call | solution.py:20
  (38 shorter events, 0.6 us)
Async XLA Ops:
  0.0 6.1 %collective-permute-start.23 = (bf16[1,128,4096]{2,1,0:T(8,128)(2,1)}, bf16[1,128,4096]{2,1,0:T(8,128)(2,1)S(1)}, u32[]{:S(2)}, u32[]{:S(2)}) collective-permute-start(bf16[1,128,4096]{2,1,0:T(8,128)(2,1)} %bitcast.9), channel_id=1, source_target_pairs={{0,1},{1,0},{2,3},{3,2},{4,5},{5,4},{6,7},{7,6},{8,9},{9,8},{10,11... | collective-permute-start | bytes 3145736 | tf_op jit(solution)/shard_map/tokens/ppermute | solution.py:34
  0.5 1.2 %copy-start = (bf16[128,4096]{1,0:T(8,128)(2,1)S(1)}, bf16[128,4096]{1,0:T(8,128)(2,1)}, u32[]{:S(2)}) copy-start(bf16[128,4096]{1,0:T(8,128)(2,1)} %tokens.1) | copy-start | bytes 3145732
  1.7 0.9 %copy-start.3 = (f32[1,4,128,128]{3,2,1,0:T(8,128)S(1)}, f32[1,4,128,128]{3,2,1,0:T(8,128)}, u32[]{:S(2)}) copy-start(f32[1,4,128,128]{3,2,1,0:T(8,128)} %masters.1) | copy-start | bytes 786436
  2.6 3.5 %copy-start.1 = (bf16[128,4096]{1,0:T(8,128)(2,1)S(1)}, bf16[128,4096]{1,0:T(8,128)(2,1)}, u32[]{:S(2)}) copy-start(bf16[128,4096]{1,0:T(8,128)(2,1)} %tokens.1) | copy-start | bytes 3145732
  2.7 8.3 %copy-start.6 = (s32[1,64]{1,0:T(1,128)S(1)}, s32[1,64]{1,0:T(1,128)}, u32[]{:S(2)}) copy-start(s32[1,64]{1,0:T(1,128)} %refs_0_.1) | copy-start | bytes 772
  2.8 5.3 %collective-permute-start.16 = (bf16[4,64,128]{2,1,0:T(8,128)(2,1)S(1)}, bf16[4,64,128]{2,1,0:T(8,128)(2,1)S(1)}, u32[]{:S(2)}, u32[]{:S(2)}) collective-permute-start(bf16[4,64,128]{2,1,0:T(8,128)(2,1)S(1)} %get-tuple-element.223), channel_id=1, source_target_pairs={{0,2},{2,0},{4,6},{6,4},{8,10},{10,8},{12,14},{14,12},{16,18},{18,... | collective-permute-start | bytes 196616 | tf_op jit(solution)/shard_map/weights/ppermute | solution.py:34
  7.3 9.4 %copy-start.4 = (s32[1,32]{1,0:T(1,128)S(1)}, s32[1,32]{1,0:T(1,128)}, u32[]{:S(2)}) copy-start(s32[1,32]{1,0:T(1,128)} %columns.1) | copy-start | bytes 388
  7.3 9.4 %copy-start.5 = (s32[2,64]{1,0:T(2,128)S(1)}, s32[2,64]{1,0:T(2,128)}, u32[]{:S(2)}) copy-start(s32[2,64]{1,0:T(2,128)} %constant.16.clone.found) | copy-start | bytes 1540
  7.3 28.3 %collective-permute-start.24 = (bf16[32,128,128]{2,1,0:T(8,128)(2,1)S(1)}, bf16[32,128,128]{2,1,0:T(8,128)(2,1)S(1)}, u32[]{:S(2)}, u32[]{:S(2)}) collective-permute-start(bf16[32,128,128]{2,1,0:T(8,128)(2,1)S(1)} %select_rows.1.refs_4_), channel_id=1, source_target_pairs={{0,2},{2,0},{4,6},{6,4},{8,10},{10,8},{12,14},{14,12},{16,18},{18,... | collective-permute-start | bytes 3145736 | tf_op jit(solution)/shard_map/weights/ppermute | solution.py:34
  8.1 9.4 %collective-permute-start.17 = (bf16[8,64,128]{2,1,0:T(8,128)(2,1)S(1)}, bf16[8,64,128]{2,1,0:T(8,128)(2,1)S(1)}, u32[]{:S(2)}, u32[]{:S(2)}) collective-permute-start(bf16[8,64,128]{2,1,0:T(8,128)(2,1)S(1)} %pad_maximum_fusion), channel_id=1, source_target_pairs={{0,16},{2,18},{4,20},{6,22},{8,24},{10,26},{12,28},{14,30},{16,0},... | collective-permute-start | bytes 393224 | tf_op jit(solution)/shard_map/weights/ppermute | solution.py:34
  11.0 5.7 %collective-permute-start.20 = (s32[1,1,64]{2,1,0:T(1,128)S(1)}, s32[1,1,64]{2,1,0:T(1,128)S(1)}, u32[]{:S(2)}, u32[]{:S(2)}) collective-permute-start(s32[1,1,64]{2,1,0:T(1,128)S(1)} %bitcast.12), channel_id=1, source_target_pairs={{0,1},{1,0},{2,3},{3,2},{4,5},{5,4},{6,7},{7,6},{8,9},{9,8},{10,11... | collective-permute-start | bytes 776 | tf_op jit(solution)/shard_map/tokens/ppermute | solution.py:34
  11.0 2.0 %copy-start.2 = (bf16[128,14336]{1,0:T(8,128)(2,1)S(1)}, bf16[128,14336]{1,0:T(8,128)(2,1)}, u32[]{:S(2)}) copy-start(bf16[128,14336]{1,0:T(8,128)(2,1)} %grad.1) | copy-start | bytes 11010052
  17.6 6.0 %collective-permute-start.18 = (bf16[8,64,128]{2,1,0:T(8,128)(2,1)S(1)}, bf16[8,64,128]{2,1,0:T(8,128)(2,1)S(1)}, u32[]{:S(2)}, u32[]{:S(2)}) collective-permute-start(bf16[8,64,128]{2,1,0:T(8,128)(2,1)S(1)} %pad_maximum_fusion), channel_id=1, source_target_pairs={{0,4},{2,6},{4,0},{6,2},{8,12},{10,14},{12,8},{14,10},{16,20},{18,... | collective-permute-start | bytes 393224 | tf_op jit(solution)/shard_map/weights/ppermute | solution.py:34
  19.2 5.6 %collective-permute-start.19 = (bf16[8,64,128]{2,1,0:T(8,128)(2,1)S(1)}, bf16[8,64,128]{2,1,0:T(8,128)(2,1)S(1)}, u32[]{:S(2)}, u32[]{:S(2)}) collective-permute-start(bf16[8,64,128]{2,1,0:T(8,128)(2,1)S(1)} %collective-permute-done.17), channel_id=1, source_target_pairs={{0,8},{2,10},{4,12},{6,14},{8,0},{10,2},{12,4},{14,6},{16,24},{18,... | collective-permute-start | bytes 393224 | tf_op jit(solution)/shard_map/weights/ppermute | solution.py:34
  24.8 7.7 %collective-permute-start.22 = (bf16[16,64,128]{2,1,0:T(8,128)(2,1)S(1)}, bf16[16,64,128]{2,1,0:T(8,128)(2,1)S(1)}, u32[]{:S(2)}, u32[]{:S(2)}) collective-permute-start(bf16[16,64,128]{2,1,0:T(8,128)(2,1)S(1)} %constant_dynamic-update-slice_fusion.2.refs_2_), channel_id=1, source_target_pairs={{0,4},{2,6},{4,0},{6,2},{8,12},{10,14},{12,8},{14,10},{16,20},{18,... | collective-permute-start | bytes 786440 | tf_op jit(solution)/shard_map/weights/ppermute | solution.py:34
  25.4 7.5 %collective-permute-start.21 = (bf16[16,64,128]{2,1,0:T(8,128)(2,1)S(1)}, bf16[16,64,128]{2,1,0:T(8,128)(2,1)S(1)}, u32[]{:S(2)}, u32[]{:S(2)}) collective-permute-start(bf16[16,64,128]{2,1,0:T(8,128)(2,1)S(1)} %constant_dynamic-update-slice_fusion.refs_0_), channel_id=1, source_target_pairs={{0,8},{2,10},{4,12},{6,14},{8,0},{10,2},{12,4},{14,6},{16,24},{18,... | collective-permute-start | bytes 786440 | tf_op jit(solution)/shard_map/weights/ppermute | solution.py:34
  27.0 12.0 %collective-permute-start.25 = (bf16[32,32,128]{2,1,0:T(8,128)(2,1)S(1)}, bf16[32,32,128]{2,1,0:T(8,128)(2,1)S(1)}, u32[]{:S(2)}, u32[]{:S(2)}) collective-permute-start(bf16[32,32,128]{2,1,0:T(8,128)(2,1)S(1)} %get-tuple-element.166), channel_id=1, source_target_pairs={{0,2},{2,0},{4,6},{6,4},{8,10},{10,8},{12,14},{14,12},{16,18},{18,... | collective-permute-start | bytes 786440 | tf_op jit(solution)/shard_map/upstream/ppermute | solution.py:34
  28.5 15.4 %collective-permute-start.26 = (bf16[32,32,128]{2,1,0:T(8,128)(2,1)S(1)}, bf16[32,32,128]{2,1,0:T(8,128)(2,1)S(1)}, u32[]{:S(2)}, u32[]{:S(2)}) collective-permute-start(bf16[32,32,128]{2,1,0:T(8,128)(2,1)S(1)} %get-tuple-element.168), channel_id=1, source_target_pairs={{0,2},{2,0},{4,6},{6,4},{8,10},{10,8},{12,14},{14,12},{16,18},{18,... | collective-permute-start | bytes 786440 | tf_op jit(solution)/shard_map/upstream/ppermute | solution.py:34
  39.9 8.1 %collective-permute-start.27 = (bf16[45,16,128]{2,1,0:T(8,128)(2,1)S(1)}, bf16[45,16,128]{2,1,0:T(8,128)(2,1)S(1)}, u32[]{:S(2)}, u32[]{:S(2)}) collective-permute-start(bf16[45,16,128]{2,1,0:T(8,128)(2,1)S(1)} %get-tuple-element.170), channel_id=1, source_target_pairs={{0,8},{2,10},{4,12},{6,14},{8,0},{10,2},{12,4},{14,6},{16,24},{18,... | collective-permute-start | bytes 552968 | tf_op jit(solution)/shard_map/ppermute | solution.py:34
  41.6 7.2 %collective-permute-start.31 = (bf16[45,16,128]{2,1,0:T(8,128)(2,1)S(1)}, bf16[45,16,128]{2,1,0:T(8,128)(2,1)S(1)}, u32[]{:S(2)}, u32[]{:S(2)}) collective-permute-start(bf16[45,16,128]{2,1,0:T(8,128)(2,1)S(1)} %get-tuple-element.180), channel_id=1, source_target_pairs={{0,4},{2,6},{4,0},{6,2},{8,12},{10,14},{12,8},{14,10},{16,20},{18,... | collective-permute-start | bytes 552968 | tf_op jit(solution)/shard_map/ppermute | solution.py:34
  44.8 6.7 %collective-permute-start.30 = (bf16[45,16,128]{2,1,0:T(8,128)(2,1)S(1)}, bf16[45,16,128]{2,1,0:T(8,128)(2,1)S(1)}, u32[]{:S(2)}, u32[]{:S(2)}) collective-permute-start(bf16[45,16,128]{2,1,0:T(8,128)(2,1)S(1)} %get-tuple-element.178), channel_id=1, source_target_pairs={{0,8},{2,10},{4,12},{6,14},{8,0},{10,2},{12,4},{14,6},{16,24},{18,... | collective-permute-start | bytes 552968 | tf_op jit(solution)/shard_map/ppermute | solution.py:34
  46.5 7.6 %collective-permute-start.29 = (bf16[45,16,128]{2,1,0:T(8,128)(2,1)S(1)}, bf16[45,16,128]{2,1,0:T(8,128)(2,1)S(1)}, u32[]{:S(2)}, u32[]{:S(2)}) collective-permute-start(bf16[45,16,128]{2,1,0:T(8,128)(2,1)S(1)} %get-tuple-element.177), channel_id=1, source_target_pairs={{0,4},{2,6},{4,0},{6,2},{8,12},{10,14},{12,8},{14,10},{16,20},{18,... | collective-permute-start | bytes 552968 | tf_op jit(solution)/shard_map/ppermute | solution.py:34
  48.2 7.8 %collective-permute-start.28 = (bf16[29,16,128]{2,1,0:T(8,128)(2,1)S(1)}, bf16[29,16,128]{2,1,0:T(8,128)(2,1)S(1)}, u32[]{:S(2)}, u32[]{:S(2)}) collective-permute-start(bf16[29,16,128]{2,1,0:T(8,128)(2,1)S(1)} %get-tuple-element.175), channel_id=1, source_target_pairs={{0,4},{2,6},{4,0},{6,2},{8,12},{10,14},{12,8},{14,10},{16,20},{18,... | collective-permute-start | bytes 356360 | tf_op jit(solution)/shard_map/ppermute | solution.py:34
  48.9 9.9 %collective-permute-start.35 = (bf16[29,16,128]{2,1,0:T(8,128)(2,1)S(1)}, bf16[29,16,128]{2,1,0:T(8,128)(2,1)S(1)}, u32[]{:S(2)}, u32[]{:S(2)}) collective-permute-start(bf16[29,16,128]{2,1,0:T(8,128)(2,1)S(1)} %get-tuple-element.192), channel_id=1, source_target_pairs={{0,16},{2,18},{4,20},{6,22},{8,24},{10,26},{12,28},{14,30},{16,0},... | collective-permute-start | bytes 356360 | tf_op jit(solution)/shard_map/ppermute | solution.py:34
  51.7 7.7 %collective-permute-start.34 = (bf16[29,16,128]{2,1,0:T(8,128)(2,1)S(1)}, bf16[29,16,128]{2,1,0:T(8,128)(2,1)S(1)}, u32[]{:S(2)}, u32[]{:S(2)}) collective-permute-start(bf16[29,16,128]{2,1,0:T(8,128)(2,1)S(1)} %get-tuple-element.191), channel_id=1, source_target_pairs={{0,4},{2,6},{4,0},{6,2},{8,12},{10,14},{12,8},{14,10},{16,20},{18,... | collective-permute-start | bytes 356360 | tf_op jit(solution)/shard_map/ppermute | solution.py:34
  54.2 7.8 %collective-permute-start.33 = (bf16[29,16,128]{2,1,0:T(8,128)(2,1)S(1)}, bf16[29,16,128]{2,1,0:T(8,128)(2,1)S(1)}, u32[]{:S(2)}, u32[]{:S(2)}) collective-permute-start(bf16[29,16,128]{2,1,0:T(8,128)(2,1)S(1)} %get-tuple-element.190), channel_id=1, source_target_pairs={{0,8},{2,10},{4,12},{6,14},{8,0},{10,2},{12,4},{14,6},{16,24},{18,... | collective-permute-start | bytes 356360 | tf_op jit(solution)/shard_map/ppermute | solution.py:34
  56.1 8.3 %collective-permute-start.32 = (bf16[20,16,128]{2,1,0:T(8,128)(2,1)S(1)}, bf16[20,16,128]{2,1,0:T(8,128)(2,1)S(1)}, u32[]{:S(2)}, u32[]{:S(2)}) collective-permute-start(bf16[20,16,128]{2,1,0:T(8,128)(2,1)S(1)} %get-tuple-element.189), channel_id=1, source_target_pairs={{0,16},{2,18},{4,20},{6,22},{8,24},{10,26},{12,28},{14,30},{16,0},... | collective-permute-start | bytes 245768 | tf_op jit(solution)/shard_map/ppermute | solution.py:34
  58.9 5.7 %collective-permute-start.37 = (bf16[20,16,128]{2,1,0:T(8,128)(2,1)S(1)}, bf16[20,16,128]{2,1,0:T(8,128)(2,1)S(1)}, u32[]{:S(2)}, u32[]{:S(2)}) collective-permute-start(bf16[20,16,128]{2,1,0:T(8,128)(2,1)S(1)} %get-tuple-element.202), channel_id=1, source_target_pairs={{0,8},{2,10},{4,12},{6,14},{8,0},{10,2},{12,4},{14,6},{16,24},{18,... | collective-permute-start | bytes 245768 | tf_op jit(solution)/shard_map/ppermute | solution.py:34
  59.6 8.0 %collective-permute-start.39 = (bf16[20,16,128]{2,1,0:T(8,128)(2,1)S(1)}, bf16[20,16,128]{2,1,0:T(8,128)(2,1)S(1)}, u32[]{:S(2)}, u32[]{:S(2)}) collective-permute-start(bf16[20,16,128]{2,1,0:T(8,128)(2,1)S(1)} %get-tuple-element.206), channel_id=1, source_target_pairs={{0,16},{2,18},{4,20},{6,22},{8,24},{10,26},{12,28},{14,30},{16,0},... | collective-permute-start | bytes 245768 | tf_op jit(solution)/shard_map/ppermute | solution.py:34
  62.2 6.3 %collective-permute-start.41 = (bf16[20,16,128]{2,1,0:T(8,128)(2,1)S(1)}, bf16[20,16,128]{2,1,0:T(8,128)(2,1)S(1)}, u32[]{:S(2)}, u32[]{:S(2)}) collective-permute-start(bf16[20,16,128]{2,1,0:T(8,128)(2,1)S(1)} %get-tuple-element.210), channel_id=1, source_target_pairs={{0,16},{2,18},{4,20},{6,22},{8,24},{10,26},{12,28},{14,30},{16,0},... | collective-permute-start | bytes 245768 | tf_op jit(solution)/shard_map/ppermute | solution.py:34
  64.7 7.1 %collective-permute-start.38 = (bf16[12,16,128]{2,1,0:T(8,128)(2,1)S(1)}, bf16[12,16,128]{2,1,0:T(8,128)(2,1)S(1)}, u32[]{:S(2)}, u32[]{:S(2)}) collective-permute-start(bf16[12,16,128]{2,1,0:T(8,128)(2,1)S(1)} %get-tuple-element.205), channel_id=1, source_target_pairs={{0,2},{2,0},{4,6},{6,4},{8,10},{10,8},{12,14},{14,12},{16,18},{18,... | collective-permute-start | bytes 147464 | tf_op jit(solution)/shard_map/ppermute | solution.py:34
  65.3 6.6 %collective-permute-start.36 = (bf16[12,16,128]{2,1,0:T(8,128)(2,1)S(1)}, bf16[12,16,128]{2,1,0:T(8,128)(2,1)S(1)}, u32[]{:S(2)}, u32[]{:S(2)}) collective-permute-start(bf16[12,16,128]{2,1,0:T(8,128)(2,1)S(1)} %get-tuple-element.201), channel_id=1, source_target_pairs={{0,2},{2,0},{4,6},{6,4},{8,10},{10,8},{12,14},{14,12},{16,18},{18,... | collective-permute-start | bytes 147464 | tf_op jit(solution)/shard_map/ppermute | solution.py:34
  68.6 4.2 %collective-permute-start.42 = (bf16[12,16,128]{2,1,0:T(8,128)(2,1)S(1)}, bf16[12,16,128]{2,1,0:T(8,128)(2,1)S(1)}, u32[]{:S(2)}, u32[]{:S(2)}) collective-permute-start(bf16[12,16,128]{2,1,0:T(8,128)(2,1)S(1)} %get-tuple-element.213), channel_id=1, source_target_pairs={{0,2},{2,0},{4,6},{6,4},{8,10},{10,8},{12,14},{14,12},{16,18},{18,... | collective-permute-start | bytes 147464 | tf_op jit(solution)/shard_map/ppermute | solution.py:34
  69.2 4.1 %collective-permute-start.40 = (bf16[12,16,128]{2,1,0:T(8,128)(2,1)S(1)}, bf16[12,16,128]{2,1,0:T(8,128)(2,1)S(1)}, u32[]{:S(2)}, u32[]{:S(2)}) collective-permute-start(bf16[12,16,128]{2,1,0:T(8,128)(2,1)S(1)} %get-tuple-element.209), channel_id=1, source_target_pairs={{0,2},{2,0},{4,6},{6,4},{8,10},{10,8},{12,14},{14,12},{16,18},{18,... | collective-permute-start | bytes 147464 | tf_op jit(solution)/shard_map/ppermute | solution.py:34

commit v7 on v5

--- a/solution.py
+++ b/solution.py
@@ -178,15 +178,26 @@
     kept[...] = total[pl.ds(jnp.minimum(scalar(table, kept_row), count), room)]
 
 
-def finish(count_row, pair_row, table, *refs):
+def turn_own(count_row, pair_row, table, *refs):
     ends, out = refs[:-1], refs[-1]
     count, swapped = scalar(table, count_row), scalar(table, pair_row) != 0
+    for slot in range(out.shape[0]):
+        mine = jnp.concatenate([end[slot] for end in ends], axis=0)
+        mine = jnp.where(slot < count, mine, 0.0)
+        zero = jnp.zeros(mine.shape, F32)
+        low, high = jnp.where(swapped, zero, mine), jnp.where(swapped, mine, zero)
+        out[slot] = jnp.concatenate([low, high], axis=0).T
+
+
+def finish(count_row, pair_row, table, own, *refs):
+    ends, out = refs[:-1], refs[-1]
+    count, swapped = scalar(table, count_row), scalar(table, pair_row) != 0
+    half = sum(end.shape[1] for end in ends)
+    high = (lax.broadcasted_iota(jnp.int32, out.shape[2:], 1) >= half) != swapped
     for slot in range(out.shape[1]):
-        mine = jnp.concatenate([end[slot] for end in ends[0::2]], axis=0)
-        other = jnp.concatenate([end[slot] for end in ends[1::2]], axis=0).astype(F32)
-        low, high = jnp.where(swapped, other, mine), jnp.where(swapped, mine, other)
-        whole = jnp.concatenate([low, high], axis=0).T
-        out[0, slot] = jnp.where(slot < count, whole, 0.0)
+        other = jnp.concatenate([end[slot] for end in ends], axis=0).astype(F32).T
+        other = jnp.concatenate([other, other], axis=1)
+        out[0, slot] = jnp.where(jnp.logical_and(slot < count, high), other, own[slot])
 
 
 def axes_of(owner_count):
@@ -407,7 +418,12 @@
             turn = outs[1]
             for key, sent, kept in zip(made, outs[0::2], outs[1::2]):
                 state[key] = kept, swap(sent, "dp", orders[key[0]][n])
-        return [end for key in sorted(state) for end in state[key]]
+        kept, got = zip(*(state[key] for key in sorted(state)))
+        own = call(
+            functools.partial(turn_own, rows["end"], rows["pair"]), "turn_own", [struct((capacity, side, side), F32)],
+            [VMEM] * (1 + len(kept)), [table, *kept],
+        )[0]
+        return own, *got
 
     operands = (table, slope, other_chosen, other_up, grad)
     ends = reduce(load_of, *operands)

time: 74.7 us -> 74.6 us (level)
    pallas_call x21 -> x22, Pallas kernels: 15.5 us -> 15.8 us  [call(): pl.pallas_call(body, name=name, out_shape=tuple(outs), in_specs=in_specs,...]
  transfers between devices with their start and end apart: 27 -> 27, of which waited for: 15 -> 15; matrix products, arithmetic and copies ran while one was open for 2% -> 2% of each run, Pallas kernels for 19% -> 20%
where the time goes in v7:
time: 74.6 us; the launch traced here: 74.4 us
  starting transfers between devices  33.6 us (45%)
  waiting for transfers between devices  18.3 us (25%)
  Pallas kernels  15.8 us (21%)
  local copies, waits for them, and re-layouts  5.57 us (7%)
  between operations  0.97 us (1%)
    ppermute x27, starting transfers between devices, swap(): return lax.ppermute(value, axis, [(i, i ^ 1 << bit) for i in range(size)])  33.6 us
    ppermute x27, waiting for transfers between devices, swap(): return lax.ppermute(value, axis, [(i, i ^ 1 << bit) for i in range(size)])  18.3 us
    pallas_call x22, Pallas kernels, call(): pl.pallas_call(body, name=name, out_shape=tuple(outs), in_specs=in_specs,...  15.8 us
    unnamed x16, local copies, waits for them, and re-layouts  4.26 us
  transfers between devices with their start and end apart: 27, of which 15 were waited for; matrix products, arithmetic and copies ran while one was open for 2% of the time, Pallas kernels for 20%

profile of v7, /device:TPU:0, one launch (start us, length us, event | category | flops | bytes accessed | tf_op | source)
XLA Modules:
  0.0 74.4 jit_solution(5212619656070385877)
XLA Ops:
  0.0 0.5 collective-permute-start.23
  0.5 1.2 %copy-done = bf16[128,4096]{1,0:T(8,128)(2,1)S(1)} copy-done((bf16[128,4096]{1,0:T(8,128)(2,1)S(1)}, bf16[128,4096]{1,0:T(8,128)(2,1)}, u32[]{:S(2)}) %copy-start) | copy-done | bytes 1048600
  1.7 0.9 %copy-done.3 = f32[1,4,128,128]{3,2,1,0:T(8,128)S(1)} copy-done((f32[1,4,128,128]{3,2,1,0:T(8,128)S(1)}, f32[1,4,128,128]{3,2,1,0:T(8,128)}, u32[]{:S(2)}) %copy-start.3) | copy-done | bytes 262168
  2.8 2.6 %collective-permute-start.16 = (bf16[4,64,128]{2,1,0:T(8,128)(2,1)S(1)}, bf16[4,64,128]{2,1,0:T(8,128)(2,1)S(1)}, u32[]{:S(2)}, u32[]{:S(2)}) collective-permute-start(bf16[4,64,128]{2,1,0:T(8,128)(2,1)S(1)} %get-tuple-element.211), channel_id=1, source_target_pairs={{0,2},{2,0},{4,6},{6,4},{8,10},{10,8},{12,14},{14,12},{16,18},{18,... | collective-permute-start | bytes 196616 | tf_op jit(solution)/shard_map/weights/ppermute | solution.py:34
  5.3 0.7 %concatenate.12.place = s32[67]{0:T(128)S(1)} concatenate(s32[1]{0:T(128)} %bitcast, s32[1]{0:T(128)} %bitcast.1, s32[1]{0:T(128)} %bitcast.2, s32[32]{0:T(128)} %bitcast.14, s32[32]{0:T(128)} %bitcast.11), dimensions={0} | concatenate | bytes 536 | tf_op jit(solution)/shard_map/concatenate | solution.py:299
  6.1 1.2 %select_rows.1.refs_4_ = bf16[32,128,128]{2,1,0:T(8,128)(2,1)S(1)} custom-call(s32[67]{0:T(128)S(1)} %concatenate.12.place, bf16[1,128,4096]{2,1,0:T(8,128)(2,1)S(1)} %bitcast.10, bf16[1,128,4096]{2,1,0:T(8,128)(2,1)S(1)} %collective-permute-done.23.refs_1_), custom_call_target="tpu_custom_call" | custom-call | bytes 3145996 | tf_op jit(solution)/shard_map/tokens/select_rows/pallas_call | solution.py:20
  7.3 0.3 collective-permute-start.24
  7.6 0.5 collective-permute-done.16
  8.1 2.9 %collective-permute-start.17 = (bf16[8,64,128]{2,1,0:T(8,128)(2,1)S(1)}, bf16[8,64,128]{2,1,0:T(8,128)(2,1)S(1)}, u32[]{:S(2)}, u32[]{:S(2)}) collective-permute-start(bf16[8,64,128]{2,1,0:T(8,128)(2,1)S(1)} %pad_maximum_fusion), channel_id=1, source_target_pairs={{0,16},{2,18},{4,20},{6,22},{8,24},{10,26},{12,28},{14,30},{16,0},... | collective-permute-start | bytes 393224 | tf_op jit(solution)/shard_map/weights/ppermute | solution.py:34
  11.0 2.0 %copy-done.2 = bf16[128,14336]{1,0:T(8,128)(2,1)S(1)} copy-done((bf16[128,14336]{1,0:T(8,128)(2,1)S(1)}, bf16[128,14336]{1,0:T(8,128)(2,1)}, u32[]{:S(2)}) %copy-start.2) | copy-done | bytes 3670040
  13.1 3.6 %split_upstream.1 = (bf16[32,64,128]{2,1,0:T(8,128)(2,1)S(1)}, bf16[32,32,128]{2,1,0:T(8,128)(2,1)S(1)}, bf16[32,32,128]{2,1,0:T(8,128)(2,1)S(1)}) custom-call(s32[67]{0:T(128)S(1)} %concatenate.12.place, bf16[128,14336]{1,0:T(8,128)(2,1)S(1)} %copy-done.2), custom_call_target="tpu_custom_call" | custom-call | bytes 4718860 | tf_op jit(solution)/shard_map/weights/split_upstream/pallas_call | solution.py:20
  16.7 0.8 %make_plan.1.table.plan = s32[24,64]{1,0:T(8,128)S(1)} custom-call(s32[67]{0:T(128)S(1)} %concatenate.12.place, s32[1,32]{1,0:T(1,128)S(1)} %copy-done.4, s32[2,64]{1,0:T(2,128)S(1)} %copy-done.5, s32[1,64]{1,0:T(1,128)S(1)} %copy-done.6, s32[1,64]{1,0:T(1,128)S(1)} %bitcast.13), custom_call_target="tpu_custom_call" | custom-call | bytes 7564 | tf_op jit(solution)/shard_map/plan/make_plan/pallas_call | solution.py:20
  17.6 1.6 %collective-permute-start.18 = (bf16[8,64,128]{2,1,0:T(8,128)(2,1)S(1)}, bf16[8,64,128]{2,1,0:T(8,128)(2,1)S(1)}, u32[]{:S(2)}, u32[]{:S(2)}) collective-permute-start(bf16[8,64,128]{2,1,0:T(8,128)(2,1)S(1)} %pad_maximum_fusion), channel_id=1, source_target_pairs={{0,4},{2,6},{4,0},{6,2},{8,12},{10,14},{12,8},{14,10},{16,20},{18,... | collective-permute-start | bytes 393224 | tf_op jit(solution)/shard_map/weights/ppermute | solution.py:34
  19.2 1.6 %collective-permute-start.19 = (bf16[8,64,128]{2,1,0:T(8,128)(2,1)S(1)}, bf16[8,64,128]{2,1,0:T(8,128)(2,1)S(1)}, u32[]{:S(2)}, u32[]{:S(2)}) collective-permute-start(bf16[8,64,128]{2,1,0:T(8,128)(2,1)S(1)} %collective-permute-done.17), channel_id=1, source_target_pairs={{0,8},{2,10},{4,12},{6,14},{8,0},{10,2},{12,4},{14,6},{16,24},{18,... | collective-permute-start | bytes 393224 | tf_op jit(solution)/shard_map/weights/ppermute | solution.py:34
  20.8 2.8 %collective-permute-done.18 = bf16[8,64,128]{2,1,0:T(8,128)(2,1)S(1)} collective-permute-done((bf16[8,64,128]{2,1,0:T(8,128)(2,1)S(1)}, bf16[8,64,128]{2,1,0:T(8,128)(2,1)S(1)}, u32[]{:S(2)}, u32[]{:S(2)}) %collective-permute-start.18) | collective-permute-done | bytes 131104 | tf_op jit(solution)/shard_map/weights/ppermute | solution.py:34
  23.5 1.2 %collective-permute-done.19 = bf16[8,64,128]{2,1,0:T(8,128)(2,1)S(1)} collective-permute-done((bf16[8,64,128]{2,1,0:T(8,128)(2,1)S(1)}, bf16[8,64,128]{2,1,0:T(8,128)(2,1)S(1)}, u32[]{:S(2)}, u32[]{:S(2)}) %collective-permute-start.19) | collective-permute-done | bytes 131104 | tf_op jit(solution)/shard_map/weights/ppermute | solution.py:34
  24.8 0.6 collective-permute-start.22
  25.4 1.6 %collective-permute-start.21 = (bf16[16,64,128]{2,1,0:T(8,128)(2,1)S(1)}, bf16[16,64,128]{2,1,0:T(8,128)(2,1)S(1)}, u32[]{:S(2)}, u32[]{:S(2)}) collective-permute-start(bf16[16,64,128]{2,1,0:T(8,128)(2,1)S(1)} %constant_dynamic-update-slice_fusion.refs_0_), channel_id=1, source_target_pairs={{0,8},{2,10},{4,12},{6,14},{8,0},{10,2},{12,4},{14,6},{16,24},{18,... | collective-permute-start | bytes 786440 | tf_op jit(solution)/shard_map/weights/ppermute | solution.py:34
  27.0 1.5 %collective-permute-start.25 = (bf16[32,32,128]{2,1,0:T(8,128)(2,1)S(1)}, bf16[32,32,128]{2,1,0:T(8,128)(2,1)S(1)}, u32[]{:S(2)}, u32[]{:S(2)}) collective-permute-start(bf16[32,32,128]{2,1,0:T(8,128)(2,1)S(1)} %get-tuple-element.157), channel_id=1, source_target_pairs={{0,2},{2,0},{4,6},{6,4},{8,10},{10,8},{12,14},{14,12},{16,18},{18,... | collective-permute-start | bytes 786440 | tf_op jit(solution)/shard_map/upstream/ppermute | solution.py:34
  28.5 0.5 collective-permute-start.26
  29.1 3.4 %collective-permute-done.22.refs_3_ = bf16[16,64,128]{2,1,0:T(8,128)(2,1)S(1)} collective-permute-done((bf16[16,64,128]{2,1,0:T(8,128)(2,1)S(1)}, bf16[16,64,128]{2,1,0:T(8,128)(2,1)S(1)}, u32[]{:S(2)}, u32[]{:S(2)}) %collective-permute-start.22) | collective-permute-done | bytes 262176 | tf_op jit(solution)/shard_map/weights/ppermute | solution.py:34
  32.5 0.4 collective-permute-done.21.refs_1_
  32.9 2.7 %own_part.1 = (bf16[32,128,128]{2,1,0:T(8,128)(2,1)S(1)}, f32[32,128,128]{2,1,0:T(8,128)S(1)}) custom-call(s32[24,64]{1,0:T(8,128)S(1)} %make_plan.1.table.plan, bf16[16,64,128]{2,1,0:T(8,128)(2,1)S(1)} %constant_dynamic-update-slice_fusion.refs_0_, bf16[16,64,128]{2,1,0:T(8,128)(2,1)S(1)} %collective-permute-done.21.refs_1_, ...), custom_call_target="tpu_custom_call" | custom-call | flops 268435456 | bytes 5773312 | tf_op jit(solution)/shard_map/own_tokens/own_part/pallas_call | solution.py:20
  35.6 2.2 %other_slopes.1.slope = f32[32,128,128]{2,1,0:T(8,128)S(1)} custom-call(s32[24,64]{1,0:T(8,128)S(1)} %make_plan.1.table.plan, bf16[32,128,128]{2,1,0:T(8,128)(2,1)S(1)} %get-tuple-element.156.weights, bf16[32,128,128]{2,1,0:T(8,128)(2,1)S(1)} %collective-permute-done.24.other_tokens), custom_call_target="tpu_custom_call" | custom-call | flops 134217728 | bytes 4200448 | tf_op jit(solution)/shard_map/other_tokens/other_slopes/pallas_call | solution.py:20
  37.8 1.2 %collective-permute-done.25.other_up = bf16[32,32,128]{2,1,0:T(8,128)(2,1)S(1)} collective-permute-done((bf16[32,32,128]{2,1,0:T(8,128)(2,1)S(1)}, bf16[32,32,128]{2,1,0:T(8,128)(2,1)S(1)}, u32[]{:S(2)}, u32[]{:S(2)}) %collective-permute-start.25) | collective-permute-done | bytes 262176 | tf_op jit(solution)/shard_map/upstream/ppermute | solution.py:34
  39.0 0.9 %other_part.6 = (bf16[44,16,128]{2,1,0:T(8,128)(2,1)S(1)}, f32[44,16,128]{2,1,0:T(8,128)S(1)}, bf16[44,16,128]{2,1,0:T(8,128)(2,1)S(1)}, f32[44,16,128]{2,1,0:T(8,128)S(1)}) custom-call(s32[24,64]{1,0:T(8,128)S(1)} %make_plan.1.table.plan, f32[32,128,128]{2,1,0:T(8,128)S(1)} %other_slopes.1.slope, ...), custom_call_target="tpu_custom_call" | custom-call | flops 67108864 | bytes 6592512 | tf_op jit(solution)/shard_map/other_part/pallas_call | solution.py:20
  39.9 1.6 %collective-permute-start.27 = (bf16[44,16,128]{2,1,0:T(8,128)(2,1)S(1)}, bf16[44,16,128]{2,1,0:T(8,128)(2,1)S(1)}, u32[]{:S(2)}, u32[]{:S(2)}) collective-permute-start(bf16[44,16,128]{2,1,0:T(8,128)(2,1)S(1)} %get-tuple-element.161), channel_id=1, source_target_pairs={{0,8},{2,10},{4,12},{6,14},{8,0},{10,2},{12,4},{14,6},{16,24},{18,... | collective-permute-start | bytes 540680 | tf_op jit(solution)/shard_map/ppermute | solution.py:34
  41.6 1.5 %collective-permute-start.31 = (bf16[44,16,128]{2,1,0:T(8,128)(2,1)S(1)}, bf16[44,16,128]{2,1,0:T(8,128)(2,1)S(1)}, u32[]{:S(2)}, u32[]{:S(2)}) collective-permute-start(bf16[44,16,128]{2,1,0:T(8,128)(2,1)S(1)} %get-tuple-element.171), channel_id=1, source_target_pairs={{0,4},{2,6},{4,0},{6,2},{8,12},{10,14},{12,8},{14,10},{16,20},{18,... | collective-permute-start | bytes 540680 | tf_op jit(solution)/shard_map/ppermute | solution.py:34
  43.1 0.8 %collective-permute-done.26.other_up = bf16[32,32,128]{2,1,0:T(8,128)(2,1)S(1)} collective-permute-done((bf16[32,32,128]{2,1,0:T(8,128)(2,1)S(1)}, bf16[32,32,128]{2,1,0:T(8,128)(2,1)S(1)}, u32[]{:S(2)}, u32[]{:S(2)}) %collective-permute-start.26) | collective-permute-done | bytes 262176 | tf_op jit(solution)/shard_map/upstream/ppermute | solution.py:34
  43.9 0.9 %other_part.7 = (bf16[44,16,128]{2,1,0:T(8,128)(2,1)S(1)}, f32[44,16,128]{2,1,0:T(8,128)S(1)}, bf16[44,16,128]{2,1,0:T(8,128)(2,1)S(1)}, f32[44,16,128]{2,1,0:T(8,128)S(1)}) custom-call(s32[24,64]{1,0:T(8,128)S(1)} %make_plan.1.table.plan, f32[32,128,128]{2,1,0:T(8,128)S(1)} %other_slopes.1.slope, ...), custom_call_target="tpu_custom_call" | custom-call | flops 67108864 | bytes 6592512 | tf_op jit(solution)/shard_map/other_part/pallas_call | solution.py:20
  44.8 1.6 %collective-permute-start.30 = (bf16[44,16,128]{2,1,0:T(8,128)(2,1)S(1)}, bf16[44,16,128]{2,1,0:T(8,128)(2,1)S(1)}, u32[]{:S(2)}, u32[]{:S(2)}) collective-permute-start(bf16[44,16,128]{2,1,0:T(8,128)(2,1)S(1)} %get-tuple-element.169), channel_id=1, source_target_pairs={{0,8},{2,10},{4,12},{6,14},{8,0},{10,2},{12,4},{14,6},{16,24},{18,... | collective-permute-start | bytes 540680 | tf_op jit(solution)/shard_map/ppermute | solution.py:34
  46.5 1.5 %collective-permute-start.29 = (bf16[44,16,128]{2,1,0:T(8,128)(2,1)S(1)}, bf16[44,16,128]{2,1,0:T(8,128)(2,1)S(1)}, u32[]{:S(2)}, u32[]{:S(2)}) collective-permute-start(bf16[44,16,128]{2,1,0:T(8,128)(2,1)S(1)} %get-tuple-element.168), channel_id=1, source_target_pairs={{0,4},{2,6},{4,0},{6,2},{8,12},{10,14},{12,8},{14,10},{16,20},{18,... | collective-permute-start | bytes 540680 | tf_op jit(solution)/shard_map/ppermute | solution.py:34
  48.0 0.2 combine.36
  48.2 0.6 collective-permute-start.28
  48.7 0.2 combine.37
  48.9 2.7 %collective-permute-start.35 = (bf16[28,16,128]{2,1,0:T(8,128)(2,1)S(1)}, bf16[28,16,128]{2,1,0:T(8,128)(2,1)S(1)}, u32[]{:S(2)}, u32[]{:S(2)}) collective-permute-start(bf16[28,16,128]{2,1,0:T(8,128)(2,1)S(1)} %get-tuple-element.183), channel_id=1, source_target_pairs={{0,16},{2,18},{4,20},{6,22},{8,24},{10,26},{12,28},{14,30},{16,0},... | collective-permute-start | bytes 344072 | tf_op jit(solution)/shard_map/ppermute | solution.py:34
  51.6 0.2 combine.38
  51.7 1.6 %collective-permute-start.34 = (bf16[28,16,128]{2,1,0:T(8,128)(2,1)S(1)}, bf16[28,16,128]{2,1,0:T(8,128)(2,1)S(1)}, u32[]{:S(2)}, u32[]{:S(2)}) collective-permute-start(bf16[28,16,128]{2,1,0:T(8,128)(2,1)S(1)} %get-tuple-element.182), channel_id=1, source_target_pairs={{0,4},{2,6},{4,0},{6,2},{8,12},{10,14},{12,8},{14,10},{16,20},{18,... | collective-permute-start | bytes 344072 | tf_op jit(solution)/shard_map/ppermute | solution.py:34
  53.3 0.6 collective-permute-done.29.refs_1_
  53.9 0.2 combine.39
  54.0 0.3 collective-permute-start.33
  54.3 1.4 %collective-permute-done.28.refs_1_ = bf16[28,16,128]{2,1,0:T(8,128)(2,1)S(1)} collective-permute-done((bf16[28,16,128]{2,1,0:T(8,128)(2,1)S(1)}, bf16[28,16,128]{2,1,0:T(8,128)(2,1)S(1)}, u32[]{:S(2)}, u32[]{:S(2)}) %collective-permute-start.28) | collective-permute-done | bytes 114720 | tf_op jit(solution)/shard_map/ppermute | solution.py:34
  55.8 0.1 combine.40
  55.9 2.7 %collective-permute-start.32 = (bf16[20,16,128]{2,1,0:T(8,128)(2,1)S(1)}, bf16[20,16,128]{2,1,0:T(8,128)(2,1)S(1)}, u32[]{:S(2)}, u32[]{:S(2)}) collective-permute-start(bf16[20,16,128]{2,1,0:T(8,128)(2,1)S(1)} %get-tuple-element.180), channel_id=1, source_target_pairs={{0,16},{2,18},{4,20},{6,22},{8,24},{10,26},{12,28},{14,30},{16,0},... | collective-permute-start | bytes 245768 | tf_op jit(solution)/shard_map/ppermute | solution.py:34
  58.6 0.1 combine.41
  58.7 0.5 collective-permute-start.36
  59.3 0.1 combine.42
  59.4 0.4 collective-permute-start.37
  59.8 1.8 %collective-permute-done.33.refs_1_ = bf16[28,16,128]{2,1,0:T(8,128)(2,1)S(1)} collective-permute-done((bf16[28,16,128]{2,1,0:T(8,128)(2,1)S(1)}, bf16[28,16,128]{2,1,0:T(8,128)(2,1)S(1)}, u32[]{:S(2)}, u32[]{:S(2)}) %collective-permute-start.33) | collective-permute-done | bytes 114720 | tf_op jit(solution)/shard_map/ppermute | solution.py:34
  61.7 0.1 combine.43
  61.8 0.8 %collective-permute-start.38 = (bf16[20,16,128]{2,1,0:T(8,128)(2,1)S(1)}, bf16[20,16,128]{2,1,0:T(8,128)(2,1)S(1)}, u32[]{:S(2)}, u32[]{:S(2)}) collective-permute-start(bf16[20,16,128]{2,1,0:T(8,128)(2,1)S(1)} %get-tuple-element.198), channel_id=1, source_target_pairs={{0,16},{2,18},{4,20},{6,22},{8,24},{10,26},{12,28},{14,30},{16,0},... | collective-permute-start | bytes 245768 | tf_op jit(solution)/shard_map/ppermute | solution.py:34
  62.6 1.6 %collective-permute-done.32.refs_1_ = bf16[20,16,128]{2,1,0:T(8,128)(2,1)S(1)} collective-permute-done((bf16[20,16,128]{2,1,0:T(8,128)(2,1)S(1)}, bf16[20,16,128]{2,1,0:T(8,128)(2,1)S(1)}, u32[]{:S(2)}, u32[]{:S(2)}) %collective-permute-start.32) | collective-permute-done | bytes 81952 | tf_op jit(solution)/shard_map/ppermute | solution.py:34
  64.4 0.1 combine.45
  64.6 0.6 collective-permute-start.40
  65.2 1.5 %collective-permute-start.39 = (bf16[12,16,128]{2,1,0:T(8,128)(2,1)S(1)}, bf16[12,16,128]{2,1,0:T(8,128)(2,1)S(1)}, u32[]{:S(2)}, u32[]{:S(2)}) collective-permute-start(bf16[12,16,128]{2,1,0:T(8,128)(2,1)S(1)} %get-tuple-element.201), channel_id=1, source_target_pairs={{0,2},{2,0},{4,6},{6,4},{8,10},{10,8},{12,14},{14,12},{16,18},{18,... | collective-permute-start | bytes 147464 | tf_op jit(solution)/shard_map/ppermute | solution.py:34
  66.7 0.7 collective-permute-done.37.refs_1_
  67.5 0.7 collective-permute-done.38.refs_1_
  68.4 0.6 collective-permute-start.42
  69.0 1.5 %collective-permute-start.41 = (bf16[12,16,128]{2,1,0:T(8,128)(2,1)S(1)}, bf16[12,16,128]{2,1,0:T(8,128)(2,1)S(1)}, u32[]{:S(2)}, u32[]{:S(2)}) collective-permute-start(bf16[12,16,128]{2,1,0:T(8,128)(2,1)S(1)} %get-tuple-element.203), channel_id=1, source_target_pairs={{0,2},{2,0},{4,6},{6,4},{8,10},{10,8},{12,14},{14,12},{16,18},{18,... | collective-permute-start | bytes 147464 | tf_op jit(solution)/shard_map/ppermute | solution.py:34
  70.5 0.5 slice.3
  71.7 0.4 turn_own.3
  72.1 0.5 collective-permute-done.42
  72.6 0.5 collective-permute-done.41
  73.1 1.2 %finish.1 = f32[1,12,128,128]{3,2,1,0:T(8,128)} custom-call(s32[24,64]{1,0:T(8,128)S(1)} %make_plan.1.table.plan, f32[12,128,128]{2,1,0:T(8,128)S(1)} %get-tuple-element.205.own, bf16[12,16,128]{2,1,0:T(8,128)(2,1)S(1)} %get-tuple-element.206.refs_0_, bf16[12,16,128]{2,1,0:T(8,128)(2,1)S(1)} %get-tuple-element.207.refs_1_, ...), custom_call_target="tpu_custom_call" | custom-call | bytes 1775616 | tf_op jit(solution)/shard_map/finish/pallas_call | solution.py:20
  (39 shorter events, 0.7 us)
Async XLA Ops:
  0.0 6.1 %collective-permute-start.23 = (bf16[1,128,4096]{2,1,0:T(8,128)(2,1)}, bf16[1,128,4096]{2,1,0:T(8,128)(2,1)S(1)}, u32[]{:S(2)}, u32[]{:S(2)}) collective-permute-start(bf16[1,128,4096]{2,1,0:T(8,128)(2,1)} %bitcast.9), channel_id=1, source_target_pairs={{0,1},{1,0},{2,3},{3,2},{4,5},{5,4},{6,7},{7,6},{8,9},{9,8},{10,11... | collective-permute-start | bytes 3145736 | tf_op jit(solution)/shard_map/tokens/ppermute | solution.py:34
  0.5 1.2 %copy-start = (bf16[128,4096]{1,0:T(8,128)(2,1)S(1)}, bf16[128,4096]{1,0:T(8,128)(2,1)}, u32[]{:S(2)}) copy-start(bf16[128,4096]{1,0:T(8,128)(2,1)} %tokens.1) | copy-start | bytes 3145732
  1.7 0.9 %copy-start.3 = (f32[1,4,128,128]{3,2,1,0:T(8,128)S(1)}, f32[1,4,128,128]{3,2,1,0:T(8,128)}, u32[]{:S(2)}) copy-start(f32[1,4,128,128]{3,2,1,0:T(8,128)} %masters.1) | copy-start | bytes 786436
  2.6 3.5 %copy-start.1 = (bf16[128,4096]{1,0:T(8,128)(2,1)S(1)}, bf16[128,4096]{1,0:T(8,128)(2,1)}, u32[]{:S(2)}) copy-start(bf16[128,4096]{1,0:T(8,128)(2,1)} %tokens.1) | copy-start | bytes 3145732
  2.7 8.3 %copy-start.6 = (s32[1,64]{1,0:T(1,128)S(1)}, s32[1,64]{1,0:T(1,128)}, u32[]{:S(2)}) copy-start(s32[1,64]{1,0:T(1,128)} %refs_0_.1) | copy-start | bytes 772
  2.8 5.3 %collective-permute-start.16 = (bf16[4,64,128]{2,1,0:T(8,128)(2,1)S(1)}, bf16[4,64,128]{2,1,0:T(8,128)(2,1)S(1)}, u32[]{:S(2)}, u32[]{:S(2)}) collective-permute-start(bf16[4,64,128]{2,1,0:T(8,128)(2,1)S(1)} %get-tuple-element.211), channel_id=1, source_target_pairs={{0,2},{2,0},{4,6},{6,4},{8,10},{10,8},{12,14},{14,12},{16,18},{18,... | collective-permute-start | bytes 196616 | tf_op jit(solution)/shard_map/weights/ppermute | solution.py:34
  7.3 9.4 %copy-start.4 = (s32[1,32]{1,0:T(1,128)S(1)}, s32[1,32]{1,0:T(1,128)}, u32[]{:S(2)}) copy-start(s32[1,32]{1,0:T(1,128)} %columns.1) | copy-start | bytes 388
  7.3 9.4 %copy-start.5 = (s32[2,64]{1,0:T(2,128)S(1)}, s32[2,64]{1,0:T(2,128)}, u32[]{:S(2)}) copy-start(s32[2,64]{1,0:T(2,128)} %constant.16.clone.found) | copy-start | bytes 1540
  7.3 28.3 %collective-permute-start.24 = (bf16[32,128,128]{2,1,0:T(8,128)(2,1)S(1)}, bf16[32,128,128]{2,1,0:T(8,128)(2,1)S(1)}, u32[]{:S(2)}, u32[]{:S(2)}) collective-permute-start(bf16[32,128,128]{2,1,0:T(8,128)(2,1)S(1)} %select_rows.1.refs_4_), channel_id=1, source_target_pairs={{0,2},{2,0},{4,6},{6,4},{8,10},{10,8},{12,14},{14,12},{16,18},{18,... | collective-permute-start | bytes 3145736 | tf_op jit(solution)/shard_map/weights/ppermute | solution.py:34
  8.1 9.4 %collective-permute-start.17 = (bf16[8,64,128]{2,1,0:T(8,128)(2,1)S(1)}, bf16[8,64,128]{2,1,0:T(8,128)(2,1)S(1)}, u32[]{:S(2)}, u32[]{:S(2)}) collective-permute-start(bf16[8,64,128]{2,1,0:T(8,128)(2,1)S(1)} %pad_maximum_fusion), channel_id=1, source_target_pairs={{0,16},{2,18},{4,20},{6,22},{8,24},{10,26},{12,28},{14,30},{16,0},... | collective-permute-start | bytes 393224 | tf_op jit(solution)/shard_map/weights/ppermute | solution.py:34
  11.0 5.7 %collective-permute-start.20 = (s32[1,1,64]{2,1,0:T(1,128)S(1)}, s32[1,1,64]{2,1,0:T(1,128)S(1)}, u32[]{:S(2)}, u32[]{:S(2)}) collective-permute-start(s32[1,1,64]{2,1,0:T(1,128)S(1)} %bitcast.12), channel_id=1, source_target_pairs={{0,1},{1,0},{2,3},{3,2},{4,5},{5,4},{6,7},{7,6},{8,9},{9,8},{10,11... | collective-permute-start | bytes 776 | tf_op jit(solution)/shard_map/tokens/ppermute | solution.py:34
  11.0 2.0 %copy-start.2 = (bf16[128,14336]{1,0:T(8,128)(2,1)S(1)}, bf16[128,14336]{1,0:T(8,128)(2,1)}, u32[]{:S(2)}) copy-start(bf16[128,14336]{1,0:T(8,128)(2,1)} %grad.1) | copy-start | bytes 11010052
  17.6 6.0 %collective-permute-start.18 = (bf16[8,64,128]{2,1,0:T(8,128)(2,1)S(1)}, bf16[8,64,128]{2,1,0:T(8,128)(2,1)S(1)}, u32[]{:S(2)}, u32[]{:S(2)}) collective-permute-start(bf16[8,64,128]{2,1,0:T(8,128)(2,1)S(1)} %pad_maximum_fusion), channel_id=1, source_target_pairs={{0,4},{2,6},{4,0},{6,2},{8,12},{10,14},{12,8},{14,10},{16,20},{18,... | collective-permute-start | bytes 393224 | tf_op jit(solution)/shard_map/weights/ppermute | solution.py:34
  19.2 5.6 %collective-permute-start.19 = (bf16[8,64,128]{2,1,0:T(8,128)(2,1)S(1)}, bf16[8,64,128]{2,1,0:T(8,128)(2,1)S(1)}, u32[]{:S(2)}, u32[]{:S(2)}) collective-permute-start(bf16[8,64,128]{2,1,0:T(8,128)(2,1)S(1)} %collective-permute-done.17), channel_id=1, source_target_pairs={{0,8},{2,10},{4,12},{6,14},{8,0},{10,2},{12,4},{14,6},{16,24},{18,... | collective-permute-start | bytes 393224 | tf_op jit(solution)/shard_map/weights/ppermute | solution.py:34
  24.8 7.7 %collective-permute-start.22 = (bf16[16,64,128]{2,1,0:T(8,128)(2,1)S(1)}, bf16[16,64,128]{2,1,0:T(8,128)(2,1)S(1)}, u32[]{:S(2)}, u32[]{:S(2)}) collective-permute-start(bf16[16,64,128]{2,1,0:T(8,128)(2,1)S(1)} %constant_dynamic-update-slice_fusion.2.refs_2_), channel_id=1, source_target_pairs={{0,4},{2,6},{4,0},{6,2},{8,12},{10,14},{12,8},{14,10},{16,20},{18,... | collective-permute-start | bytes 786440 | tf_op jit(solution)/shard_map/weights/ppermute | solution.py:34
  25.4 7.5 %collective-permute-start.21 = (bf16[16,64,128]{2,1,0:T(8,128)(2,1)S(1)}, bf16[16,64,128]{2,1,0:T(8,128)(2,1)S(1)}, u32[]{:S(2)}, u32[]{:S(2)}) collective-permute-start(bf16[16,64,128]{2,1,0:T(8,128)(2,1)S(1)} %constant_dynamic-update-slice_fusion.refs_0_), channel_id=1, source_target_pairs={{0,8},{2,10},{4,12},{6,14},{8,0},{10,2},{12,4},{14,6},{16,24},{18,... | collective-permute-start | bytes 786440 | tf_op jit(solution)/shard_map/weights/ppermute | solution.py:34
  27.0 12.0 %collective-permute-start.25 = (bf16[32,32,128]{2,1,0:T(8,128)(2,1)S(1)}, bf16[32,32,128]{2,1,0:T(8,128)(2,1)S(1)}, u32[]{:S(2)}, u32[]{:S(2)}) collective-permute-start(bf16[32,32,128]{2,1,0:T(8,128)(2,1)S(1)} %get-tuple-element.157), channel_id=1, source_target_pairs={{0,2},{2,0},{4,6},{6,4},{8,10},{10,8},{12,14},{14,12},{16,18},{18,... | collective-permute-start | bytes 786440 | tf_op jit(solution)/shard_map/upstream/ppermute | solution.py:34
  28.5 15.4 %collective-permute-start.26 = (bf16[32,32,128]{2,1,0:T(8,128)(2,1)S(1)}, bf16[32,32,128]{2,1,0:T(8,128)(2,1)S(1)}, u32[]{:S(2)}, u32[]{:S(2)}) collective-permute-start(bf16[32,32,128]{2,1,0:T(8,128)(2,1)S(1)} %get-tuple-element.159), channel_id=1, source_target_pairs={{0,2},{2,0},{4,6},{6,4},{8,10},{10,8},{12,14},{14,12},{16,18},{18,... | collective-permute-start | bytes 786440 | tf_op jit(solution)/shard_map/upstream/ppermute | solution.py:34
  39.9 8.1 %collective-permute-start.27 = (bf16[44,16,128]{2,1,0:T(8,128)(2,1)S(1)}, bf16[44,16,128]{2,1,0:T(8,128)(2,1)S(1)}, u32[]{:S(2)}, u32[]{:S(2)}) collective-permute-start(bf16[44,16,128]{2,1,0:T(8,128)(2,1)S(1)} %get-tuple-element.161), channel_id=1, source_target_pairs={{0,8},{2,10},{4,12},{6,14},{8,0},{10,2},{12,4},{14,6},{16,24},{18,... | collective-permute-start | bytes 540680 | tf_op jit(solution)/shard_map/ppermute | solution.py:34
  41.6 7.2 %collective-permute-start.31 = (bf16[44,16,128]{2,1,0:T(8,128)(2,1)S(1)}, bf16[44,16,128]{2,1,0:T(8,128)(2,1)S(1)}, u32[]{:S(2)}, u32[]{:S(2)}) collective-permute-start(bf16[44,16,128]{2,1,0:T(8,128)(2,1)S(1)} %get-tuple-element.171), channel_id=1, source_target_pairs={{0,4},{2,6},{4,0},{6,2},{8,12},{10,14},{12,8},{14,10},{16,20},{18,... | collective-permute-start | bytes 540680 | tf_op jit(solution)/shard_map/ppermute | solution.py:34
  44.8 6.7 %collective-permute-start.30 = (bf16[44,16,128]{2,1,0:T(8,128)(2,1)S(1)}, bf16[44,16,128]{2,1,0:T(8,128)(2,1)S(1)}, u32[]{:S(2)}, u32[]{:S(2)}) collective-permute-start(bf16[44,16,128]{2,1,0:T(8,128)(2,1)S(1)} %get-tuple-element.169), channel_id=1, source_target_pairs={{0,8},{2,10},{4,12},{6,14},{8,0},{10,2},{12,4},{14,6},{16,24},{18,... | collective-permute-start | bytes 540680 | tf_op jit(solution)/shard_map/ppermute | solution.py:34
  46.5 7.4 %collective-permute-start.29 = (bf16[44,16,128]{2,1,0:T(8,128)(2,1)S(1)}, bf16[44,16,128]{2,1,0:T(8,128)(2,1)S(1)}, u32[]{:S(2)}, u32[]{:S(2)}) collective-permute-start(bf16[44,16,128]{2,1,0:T(8,128)(2,1)S(1)} %get-tuple-element.168), channel_id=1, source_target_pairs={{0,4},{2,6},{4,0},{6,2},{8,12},{10,14},{12,8},{14,10},{16,20},{18,... | collective-permute-start | bytes 540680 | tf_op jit(solution)/shard_map/ppermute | solution.py:34
  48.2 7.6 %collective-permute-start.28 = (bf16[28,16,128]{2,1,0:T(8,128)(2,1)S(1)}, bf16[28,16,128]{2,1,0:T(8,128)(2,1)S(1)}, u32[]{:S(2)}, u32[]{:S(2)}) collective-permute-start(bf16[28,16,128]{2,1,0:T(8,128)(2,1)S(1)} %get-tuple-element.166), channel_id=1, source_target_pairs={{0,4},{2,6},{4,0},{6,2},{8,12},{10,14},{12,8},{14,10},{16,20},{18,... | collective-permute-start | bytes 344072 | tf_op jit(solution)/shard_map/ppermute | solution.py:34
  48.9 9.7 %collective-permute-start.35 = (bf16[28,16,128]{2,1,0:T(8,128)(2,1)S(1)}, bf16[28,16,128]{2,1,0:T(8,128)(2,1)S(1)}, u32[]{:S(2)}, u32[]{:S(2)}) collective-permute-start(bf16[28,16,128]{2,1,0:T(8,128)(2,1)S(1)} %get-tuple-element.183), channel_id=1, source_target_pairs={{0,16},{2,18},{4,20},{6,22},{8,24},{10,26},{12,28},{14,30},{16,0},... | collective-permute-start | bytes 344072 | tf_op jit(solution)/shard_map/ppermute | solution.py:34
  51.7 7.5 %collective-permute-start.34 = (bf16[28,16,128]{2,1,0:T(8,128)(2,1)S(1)}, bf16[28,16,128]{2,1,0:T(8,128)(2,1)S(1)}, u32[]{:S(2)}, u32[]{:S(2)}) collective-permute-start(bf16[28,16,128]{2,1,0:T(8,128)(2,1)S(1)} %get-tuple-element.182), channel_id=1, source_target_pairs={{0,4},{2,6},{4,0},{6,2},{8,12},{10,14},{12,8},{14,10},{16,20},{18,... | collective-permute-start | bytes 344072 | tf_op jit(solution)/shard_map/ppermute | solution.py:34
  54.0 7.7 %collective-permute-start.33 = (bf16[28,16,128]{2,1,0:T(8,128)(2,1)S(1)}, bf16[28,16,128]{2,1,0:T(8,128)(2,1)S(1)}, u32[]{:S(2)}, u32[]{:S(2)}) collective-permute-start(bf16[28,16,128]{2,1,0:T(8,128)(2,1)S(1)} %get-tuple-element.181), channel_id=1, source_target_pairs={{0,8},{2,10},{4,12},{6,14},{8,0},{10,2},{12,4},{14,6},{16,24},{18,... | collective-permute-start | bytes 344072 | tf_op jit(solution)/shard_map/ppermute | solution.py:34
  55.9 8.4 %collective-permute-start.32 = (bf16[20,16,128]{2,1,0:T(8,128)(2,1)S(1)}, bf16[20,16,128]{2,1,0:T(8,128)(2,1)S(1)}, u32[]{:S(2)}, u32[]{:S(2)}) collective-permute-start(bf16[20,16,128]{2,1,0:T(8,128)(2,1)S(1)} %get-tuple-element.180), channel_id=1, source_target_pairs={{0,16},{2,18},{4,20},{6,22},{8,24},{10,26},{12,28},{14,30},{16,0},... | collective-permute-start | bytes 245768 | tf_op jit(solution)/shard_map/ppermute | solution.py:34
  58.7 5.7 %collective-permute-start.36 = (bf16[20,16,128]{2,1,0:T(8,128)(2,1)S(1)}, bf16[20,16,128]{2,1,0:T(8,128)(2,1)S(1)}, u32[]{:S(2)}, u32[]{:S(2)}) collective-permute-start(bf16[20,16,128]{2,1,0:T(8,128)(2,1)S(1)} %get-tuple-element.192), channel_id=1, source_target_pairs={{0,8},{2,10},{4,12},{6,14},{8,0},{10,2},{12,4},{14,6},{16,24},{18,... | collective-permute-start | bytes 245768 | tf_op jit(solution)/shard_map/ppermute | solution.py:34
  59.4 8.0 %collective-permute-start.37 = (bf16[20,16,128]{2,1,0:T(8,128)(2,1)S(1)}, bf16[20,16,128]{2,1,0:T(8,128)(2,1)S(1)}, u32[]{:S(2)}, u32[]{:S(2)}) collective-permute-start(bf16[20,16,128]{2,1,0:T(8,128)(2,1)S(1)} %get-tuple-element.195), channel_id=1, source_target_pairs={{0,16},{2,18},{4,20},{6,22},{8,24},{10,26},{12,28},{14,30},{16,0},... | collective-permute-start | bytes 245768 | tf_op jit(solution)/shard_map/ppermute | solution.py:34
  61.8 6.4 %collective-permute-start.38 = (bf16[20,16,128]{2,1,0:T(8,128)(2,1)S(1)}, bf16[20,16,128]{2,1,0:T(8,128)(2,1)S(1)}, u32[]{:S(2)}, u32[]{:S(2)}) collective-permute-start(bf16[20,16,128]{2,1,0:T(8,128)(2,1)S(1)} %get-tuple-element.198), channel_id=1, source_target_pairs={{0,16},{2,18},{4,20},{6,22},{8,24},{10,26},{12,28},{14,30},{16,0},... | collective-permute-start | bytes 245768 | tf_op jit(solution)/shard_map/ppermute | solution.py:34
  64.6 7.5 %collective-permute-start.40 = (bf16[12,16,128]{2,1,0:T(8,128)(2,1)S(1)}, bf16[12,16,128]{2,1,0:T(8,128)(2,1)S(1)}, u32[]{:S(2)}, u32[]{:S(2)}) collective-permute-start(bf16[12,16,128]{2,1,0:T(8,128)(2,1)S(1)} %get-tuple-element.202), channel_id=1, source_target_pairs={{0,2},{2,0},{4,6},{6,4},{8,10},{10,8},{12,14},{14,12},{16,18},{18,... | collective-permute-start | bytes 147464 | tf_op jit(solution)/shard_map/ppermute | solution.py:34
  65.2 6.9 %collective-permute-start.39 = (bf16[12,16,128]{2,1,0:T(8,128)(2,1)S(1)}, bf16[12,16,128]{2,1,0:T(8,128)(2,1)S(1)}, u32[]{:S(2)}, u32[]{:S(2)}) collective-permute-start(bf16[12,16,128]{2,1,0:T(8,128)(2,1)S(1)} %get-tuple-element.201), channel_id=1, source_target_pairs={{0,2},{2,0},{4,6},{6,4},{8,10},{10,8},{12,14},{14,12},{16,18},{18,... | collective-permute-start | bytes 147464 | tf_op jit(solution)/shard_map/ppermute | solution.py:34
  68.4 4.2 %collective-permute-start.42 = (bf16[12,16,128]{2,1,0:T(8,128)(2,1)S(1)}, bf16[12,16,128]{2,1,0:T(8,128)(2,1)S(1)}, u32[]{:S(2)}, u32[]{:S(2)}) collective-permute-start(bf16[12,16,128]{2,1,0:T(8,128)(2,1)S(1)} %get-tuple-element.204), channel_id=1, source_target_pairs={{0,2},{2,0},{4,6},{6,4},{8,10},{10,8},{12,14},{14,12},{16,18},{18,... | collective-permute-start | bytes 147464 | tf_op jit(solution)/shard_map/ppermute | solution.py:34
  69.0 4.1 %collective-permute-start.41 = (bf16[12,16,128]{2,1,0:T(8,128)(2,1)S(1)}, bf16[12,16,128]{2,1,0:T(8,128)(2,1)S(1)}, u32[]{:S(2)}, u32[]{:S(2)}) collective-permute-start(bf16[12,16,128]{2,1,0:T(8,128)(2,1)S(1)} %get-tuple-element.203), channel_id=1, source_target_pairs={{0,2},{2,0},{4,6},{6,4},{8,10},{10,8},{12,14},{14,12},{16,18},{18,... | collective-permute-start | bytes 147464 | tf_op jit(solution)/shard_map/ppermute | solution.py:34
